TPU v7x, 32 devices: a whole 2x2x4 slice. The times are simulated.
32 devices in a mesh: energy: 2 (over core), space: 16 (over z, y, x).
Axes of the slice: x: 2, y: 2, z: 4, core: 2. Of those that a mesh axis runs over, the one named last changes fastest.
Arguments:
- precond: bfloat16 [2, 32, 2, 512, 512], P('energy', 'space'), may hold values from -2 to 2
- coupling: bfloat16 [32, 2, 512, 512], P('space'), may hold values from -0.046875 to 0.046875
- source: float32 [2, 32, 2, 512, 128], P('energy', 'space'), may hold values from -6 to 6
- sigma_ret: float32 [2, 32, 2, 512], P('energy', 'space'), may hold values from -0.4 to 0.4
- occupation: float32 [2, 128], replicated, may hold values from 0.05 to 0.95
- shift_offsets: int32 [2, 4], replicated, may hold values from -1 to 1, as said below
- shift_weights: float32 [2, 4], replicated, may hold values from 0.3 to 3
Outputs:
- sigma_lesser: bfloat16 [2, 32, 2, 512, 512], P('energy', 'space')
- sigma_greater: bfloat16 [2, 32, 2, 512, 512], P('energy', 'space')
Inputs may be any that keep to these rules, and one draw needn't show every extreme that they name: `shift_offsets`: in every energy's list one offset is -1 or 1.
All inputs are finite; a program needn't handle non-finite values.
Results may differ from a plain program's by a relative error of at most 0.015.
Values may be sent and summed in bfloat16 or wider, within the bound.
No kernel may reach another device: no remote copies, remote signals or barrier semaphores. Data moves between devices by JAX's collectives and lax.ppermute only.
A program may use at most 64 MiB of HBM per device.

v0:
```python
import jax
import jax.numpy as jnp
from jax import lax
from jax.sharding import PartitionSpec as P

SWEEPS = 4


def from_behind(block, axis, distance):
    devices = range(lax.axis_size(axis))
    route = [(i - distance, i) for i in devices if i - distance in devices]
    return lax.ppermute(block, axis, route)


def extended(array, sides, width):
    for axis, dim in sides:
        peers, length = (lax.axis_size(axis), array.shape[dim])
        up = [(i, (i + 1) % peers) for i in range(peers - 1)]
        down = [(j, i) for i, j in up]
        last = lax.slice_in_dim(array, length - width, length, axis=dim)
        first = lax.slice_in_dim(array, 0, width, axis=dim)
        before = lax.ppermute(last, axis, up)
        after = lax.ppermute(first, axis, down)
        array = jnp.concatenate([before, array, after], axis=dim)
    return array


def multiply(first_operand, second_operand):
    return jnp.einsum(
        "...mn,...nk->...mk", first_operand, second_operand, preferred_element_type=jnp.float32
    )


def multiply_adjoint(first_operand, second_operand):
    return jnp.einsum(
        "...nm,...nk->...mk", first_operand, second_operand, preferred_element_type=jnp.float32
    )


def complex_product(matrix, states):
    real_part = multiply(matrix[..., 0, :, :], states[..., 0, :, :]) - multiply(
        matrix[..., 1, :, :], states[..., 1, :, :]
    )
    imag_part = multiply(matrix[..., 0, :, :], states[..., 1, :, :]) + multiply(
        matrix[..., 1, :, :], states[..., 0, :, :]
    )
    return jnp.stack([real_part, imag_part], axis=-3)


def adjoint_product(matrix, states):
    real_part = multiply_adjoint(matrix[..., 0, :, :], states[..., 0, :, :]) + multiply_adjoint(
        matrix[..., 1, :, :], states[..., 1, :, :]
    )
    imag_part = multiply_adjoint(matrix[..., 0, :, :], states[..., 1, :, :]) - multiply_adjoint(
        matrix[..., 1, :, :], states[..., 0, :, :]
    )
    return jnp.stack([real_part, imag_part], axis=-3)


def self_block(picked, scale):
    scaled = (picked * scale[:, :, None, None, None, :]).astype(jnp.bfloat16)
    real_part = jnp.einsum(
        "ejsmk,ejsnk->esmn",
        picked[:, :, :, 0],
        scaled[:, :, :, 0],
        preferred_element_type=jnp.float32,
    )
    real_part = real_part + jnp.einsum(
        "ejsmk,ejsnk->esmn",
        picked[:, :, :, 1],
        scaled[:, :, :, 1],
        preferred_element_type=jnp.float32,
    )
    imag_part = jnp.einsum(
        "ejsmk,ejsnk->esmn",
        picked[:, :, :, 1],
        scaled[:, :, :, 0],
        preferred_element_type=jnp.float32,
    )
    imag_part = imag_part - jnp.einsum(
        "ejsmk,ejsnk->esmn",
        picked[:, :, :, 0],
        scaled[:, :, :, 1],
        preferred_element_type=jnp.float32,
    )
    return jnp.stack([real_part, imag_part], axis=2).astype(jnp.bfloat16)


def body(precond, coupling, source, sigma_ret, occupation, shift_offsets, shift_weights):
    local_count = source.shape[0]
    mode_count = source.shape[-1]
    energy_total = occupation.shape[0]
    states = complex_product(precond, source.astype(jnp.bfloat16)).astype(jnp.bfloat16)
    sigma_real = sigma_ret[:, :, 0, :, None]
    sigma_imag = sigma_ret[:, :, 1, :, None]
    for sweep_index in range(1, SWEEPS):
        following = from_behind(states[:, 0], "space", -1)
        beyond = jnp.concatenate([states[:, 1:], following[:, None]], axis=1)
        upper_term = complex_product(coupling, beyond)
        handed = adjoint_product(coupling, states).astype(jnp.bfloat16)
        arriving = from_behind(handed[:, -1], "space", 1)
        lower_term = jnp.concatenate([arriving[:, None], handed[:, :-1]], axis=1)
        states_real = states[:, :, 0].astype(jnp.float32)
        states_imag = states[:, :, 1].astype(jnp.float32)
        local_term = jnp.stack(
            [
                sigma_real * states_real - sigma_imag * states_imag,
                sigma_real * states_imag + sigma_imag * states_real,
            ],
            axis=2,
        )
        driven = (source + local_term + upper_term + lower_term.astype(jnp.float32)).astype(
            jnp.bfloat16
        )
        states = complex_product(precond, driven).astype(jnp.bfloat16)
    first_energy = lax.axis_index("energy") * local_count
    local_ids = first_energy + jnp.arange(local_count, dtype=jnp.int32)
    offsets = lax.dynamic_slice_in_dim(shift_offsets, first_energy, local_count, 0)
    weights_here = lax.dynamic_slice_in_dim(shift_weights, first_energy, local_count, 0)
    targets = local_ids[:, None] + offsets
    inside = (targets >= 0) & (targets < energy_total)
    clipped = jnp.clip(targets, 0, energy_total - 1)
    gathered = extended(states, (("energy", 0),), local_count)
    picked = jnp.take(gathered, targets - first_energy + local_count, axis=0)
    occupied = jnp.take(occupation, clipped, axis=0)
    weights = jnp.where(inside, weights_here, jnp.zeros_like(weights_here)) / mode_count
    sigma_lesser = self_block(picked, weights[:, :, None] * occupied)
    sigma_greater = self_block(picked, weights[:, :, None] * (1.0 - occupied))
    return (sigma_lesser, sigma_greater)


def solution(mesh):
    placed = (
        P("energy", "space", None, None, None),
        P("space", None, None, None),
        P("energy", "space", None, None, None),
        P("energy", "space", None, None),
        P(),
        P(),
        P(),
    )
    return jax.shard_map(
        body,
        mesh=mesh,
        in_specs=placed,
        out_specs=(P("energy", "space", None, None, None), P("energy", "space", None, None, None)),
        check_vma=False,
    )
```

profile of v0, /device:TPU:25, one launch (start us, length us, event | category | flops | bytes accessed | tf_op | source)
XLA Modules:
  0.0 87.8 jit_solution(6132909525063784293)
XLA Ops:
  0.7 1.4 %copy.308 = bf16[1,2,2,512,128]{4,3,1,2,0:T(8,128)(2,1)S(1)} copy(f32[1,2,2,512,128]{4,3,2,1,0:T(8,128)} %param.9) | data formatting | bytes 1572864 | tf_op args[2]
  2.1 1.7 %fusion.103 = f32[2,512,128]{2,1,0:T(8,128)S(1)} fusion(bf16[1,2,2,512,128]{4,3,1,2,0:T(8,128)(2,1)S(1)} %copy.308, bf16[1,2,2,512,512]{4,3,2,1,0:T(8,128)(2,1)} %param.7), kind=kOutput, calls=%fused_computation.144 | convolution fusion | flops 134217728 | bytes 1835008 | tf_op jit(solution)/shard_map/...mn,...nk->...mk/dot_general | solution.py:29
  4.3 0.4 fusion.16
  4.7 1.2 %fusion.111 = (f32[1,2,1,512,128]{4,3,1,2,0:T(8,128)S(1)}, f32[1,2,1,512,128]{4,3,1,2,0:T(8,128)}, bf16[2,512,128]{2,1,0:T(8,128)(2,1)S(1)}) fusion(f32[2,512]{1,0:T(2,128)S(1)} %get-tuple-element.33, f32[2,512]{1,0:T(2,128)S(1)} %get-tuple-element.34, bf16[2,512,128]{2,1,0:T(8,128)(2,1)S(1)} %fusion.16, f32[2,512,128]{2,1,0:T(8,128)S(1)} %fusion.103, ...), kind=kOutput, calls=%fused_computation.165 | convolution fusion | flops 135528448 | bytes 3416064 | tf_op jit(solution)/shard_map/...mn,...nk->...mk/dot_general | solution.py:29
  6.0 0.7 fusion.143
  6.7 3.9 %collective-permute-start = (bf16[1,2,512,128]{3,2,1,0:T(8,128)(2,1)}, bf16[1,2,512,128]{3,2,1,0:T(8,128)(2,1)}, u32[]{:S(2)}, u32[]{:S(2)}) collective-permute-start(bf16[1,2,512,128]{3,2,1,0:T(8,128)(2,1)} %get-tuple-element.22), channel_id=1, source_target_pairs={{1,0},{2,1},{3,2},{4,3},{5,4},{6,5},{7,6},{8,7},{9,8},{10,9},{11,1... | collective-permute-start | bytes 786440 | tf_op jit(solution)/shard_map/ppermute | solution.py:12
  10.7 0.5 fusion.76
  11.2 0.5 fusion.78
  11.8 0.5 fusion.36
  12.3 0.5 fusion.37
  12.8 0.7 fusion.133
  13.6 1.9 %collective-permute-start.1 = (bf16[1,2,512,128]{3,2,1,0:T(8,128)(2,1)}, bf16[1,2,512,128]{3,2,1,0:T(8,128)(2,1)}, u32[]{:S(2)}, u32[]{:S(2)}) collective-permute-start(bf16[1,2,512,128]{3,2,1,0:T(8,128)(2,1)} %fusion.133), channel_id=1, source_target_pairs={{0,1},{1,2},{2,3},{3,4},{4,5},{5,6},{6,7},{7,8},{8,9},{9,10},{10,1... | collective-permute-start | bytes 786440 | tf_op jit(solution)/shard_map/ppermute | solution.py:12
  15.5 0.6 collective-permute-done
  16.1 1.3 %fusion.66 = f32[2,128,512]{1,2,0:T(8,128)S(1)} fusion(bf16[1,1,2,512,128]{4,3,2,1,0:T(8,128)(2,1)S(1)} %get-tuple-element.23, bf16[1,1,2,512,128]{4,3,2,1,0:T(8,128)(2,1)} %bitcast.8, bf16[2,2,512,512]{3,2,1,0:T(8,128)(2,1)S(1)} %copy-done.1), kind=kOutput, calls=%fused_computation.107 | convolution fusion | flops 134742016 | bytes 2097152 | tf_op jit(solution)/shard_map/...mn,...nk->...mk/dot_general | solution.py:29
  17.4 1.3 %fusion.50 = f32[2,128,512]{1,2,0:T(8,128)S(1)} fusion(bf16[1,1,2,512,128]{4,3,2,1,0:T(8,128)(2,1)S(1)} %get-tuple-element.23, bf16[1,1,2,512,128]{4,3,2,1,0:T(8,128)(2,1)} %bitcast.8, bf16[2,2,512,512]{3,2,1,0:T(8,128)(2,1)S(1)} %copy-done.1), kind=kOutput, calls=%fused_computation.91 | convolution fusion | flops 134742016 | bytes 2097152 | tf_op jit(solution)/shard_map/...mn,...nk->...mk/dot_general | solution.py:29
  18.8 1.5 %fusion.15 = f32[1,2,1,512,128]{4,3,1,2,0:T(8,128)S(1)} fusion(f32[2,128,512]{1,2,0:T(8,128)S(1)} %fusion.66, bf16[1,1,2,512,128]{4,3,2,1,0:T(8,128)(2,1)} %bitcast.8, bf16[1,1,2,512,128]{4,3,2,1,0:T(8,128)(2,1)S(1)} %get-tuple-element.23, bf16[2,2,512,512]{3,2,1,0:T(8,128)(2,1)S(1)} %copy-done.1), kind=kOutput, calls=%fused_computation.37 | convolution fusion | flops 134873088 | bytes 2621440 | tf_op jit(solution)/shard_map/...mn,...nk->...mk/dot_general | solution.py:29
  20.3 1.3 %fusion.14 = f32[1,2,1,512,128]{4,3,1,2,0:T(8,128)S(1)} fusion(f32[2,128,512]{1,2,0:T(8,128)S(1)} %fusion.50, bf16[1,1,2,512,128]{4,3,2,1,0:T(8,128)(2,1)} %bitcast.8, bf16[1,1,2,512,128]{4,3,2,1,0:T(8,128)(2,1)S(1)} %get-tuple-element.23, bf16[2,2,512,512]{3,2,1,0:T(8,128)(2,1)S(1)} %copy-done.1), kind=kOutput, calls=%fused_computation.35 | convolution fusion | flops 134873088 | bytes 2621440 | tf_op jit(solution)/shard_map/...mn,...nk->...mk/dot_general | solution.py:29
  21.6 2.8 %collective-permute-done.1 = bf16[1,2,512,128]{3,2,1,0:T(8,128)(2,1)} collective-permute-done((bf16[1,2,512,128]{3,2,1,0:T(8,128)(2,1)}, bf16[1,2,512,128]{3,2,1,0:T(8,128)(2,1)}, u32[]{:S(2)}, u32[]{:S(2)}) %collective-permute-start.1) | collective-permute-done | bytes 262176 | tf_op jit(solution)/shard_map/ppermute | solution.py:12
  24.4 1.4 %fusion.40 = bf16[1,2,2,512,128]{4,3,1,2,0:T(8,128)(2,1)S(1)} fusion(f32[1,2,1,512,128]{4,3,1,2,0:T(8,128)S(1)} %copy-done.5, f32[1,2,1,512,128]{4,3,1,2,0:T(8,128)S(1)} %get-tuple-element.16, f32[1,2,1,512,128]{4,3,1,2,0:T(8,128)S(1)} %fusion.14, f32[1,2,1,512,128]{4,3,1,2,0:T(8,128)S(1)} %fusion.15, f32[1,2,2,512,128]{4,3,2,1,0:T(8,128)S(1)} %copy-done.4, ...), kind=kLoop, calls=%fused_computation.79 | loop fusion | flops 2359296 | bytes 4456448 | tf_op jit(solution)/shard_map/convert_element_type | solution.py:112
  26.5 0.4 fusion.97
  27.0 0.4 fusion.26
  27.4 0.5 fusion.71
  28.0 0.7 fusion.113
  28.6 0.5 fusion.69
  29.2 0.5 fusion.35
  29.8 3.0 %collective-permute-start.2 = (bf16[1,2,512,128]{3,2,1,0:T(8,128)(2,1)S(1)}, bf16[1,2,512,128]{3,2,1,0:T(8,128)(2,1)S(1)}, u32[]{:S(2)}, u32[]{:S(2)}) collective-permute-start(bf16[1,2,512,128]{3,2,1,0:T(8,128)(2,1)S(1)} %get-tuple-element.20), channel_id=1, source_target_pairs={{1,0},{2,1},{3,2},{4,3},{5,4},{6,5},{7,6},{8,7},{9,8},{10,9},{11,1... | collective-permute-start | bytes 786440 | tf_op jit(solution)/shard_map/ppermute | solution.py:12
  32.8 0.5 fusion.34
  33.3 2.5 %collective-permute-start.3 = (bf16[1,2,512,128]{3,2,1,0:T(8,128)(2,1)S(1)}, bf16[1,2,512,128]{3,2,1,0:T(8,128)(2,1)S(1)}, u32[]{:S(2)}, u32[]{:S(2)}) collective-permute-start(bf16[1,2,512,128]{3,2,1,0:T(8,128)(2,1)S(1)} %fusion.127), channel_id=1, source_target_pairs={{0,1},{1,2},{2,3},{3,4},{4,5},{5,6},{6,7},{7,8},{8,9},{9,10},{10,1... | collective-permute-start | bytes 786440 | tf_op jit(solution)/shard_map/ppermute | solution.py:12
  35.8 1.8 %collective-permute-done.2 = bf16[1,2,512,128]{3,2,1,0:T(8,128)(2,1)S(1)} collective-permute-done((bf16[1,2,512,128]{3,2,1,0:T(8,128)(2,1)S(1)}, bf16[1,2,512,128]{3,2,1,0:T(8,128)(2,1)S(1)}, u32[]{:S(2)}, u32[]{:S(2)}) %collective-permute-start.2) | collective-permute-done | bytes 262176 | tf_op jit(solution)/shard_map/ppermute | solution.py:12
  38.5 0.4 fusion.13
  39.4 3.5 %collective-permute-done.3 = bf16[1,2,512,128]{3,2,1,0:T(8,128)(2,1)S(1)} collective-permute-done((bf16[1,2,512,128]{3,2,1,0:T(8,128)(2,1)S(1)}, bf16[1,2,512,128]{3,2,1,0:T(8,128)(2,1)S(1)}, u32[]{:S(2)}, u32[]{:S(2)}) %collective-permute-start.3) | collective-permute-done | bytes 262176 | tf_op jit(solution)/shard_map/ppermute | solution.py:12
  43.5 0.4 fusion.101
  43.9 0.4 fusion.28
  44.4 0.5 fusion.64
  44.9 0.7 fusion.115
  45.6 0.5 fusion.62
  46.1 0.5 fusion.33
  46.7 5.9 %collective-permute-start.4 = (bf16[1,2,512,128]{3,2,1,0:T(8,128)(2,1)S(1)}, bf16[1,2,512,128]{3,2,1,0:T(8,128)(2,1)S(1)}, u32[]{:S(2)}, u32[]{:S(2)}) collective-permute-start(bf16[1,2,512,128]{3,2,1,0:T(8,128)(2,1)S(1)} %get-tuple-element.18), channel_id=1, source_target_pairs={{1,0},{2,1},{3,2},{4,3},{5,4},{6,5},{7,6},{8,7},{9,8},{10,9},{11,1... | collective-permute-start | bytes 786440 | tf_op jit(solution)/shard_map/ppermute | solution.py:12
  52.6 0.5 fusion.32
  53.2 1.9 %collective-permute-start.5 = (bf16[1,2,512,128]{3,2,1,0:T(8,128)(2,1)S(1)}, bf16[1,2,512,128]{3,2,1,0:T(8,128)(2,1)S(1)}, u32[]{:S(2)}, u32[]{:S(2)}) collective-permute-start(bf16[1,2,512,128]{3,2,1,0:T(8,128)(2,1)S(1)} %fusion.121), channel_id=1, source_target_pairs={{0,1},{1,2},{2,3},{3,4},{4,5},{5,6},{6,7},{7,8},{8,9},{9,10},{10,1... | collective-permute-start | bytes 786440 | tf_op jit(solution)/shard_map/ppermute | solution.py:12
  55.1 1.7 %collective-permute-done.4 = bf16[1,2,512,128]{3,2,1,0:T(8,128)(2,1)S(1)} collective-permute-done((bf16[1,2,512,128]{3,2,1,0:T(8,128)(2,1)S(1)}, bf16[1,2,512,128]{3,2,1,0:T(8,128)(2,1)S(1)}, u32[]{:S(2)}, u32[]{:S(2)}) %collective-permute-start.4) | collective-permute-done | bytes 262176 | tf_op jit(solution)/shard_map/ppermute | solution.py:12
  57.7 0.4 fusion.11
  58.2 0.4 fusion.10
  58.6 4.4 %collective-permute-done.5 = bf16[1,2,512,128]{3,2,1,0:T(8,128)(2,1)S(1)} collective-permute-done((bf16[1,2,512,128]{3,2,1,0:T(8,128)(2,1)S(1)}, bf16[1,2,512,128]{3,2,1,0:T(8,128)(2,1)S(1)}, u32[]{:S(2)}, u32[]{:S(2)}) %collective-permute-start.5) | collective-permute-done | bytes 262176 | tf_op jit(solution)/shard_map/ppermute | solution.py:12
  63.2 0.5 fusion.91
  63.7 0.5 fusion.93
  64.2 0.5 fusion.30
  64.7 0.5 fusion.31
  65.3 4.5 %collective-permute-start.7 = (bf16[1,2,2,512,128]{3,4,1,2,0:T(8,128)(2,1)S(1)}, bf16[1,2,2,512,128]{3,4,1,2,0:T(8,128)(2,1)S(1)}, u32[]{:S(2)}, u32[]{:S(2)}) collective-permute-start(bf16[1,2,2,512,128]{3,4,1,2,0:T(8,128)(2,1)S(1)} %pad_maximum_fusion.6), channel_id=1, source_target_pairs={{16,0},{17,1},{18,2},{19,3},{20,4},{21,5},{22,6},{23,7},{24,8},{25... | collective-permute-start | bytes 1572872 | tf_op jit(solution)/shard_map/ppermute | solution.py:23
  69.7 1.5 %collective-permute-start.6 = (bf16[1,2,2,512,128]{3,4,1,2,0:T(8,128)(2,1)S(1)}, bf16[1,2,2,512,128]{3,4,1,2,0:T(8,128)(2,1)S(1)}, u32[]{:S(2)}, u32[]{:S(2)}) collective-permute-start(bf16[1,2,2,512,128]{3,4,1,2,0:T(8,128)(2,1)S(1)} %pad_maximum_fusion.6), channel_id=1, source_target_pairs={{0,16},{1,17},{2,18},{3,19},{4,20},{5,21},{6,22},{7,23},{8,24},{9,... | collective-permute-start | bytes 1572872 | tf_op jit(solution)/shard_map/ppermute | solution.py:22
  71.3 0.6 gather_fusion.1
  72.0 1.6 %collective-permute-done.6 = bf16[1,2,2,512,128]{3,4,1,2,0:T(8,128)(2,1)S(1)} collective-permute-done((bf16[1,2,2,512,128]{3,4,1,2,0:T(8,128)(2,1)S(1)}, bf16[1,2,2,512,128]{3,4,1,2,0:T(8,128)(2,1)S(1)}, u32[]{:S(2)}, u32[]{:S(2)}) %collective-permute-start.6) | collective-permute-done | bytes 524320 | tf_op jit(solution)/shard_map/ppermute | solution.py:22
  73.7 2.0 %gather_fusion = bf16[4,2,2,512,128]{3,4,1,2,0:T(8,128)(2,1)} fusion(bf16[3,2,2,512,128]{3,4,1,2,0:T(8,128)(2,1)S(1)} %pad_maximum_fusion.2, s32[1024]{0:T(1024)S(1)} %pad_clamp_fusion.1), kind=kCustom, calls=%fused_computation | custom fusion | bytes 4194320 | tf_op jit(solution)/shard_map/jit(_take)/gather | solution.py:124
  75.7 2.2 %fusion.1 = (bf16[1,4,2,2,512,128]{4,5,2,3,1,0:T(8,128)(2,1)S(1)}, bf16[1,4,2,2,512,128]{4,5,2,3,1,0:T(8,128)(2,1)S(1)}) fusion(f32[4,128]{1,0:T(4,128)S(1)} %get-tuple-element.27, bf16[4,2,2,512,128]{3,4,1,2,0:T(8,128)(2,1)} %gather_fusion, pred[4]{0:T(512)(128)(4,1)S(1)} %get-tuple-element.10), kind=kLoop, calls=%fused_computation.5 | loop fusion | flops 4194304 | bytes 6293508 | tf_op jit(solution)/shard_map/convert_element_type | solution.py:61
  78.4 0.8 fusion.107
  79.1 0.8 fusion.108
  79.9 0.8 fusion.109
  80.7 0.8 fusion.110
  81.4 0.8 fusion.7
  82.2 0.8 fusion.6
  83.2 1.5 %copy.207 = bf16[1,2,2,512,512]{4,3,2,1,0:T(8,128)(2,1)} copy(bf16[1,2,2,512,512]{4,3,1,2,0:T(8,128)(2,1)S(1)} %pad_maximum_fusion) | data formatting | bytes 4194304
  84.6 0.8 fusion.9
  85.4 0.8 fusion.8
  86.4 1.5 %copy.208 = bf16[1,2,2,512,512]{4,3,2,1,0:T(8,128)(2,1)} copy(bf16[1,2,2,512,512]{4,3,1,2,0:T(8,128)(2,1)S(1)} %pad_maximum_fusion.1) | data formatting | bytes 4194304
  (45 shorter events, 5.5 us)
Async XLA Ops:
  0.6 70.7 %copy-start = (f32[2,128]{1,0:T(2,128)S(1)}, f32[2,128]{1,0:T(2,128)}, u32[]{:S(2)}) copy-start(f32[2,128]{1,0:T(2,128)} %param.11) | copy-start | bytes 3076
  0.6 3.1 %copy-start.2 = (bf16[1,2,2,512,512]{4,3,2,1,0:T(8,128)(2,1)S(1)}, bf16[1,2,2,512,512]{4,3,2,1,0:T(8,128)(2,1)}, u32[]{:S(2)}) copy-start(bf16[1,2,2,512,512]{4,3,2,1,0:T(8,128)(2,1)} %param.7) | copy-start | bytes 6291460
  2.1 2.1 %copy-start.6 = (f32[1,2,2,512]{3,2,1,0:T(2,128)S(1)}, f32[1,2,2,512]{3,2,1,0:T(2,128)}, u32[]{:S(2)}) copy-start(f32[1,2,2,512]{3,2,1,0:T(2,128)} %param.10) | copy-start | bytes 24580
  4.7 6.0 %copy-start.1 = (bf16[2,2,512,512]{3,2,1,0:T(8,128)(2,1)S(1)}, bf16[2,2,512,512]{3,2,1,0:T(8,128)(2,1)}, u32[]{:S(2)}) copy-start(bf16[2,2,512,512]{3,2,1,0:T(8,128)(2,1)} %param.8) | copy-start | bytes 6291460
  6.7 9.4 %collective-permute-start = (bf16[1,2,512,128]{3,2,1,0:T(8,128)(2,1)}, bf16[1,2,512,128]{3,2,1,0:T(8,128)(2,1)}, u32[]{:S(2)}, u32[]{:S(2)}) collective-permute-start(bf16[1,2,512,128]{3,2,1,0:T(8,128)(2,1)} %get-tuple-element.22), channel_id=1, source_target_pairs={{1,0},{2,1},{3,2},{4,3},{5,4},{6,5},{7,6},{8,7},{9,8},{10,9},{11,1... | collective-permute-start | bytes 786440 | tf_op jit(solution)/shard_map/ppermute | solution.py:12
  11.8 3.7 %copy-start.7 = (s32[2,4]{1,0:T(2,128)S(1)}, s32[2,4]{1,0:T(2,128)}, u32[]{:S(2)}) copy-start(s32[2,4]{1,0:T(2,128)} %param.12) | copy-start | bytes 100
  13.6 10.8 %collective-permute-start.1 = (bf16[1,2,512,128]{3,2,1,0:T(8,128)(2,1)}, bf16[1,2,512,128]{3,2,1,0:T(8,128)(2,1)}, u32[]{:S(2)}, u32[]{:S(2)}) collective-permute-start(bf16[1,2,512,128]{3,2,1,0:T(8,128)(2,1)} %fusion.133), channel_id=1, source_target_pairs={{0,1},{1,2},{2,3},{3,4},{4,5},{5,6},{6,7},{7,8},{8,9},{9,10},{10,1... | collective-permute-start | bytes 786440 | tf_op jit(solution)/shard_map/ppermute | solution.py:12
  18.8 5.6 %copy-start.4 = (f32[1,2,2,512,128]{4,3,2,1,0:T(8,128)S(1)}, f32[1,2,2,512,128]{4,3,2,1,0:T(8,128)}, u32[]{:S(2)}) copy-start(f32[1,2,2,512,128]{4,3,2,1,0:T(8,128)} %param.9) | copy-start | bytes 3145732
  18.8 5.6 %copy-start.5 = (f32[1,2,1,512,128]{4,3,1,2,0:T(8,128)S(1)}, f32[1,2,1,512,128]{4,3,1,2,0:T(8,128)}, u32[]{:S(2)}) copy-start(f32[1,2,1,512,128]{4,3,1,2,0:T(8,128)} %get-tuple-element.17) | copy-start | bytes 1572868
  24.4 1.7 %copy-start.3 = (bf16[1,2,2,512,512]{4,3,2,1,0:T(8,128)(2,1)S(1)}, bf16[1,2,2,512,512]{4,3,2,1,0:T(8,128)(2,1)}, u32[]{:S(2)}) copy-start(bf16[1,2,2,512,512]{4,3,2,1,0:T(8,128)(2,1)} %param.7) | copy-start | bytes 6291460
  29.8 7.8 %collective-permute-start.2 = (bf16[1,2,512,128]{3,2,1,0:T(8,128)(2,1)S(1)}, bf16[1,2,512,128]{3,2,1,0:T(8,128)(2,1)S(1)}, u32[]{:S(2)}, u32[]{:S(2)}) collective-permute-start(bf16[1,2,512,128]{3,2,1,0:T(8,128)(2,1)S(1)} %get-tuple-element.20), channel_id=1, source_target_pairs={{1,0},{2,1},{3,2},{4,3},{5,4},{6,5},{7,6},{8,7},{9,8},{10,9},{11,1... | collective-permute-start | bytes 786440 | tf_op jit(solution)/shard_map/ppermute | solution.py:12
  33.3 9.5 %collective-permute-start.3 = (bf16[1,2,512,128]{3,2,1,0:T(8,128)(2,1)S(1)}, bf16[1,2,512,128]{3,2,1,0:T(8,128)(2,1)S(1)}, u32[]{:S(2)}, u32[]{:S(2)}) collective-permute-start(bf16[1,2,512,128]{3,2,1,0:T(8,128)(2,1)S(1)} %fusion.127), channel_id=1, source_target_pairs={{0,1},{1,2},{2,3},{3,4},{4,5},{5,6},{6,7},{7,8},{8,9},{9,10},{10,1... | collective-permute-start | bytes 786440 | tf_op jit(solution)/shard_map/ppermute | solution.py:12
  46.7 10.1 %collective-permute-start.4 = (bf16[1,2,512,128]{3,2,1,0:T(8,128)(2,1)S(1)}, bf16[1,2,512,128]{3,2,1,0:T(8,128)(2,1)S(1)}, u32[]{:S(2)}, u32[]{:S(2)}) collective-permute-start(bf16[1,2,512,128]{3,2,1,0:T(8,128)(2,1)S(1)} %get-tuple-element.18), channel_id=1, source_target_pairs={{1,0},{2,1},{3,2},{4,3},{5,4},{6,5},{7,6},{8,7},{9,8},{10,9},{11,1... | collective-permute-start | bytes 786440 | tf_op jit(solution)/shard_map/ppermute | solution.py:12
  53.2 9.9 %collective-permute-start.5 = (bf16[1,2,512,128]{3,2,1,0:T(8,128)(2,1)S(1)}, bf16[1,2,512,128]{3,2,1,0:T(8,128)(2,1)S(1)}, u32[]{:S(2)}, u32[]{:S(2)}) collective-permute-start(bf16[1,2,512,128]{3,2,1,0:T(8,128)(2,1)S(1)} %fusion.121), channel_id=1, source_target_pairs={{0,1},{1,2},{2,3},{3,4},{4,5},{5,6},{6,7},{7,8},{8,9},{9,10},{10,1... | collective-permute-start | bytes 786440 | tf_op jit(solution)/shard_map/ppermute | solution.py:12
  64.7 7.1 %copy-start.8 = (f32[2,4]{1,0:T(2,128)S(1)}, f32[2,4]{1,0:T(2,128)}, u32[]{:S(2)}) copy-start(f32[2,4]{1,0:T(2,128)} %param.13) | copy-start | bytes 100
  65.3 6.7 %collective-permute-start.7 = (bf16[1,2,2,512,128]{3,4,1,2,0:T(8,128)(2,1)S(1)}, bf16[1,2,2,512,128]{3,4,1,2,0:T(8,128)(2,1)S(1)}, u32[]{:S(2)}, u32[]{:S(2)}) collective-permute-start(bf16[1,2,2,512,128]{3,4,1,2,0:T(8,128)(2,1)S(1)} %pad_maximum_fusion.6), channel_id=1, source_target_pairs={{16,0},{17,1},{18,2},{19,3},{20,4},{21,5},{22,6},{23,7},{24,8},{25... | collective-permute-start | bytes 1572872 | tf_op jit(solution)/shard_map/ppermute | solution.py:23
  69.7 3.8 %collective-permute-start.6 = (bf16[1,2,2,512,128]{3,4,1,2,0:T(8,128)(2,1)S(1)}, bf16[1,2,2,512,128]{3,4,1,2,0:T(8,128)(2,1)S(1)}, u32[]{:S(2)}, u32[]{:S(2)}) collective-permute-start(bf16[1,2,2,512,128]{3,4,1,2,0:T(8,128)(2,1)S(1)} %pad_maximum_fusion.6), channel_id=1, source_target_pairs={{0,16},{1,17},{2,18},{3,19},{4,20},{5,21},{6,22},{7,23},{8,24},{9,... | collective-permute-start | bytes 1572872 | tf_op jit(solution)/shard_map/ppermute | solution.py:22
where the time goes:
time: 89.4 us; the launch traced here: 87.8 us
  matrix products  31.1 us (35%)
  starting transfers between devices  25.1 us (28%)
  waiting for transfers between devices  16.4 us (18%)
  local copies, waits for them, and re-layouts  7.3 us (8%)
  other arithmetic  6.67 us (7%)
  between operations  1.21 us (1%)
    ppermute x6, starting transfers between devices, from_behind(): return lax.ppermute(block, axis, route)  19.1 us
    dot_general x28, matrix products, multiply(): jnp.einsum('...mn,...nk->...mk', first_operand, second_operand, preferred...  18.6 us
    ppermute x6, waiting for transfers between devices, from_behind(): return lax.ppermute(block, axis, route)  14.8 us
    dot_general x12, matrix products, multiply_adjoint(): jnp.einsum('...nm,...nk->...mk', first_operand, second_operand, preferred...  6.37 us
    unnamed x22, local copies, waits for them, and re-layouts  4.73 us
    ppermute x1, starting transfers between devices, extended(): after = lax.ppermute(first, axis, down)  4.47 us
    convert_element_type x2, other arithmetic, self_block(): scaled = (picked * scale[:, :, None, None, None, :]).astype(jnp.bfloat16)  2.61 us
    gather x1, local copies, waits for them, and re-layouts, body(): picked = jnp.take(gathered, targets - first_energy + local_count, axis=0)  2 us
  transfers between devices with their start and end apart: 8, of which 7 were waited for; matrix products, arithmetic and copies ran while one was open for 16% of the time, Pallas kernels for 0%

commit v1 on v0

v1 whole, which is shorter than its diff:
```python
import functools

import jax
import jax.numpy as jnp
from jax import lax
from jax.experimental import pallas as pl
from jax.experimental.pallas import tpu as pltpu
from jax.sharding import PartitionSpec as P

SWEEPS = 4
F32 = jnp.float32
BF16 = jnp.bfloat16
AXES = ("energy", "space")


def times_i(pair, sign):
    half = pair.shape[1] // 2
    real, imag = pair[:, :half], pair[:, half:]
    if sign > 0:
        return jnp.concatenate([-imag, real], axis=1)
    return jnp.concatenate([imag, -real], axis=1)


def product(matrix, pair):
    out = jnp.dot(matrix[0], pair, preferred_element_type=F32)
    return out + jnp.dot(matrix[1], times_i(pair, 1), preferred_element_type=F32)


def transposed_dot(matrix, pair):
    return lax.dot_general(matrix, pair, (((0,), (0,)), ((), ())), preferred_element_type=F32)


def adjoint(matrix, pair):
    out = transposed_dot(matrix[0], pair)
    return out + transposed_dot(matrix[1], times_i(pair, -1))


def joined(ref, slab):
    return jnp.concatenate([ref[slab, 0], ref[slab, 1]], axis=1)


def first_kernel(side, where, precond, coupling, source, states, send):
    odd = where[0]
    slab = odd if side else 1 - odd
    right = slab == 1
    fresh = product(precond.at[slab], joined(source, slab).astype(BF16)).astype(BF16)
    states[...] = fresh

    @pl.when(right)
    def _():
        send[...] = adjoint(coupling.at[1], fresh).astype(BF16)

    @pl.when(jnp.logical_not(right))
    def _():
        send[...] = fresh


def base_kernel(where, coupling, source, sigma, states_a, states_b, base_a, base_b):
    def local(slab, states):
        rows = states.shape[0]
        padded = jnp.concatenate([sigma[slab], jnp.zeros((6, rows), F32)], axis=0)
        columns = jnp.transpose(padded)
        real, imag = columns[:, 0:1], columns[:, 1:2]
        wide = states.astype(F32)
        half = wide.shape[1] // 2
        turned = jnp.concatenate([-wide[:, half:], wide[:, :half]], axis=1)
        return joined(source, slab) + (real * wide + imag * turned)

    def both(states_left, states_right, base_left, base_right):
        left, right = states_left[...], states_right[...]
        base_left[...] = local(0, left) + product(coupling.at[0], right)
        handed = adjoint(coupling.at[0], left).astype(BF16).astype(F32)
        base_right[...] = local(1, right) + handed

    @pl.when(where[0] == 0)
    def _():
        both(states_b, states_a, base_b, base_a)

    @pl.when(where[0] != 0)
    def _():
        both(states_a, states_b, base_a, base_b)


def step_kernel(side, last, where, precond, coupling, base, arrived, states, *rest):
    odd, inner = where[0], where[1]
    slab = odd if side else 1 - odd
    right = slab == 1

    @pl.when(right)
    def _():
        message = arrived[...]
        if side:
            message = jnp.where(inner != 0, message, jnp.zeros_like(message))
        driven = (base[...] + product(coupling.at[1], message)).astype(BF16)
        fresh = product(precond.at[1], driven).astype(BF16)
        states[...] = fresh
        if not last:
            rest[0][...] = adjoint(coupling.at[1], fresh).astype(BF16)

    @pl.when(jnp.logical_not(right))
    def _():
        message = arrived[...]
        if side:
            message = jnp.where(inner != 0, message, jnp.zeros_like(message))
        driven = (base[...] + message.astype(F32)).astype(BF16)
        fresh = product(precond.at[0], driven).astype(BF16)
        states[...] = fresh
        if not last:
            rest[0][...] = fresh


def sigma_kernel(step_rows, where, own, other, scales, *rest):
    lesser, greater, scaled = rest[-3:]
    step = pl.program_id(0)

    @pl.when(step == 0)
    def _():
        for at, states in ((0, own), (1, other)):
            wide = states[...].astype(F32)
            for kind in range(2):
                scaled[2 * at + kind] = (wide * scales[2 * at + kind][None, :]).astype(BF16)

    rows = pl.ds(pl.multiple_of(step * step_rows, step_rows), step_rows)
    contract = (((1,), (1,)), ((), ()))
    for kind, out in ((0, lesser), (1, greater)):
        real, imag = None, None
        for at, states in ((0, own), (1, other)):
            pair = states[rows, :]
            weighted = scaled[2 * at + kind]
            real_part = lax.dot_general(pair, weighted, contract, preferred_element_type=F32)
            imag_part = lax.dot_general(
                times_i(pair, -1), weighted, contract, preferred_element_type=F32
            )
            real = real_part if real is None else real + real_part
            imag = imag_part if imag is None else imag + imag_part
        out[0] = real.astype(BF16)
        out[1] = imag.astype(BF16)


def whole(count):
    return [pl.BlockSpec(memory_space=pltpu.VMEM)] * count


SCALAR = pl.BlockSpec(memory_space=pltpu.SMEM)


def call(kernel, outs, flops, read, *args):
    return pl.pallas_call(
        kernel,
        out_shape=outs,
        in_specs=[SCALAR] + whole(len(args) - 1),
        out_specs=whole(len(outs)),
        compiler_params=pltpu.CompilerParams(vmem_limit_bytes=24 * 2**20),
        cost_estimate=pl.CostEstimate(flops=flops, bytes_accessed=read, transcendentals=0),
    )(*args)


def self_blocks(where, own, other, scales, blocks, previous):
    rows, width = own.shape
    step_rows = rows // 2
    spec = pl.BlockSpec((None, 2, step_rows, rows), lambda step, at: (at[0], 0, step, 0))
    held = pl.BlockSpec((rows, width), lambda step, at: (0, 0))
    aliases = {} if previous is None else {4: 0, 5: 1}
    kept = [] if previous is None else [pl.BlockSpec(memory_space=pl.ANY)] * 2
    return pl.pallas_call(
        functools.partial(sigma_kernel, step_rows),
        out_shape=[jax.ShapeDtypeStruct(blocks, BF16)] * 2,
        grid_spec=pltpu.PrefetchScalarGridSpec(
            num_scalar_prefetch=1,
            grid=(rows // step_rows,),
            in_specs=[held, held, pl.BlockSpec(scales.shape, lambda step, at: (0, 0))] + kept,
            out_specs=[spec, spec],
            scratch_shapes=[pltpu.VMEM((4, rows, width), BF16)],
        ),
        input_output_aliases=aliases,
        compiler_params=pltpu.CompilerParams(vmem_limit_bytes=24 * 2**20),
        cost_estimate=pl.CostEstimate(
            flops=16 * rows * rows * width, bytes_accessed=8 * rows * rows, transcendentals=0
        ),
    )(where, own, other, scales, *([] if previous is None else previous))


def body(energies, chips, precond, coupling, source, sigma_ret, occupation, shift_offsets, shift_weights):
    _, slabs, _, rows, modes = source.shape
    width = 2 * modes
    energy, chip = lax.axis_index("energy"), lax.axis_index("space")
    odd = lax.rem(chip, 2)
    inner = jnp.logical_and(chip > 0, chip < chips - 1).astype(jnp.int32)
    where = jnp.stack([odd, inner]).astype(jnp.int32)

    def at(e, c):
        return e * chips + c

    pairing_a, pairing_b = [], []
    for e in range(energies):
        for c in range(chips):
            pairing_a.append((at(e, c), at(e, c ^ 1)))
            if 0 < c < chips - 1:
                pairing_b.append((at(e, c), at(e, ((c + 1) ^ 1) - 1)))
            else:
                pairing_b.append((at(e, c), at(e ^ 1, c)))
    swap = [(at(e, c), at(e ^ 1, c)) for e in range(energies) for c in range(chips)]

    precond, source, sigma = precond[0], source[0], sigma_ret[0]
    pair = jax.ShapeDtypeStruct((rows, width), BF16)
    total = jax.ShapeDtypeStruct((rows, width), F32)
    one = 4 * rows * rows * width
    big, small = 4 * rows * rows, 2 * rows * width

    states, sends, arrived = [None, None], [None, None], [None, None]
    pairings = (pairing_a, pairing_b)
    for side in range(2):
        states[side], sends[side] = call(
            functools.partial(first_kernel, side),
            [pair, pair],
            2 * one,
            2 * big + 4 * small,
            where,
            precond,
            coupling,
            source,
        )
        arrived[side] = lax.ppermute(sends[side], AXES, pairings[side])
    for sweep in range(1, SWEEPS):
        last = sweep == SWEEPS - 1
        bases = call(
            base_kernel, [total, total], 2 * one, 2 * big + 10 * small, where, coupling, source, sigma, *states
        )
        states = list(states)
        for side in range(2):
            results = call(
                functools.partial(step_kernel, side, last),
                [pair] if last else [pair, pair],
                3 * one,
                2 * big + 5 * small,
                where,
                precond,
                coupling,
                bases[side],
                arrived[side],
            )
            states[side] = results[0]
            if not last:
                arrived[side] = lax.ppermute(results[1], AXES, pairings[side])

    offsets = lax.dynamic_index_in_dim(shift_offsets, energy, 0, keepdims=False)
    weights = lax.dynamic_index_in_dim(shift_weights, energy, 0, keepdims=False) / modes
    scales = []
    for target in (energy, energy ^ 1):
        weight = jnp.sum(jnp.where(energy + offsets == target, weights, jnp.zeros_like(weights)))
        occupied = lax.dynamic_index_in_dim(occupation, target, 0, keepdims=False)
        for filled in (occupied, 1.0 - occupied):
            scales.append(jnp.tile(weight * filled, 2))
    scales = jnp.stack(scales)
    blocks = None
    for side in range(2):
        other = lax.ppermute(states[side], AXES, swap)
        slab = odd if side else 1 - odd
        blocks = self_blocks(
            slab[None].astype(jnp.int32), states[side], other, scales, (slabs, 2, rows, rows), blocks
        )
    return tuple(block[None] for block in blocks)


def solution(mesh):
    energies, chips = mesh.shape["energy"], mesh.shape["space"]
    placed = (
        P("energy", "space", None, None, None),
        P("space", None, None, None),
        P("energy", "space", None, None, None),
        P("energy", "space", None, None),
        P(),
        P(),
        P(),
    )
    return jax.shard_map(
        functools.partial(body, energies, chips),
        mesh=mesh,
        in_specs=placed,
        out_specs=(P("energy", "space", None, None, None), P("energy", "space", None, None, None)),
        check_vma=False,
    )
```

time: 89.4 us -> 62.1 us (0.69)
  the two profiles are of different devices: /device:TPU:25 before, /device:TPU:29 now
where the time goes in v1:
time: 62.1 us; the launch traced here: 61.8 us
  Pallas kernels  24.2 us (39%)
  waiting for transfers between devices  16.8 us (27%)
  starting transfers between devices  11.7 us (19%)
  local copies, waits for them, and re-layouts  6.1 us (10%)
  other arithmetic  2.03 us (3%)
  between operations  0.86 us (1%)
    pallas_call x11, Pallas kernels, call(): pl.pallas_call(kernel, out_shape=outs, in_specs=[SCALAR] + whole(len(args...  18.9 us
    ppermute x2, starting transfers between devices, body(): other = lax.ppermute(states[side], AXES, swap)  9.05 us
    ppermute x4, waiting for transfers between devices, body(): arrived[side] = lax.ppermute(results[1], AXES, pairings[side])  8.62 us
    ppermute x2, waiting for transfers between devices, body(): arrived[side] = lax.ppermute(sends[side], AXES, pairings[side])  8.22 us
    unnamed x24, local copies, waits for them, and re-layouts  6.09 us
    pallas_call x2, Pallas kernels, self_blocks(): pl.pallas_call(functools.partial(sigma_kernel, step_rows), out_shape=[jax...  5.36 us
    ppermute x2, starting transfers between devices, body(): arrived[side] = lax.ppermute(sends[side], AXES, pairings[side])  2.01 us
    another operation x1, other arithmetic, body(): scales.append(jnp.tile(weight * filled, 2))  1.26 us
  transfers between devices with their start and end apart: 8, of which 2 were waited for; matrix products, arithmetic and copies ran while one was open for 3% of the time, Pallas kernels for 33%

profile of v1, /device:TPU:29, one launch (start us, length us, event | category | flops | bytes accessed | tf_op | source)
XLA Modules:
  0.0 61.8 jit_solution(9421228731467914592)
XLA Ops:
  0.6 0.1 pad_add_fusion.where
  0.7 0.0 copy-start
  0.7 1.6 %copy-done = bf16[2,2,512,512]{3,2,1,0:T(8,128)(2,1)S(1)} copy-done((bf16[2,2,512,512]{3,2,1,0:T(8,128)(2,1)S(1)}, bf16[2,2,512,512]{3,2,1,0:T(8,128)(2,1)}, u32[]{:S(2)}) %copy-start) | copy-done | bytes 2097176
  2.3 0.0 copy-start.2
  2.3 1.6 %copy-done.2 = bf16[1,2,2,512,512]{4,3,2,1,0:T(8,128)(2,1)S(1)} copy-done((bf16[1,2,2,512,512]{4,3,2,1,0:T(8,128)(2,1)S(1)}, bf16[1,2,2,512,512]{4,3,2,1,0:T(8,128)(2,1)}, u32[]{:S(2)}) %copy-start.2) | copy-done | bytes 2097176
  3.9 0.0 copy-start.4
  3.9 1.2 %copy-done.4 = f32[1,2,2,512,128]{4,3,2,1,0:T(8,128)S(1)} copy-done((f32[1,2,2,512,128]{4,3,2,1,0:T(8,128)S(1)}, f32[1,2,2,512,128]{4,3,2,1,0:T(8,128)}, u32[]{:S(2)}) %copy-start.4) | copy-done | bytes 1048600
  5.1 1.5 %shard_map.86 = (bf16[512,256]{1,0:T(8,128)(2,1)S(1)}, bf16[512,256]{1,0:T(8,128)(2,1)S(1)}) custom-call(s32[2]{0:T(128)S(1)} %pad_add_fusion.where, bf16[2,2,512,512]{3,2,1,0:T(8,128)(2,1)S(1)} %bitcast.20, bf16[2,2,512,512]{3,2,1,0:T(8,128)(2,1)S(1)} %copy-done, f32[2,2,512,128]{3,2,1,0:T(8,128)S(1)} %bitcast.28), custom_call_target="tpu_custom_call" | custom-call | flops 536870912 | bytes 3145728 | tf_op jit(solution)/shard_map/pallas_call | solution.py:148
  6.6 0.0 copy-start.1
  6.6 0.0 copy-start.5
  6.6 0.0 copy-start.8
  6.6 0.8 %collective-permute-start = (bf16[512,256]{1,0:T(8,128)(2,1)S(1)}, bf16[512,256]{1,0:T(8,128)(2,1)S(1)}, u32[]{:S(2)}, u32[]{:S(2)}) collective-permute-start(bf16[512,256]{1,0:T(8,128)(2,1)S(1)} %get-tuple-element.27), channel_id=1, source_target_pairs={{0,1},{1,0},{2,3},{3,2},{4,5},{5,4},{6,7},{7,6},{8,9},{9,8},{10,11... | collective-permute-start | bytes 786440 | tf_op jit(solution)/shard_map/ppermute | solution.py:223
  7.4 1.0 %shard_map.87 = (bf16[512,256]{1,0:T(8,128)(2,1)S(1)}, bf16[512,256]{1,0:T(8,128)(2,1)S(1)}) custom-call(s32[2]{0:T(128)S(1)} %pad_add_fusion.where, bf16[2,2,512,512]{3,2,1,0:T(8,128)(2,1)S(1)} %bitcast.21, bf16[2,2,512,512]{3,2,1,0:T(8,128)(2,1)S(1)} %copy-done, f32[2,2,512,128]{3,2,1,0:T(8,128)S(1)} %bitcast.29), custom_call_target="tpu_custom_call" | custom-call | flops 536870912 | bytes 3145728 | tf_op jit(solution)/shard_map/pallas_call | solution.py:148
  8.5 1.2 %collective-permute-start.1 = (bf16[512,256]{1,0:T(8,128)(2,1)S(1)}, bf16[512,256]{1,0:T(8,128)(2,1)S(1)}, u32[]{:S(2)}, u32[]{:S(2)}) collective-permute-start(bf16[512,256]{1,0:T(8,128)(2,1)S(1)} %get-tuple-element.30), channel_id=1, source_target_pairs={{0,16},{1,2},{2,1},{3,4},{4,3},{5,6},{6,5},{7,8},{8,7},{9,10},{10,... | collective-permute-start | bytes 786440 | tf_op jit(solution)/shard_map/ppermute | solution.py:223
  9.7 0.0 copy-done.1
  9.7 0.0 copy-done.5
  9.7 0.0 copy-done.8
  9.7 1.6 %shard_map.88 = (f32[512,256]{1,0:T(8,128)S(1)}, f32[512,256]{1,0:T(8,128)S(1)}) custom-call(s32[2]{0:T(128)S(1)} %pad_add_fusion.where, bf16[2,2,512,512]{3,2,1,0:T(8,128)(2,1)S(1)} %copy-done.1, f32[2,2,512,128]{3,2,1,0:T(8,128)S(1)} %bitcast.30, f32[2,2,512]{2,1,0:T(2,128)S(1)} %bitcast.33, bf16[512,256]{1,0:T(8,128)(2,1)S(1)} %get-tuple-element.24.states_a, ...), custom_call_target="tpu_custom_call" | custom-call | flops 536870912 | bytes 4718592 | tf_op jit(solution)/shard_map/pallas_call | solution.py:148
  11.3 8.2 %collective-permute-done.arrived = bf16[512,256]{1,0:T(8,128)(2,1)S(1)} collective-permute-done((bf16[512,256]{1,0:T(8,128)(2,1)S(1)}, bf16[512,256]{1,0:T(8,128)(2,1)S(1)}, u32[]{:S(2)}, u32[]{:S(2)}) %collective-permute-start) | collective-permute-done | bytes 262176 | tf_op jit(solution)/shard_map/ppermute | solution.py:223
  19.5 2.2 %shard_map.89 = (bf16[512,256]{1,0:T(8,128)(2,1)S(1)}, bf16[512,256]{1,0:T(8,128)(2,1)S(1)}) custom-call(s32[2]{0:T(128)S(1)} %pad_add_fusion.where, bf16[2,2,512,512]{3,2,1,0:T(8,128)(2,1)S(1)} %bitcast.22, bf16[2,2,512,512]{3,2,1,0:T(8,128)(2,1)S(1)} %copy-done.1, f32[512,256]{1,0:T(8,128)S(1)} %get-tuple-element.26.base, ...), custom_call_target="tpu_custom_call" | custom-call | flops 805306368 | bytes 3407872 | tf_op jit(solution)/shard_map/pallas_call | solution.py:148
  21.7 0.1 collective-permute-start.2
  21.7 0.0 collective-permute-done.1.arrived
  21.8 1.0 %shard_map.90 = (bf16[512,256]{1,0:T(8,128)(2,1)S(1)}, bf16[512,256]{1,0:T(8,128)(2,1)S(1)}) custom-call(s32[2]{0:T(128)S(1)} %pad_add_fusion.where, bf16[2,2,512,512]{3,2,1,0:T(8,128)(2,1)S(1)} %bitcast.23, bf16[2,2,512,512]{3,2,1,0:T(8,128)(2,1)S(1)} %copy-done.1, f32[512,256]{1,0:T(8,128)S(1)} %get-tuple-element.29.base, ...), custom_call_target="tpu_custom_call" | custom-call | flops 805306368 | bytes 3407872 | tf_op jit(solution)/shard_map/pallas_call | solution.py:148
  22.8 0.6 collective-permute-start.3
  23.4 1.6 %shard_map.91 = (f32[512,256]{1,0:T(8,128)S(1)}, f32[512,256]{1,0:T(8,128)S(1)}) custom-call(s32[2]{0:T(128)S(1)} %pad_add_fusion.where, bf16[2,2,512,512]{3,2,1,0:T(8,128)(2,1)S(1)} %copy-done.1, f32[2,2,512,128]{3,2,1,0:T(8,128)S(1)} %bitcast.31, f32[2,2,512]{2,1,0:T(2,128)S(1)} %bitcast.34, bf16[512,256]{1,0:T(8,128)(2,1)S(1)} %get-tuple-element.28.states_a, ...), custom_call_target="tpu_custom_call" | custom-call | flops 536870912 | bytes 4718592 | tf_op jit(solution)/shard_map/pallas_call | solution.py:148
  25.0 8.6 %collective-permute-done.2.arrived = bf16[512,256]{1,0:T(8,128)(2,1)S(1)} collective-permute-done((bf16[512,256]{1,0:T(8,128)(2,1)S(1)}, bf16[512,256]{1,0:T(8,128)(2,1)S(1)}, u32[]{:S(2)}, u32[]{:S(2)}) %collective-permute-start.2) | collective-permute-done | bytes 262176 | tf_op jit(solution)/shard_map/ppermute | solution.py:244
  33.6 2.9 %shard_map.92 = (bf16[512,256]{1,0:T(8,128)(2,1)S(1)}, bf16[512,256]{1,0:T(8,128)(2,1)}) custom-call(s32[2]{0:T(128)S(1)} %pad_add_fusion.where, bf16[2,2,512,512]{3,2,1,0:T(8,128)(2,1)S(1)} %bitcast.24, bf16[2,2,512,512]{3,2,1,0:T(8,128)(2,1)S(1)} %copy-done.1, f32[512,256]{1,0:T(8,128)S(1)} %get-tuple-element.32.base, ...), custom_call_target="tpu_custom_call" | custom-call | flops 805306368 | bytes 3407872 | tf_op jit(solution)/shard_map/pallas_call | solution.py:148
  36.5 0.0 collective-permute-start.6
  36.5 0.0 collective-permute-done.3.arrived
  36.5 0.0 copy-start.10
  36.5 0.0 copy-start.11
  36.5 1.7 %shard_map.93 = (bf16[512,256]{1,0:T(8,128)(2,1)S(1)}, bf16[512,256]{1,0:T(8,128)(2,1)}) custom-call(s32[2]{0:T(128)S(1)} %pad_add_fusion.where, bf16[2,2,512,512]{3,2,1,0:T(8,128)(2,1)S(1)} %bitcast.25, bf16[2,2,512,512]{3,2,1,0:T(8,128)(2,1)S(1)} %copy-done.1, f32[512,256]{1,0:T(8,128)S(1)} %get-tuple-element.35.base, ...), custom_call_target="tpu_custom_call" | custom-call | flops 805306368 | bytes 3407872 | tf_op jit(solution)/shard_map/pallas_call | solution.py:148
  38.2 0.0 copy-start.6
  38.2 0.7 %copy-done.6 = bf16[512,256]{1,0:T(8,128)(2,1)} copy-done((bf16[512,256]{1,0:T(8,128)(2,1)}, bf16[512,256]{1,0:T(8,128)(2,1)S(1)}, u32[]{:S(2)}) %copy-start.6) | copy-done | bytes 262168
  38.9 0.0 collective-permute-start.4
  38.9 0.0 copy-done.10
  38.9 0.0 copy-done.11
  38.9 0.0 copy-start.3
  38.9 0.7 %fusion.2 = (f32[]{:T(128)}, f32[]{:T(128)}) fusion(s32[]{:T(128)S(6)} %axis_index.25, f32[2,4]{1,0:T(2,128)S(1)} %copy-done.10, s32[]{:T(128)S(6)} %select_n.20, s32[2,4]{1,0:T(2,128)S(1)} %copy-done.11, s32[]{:T(128)S(6)} %xor.3), kind=kLoop, calls=%fused_computation.9 | loop fusion | flops 30 | bytes 52 | tf_op jit(solution)/shard_map/reduce_sum | solution.py:250
  39.6 0.0 copy-start.7
  39.6 0.9 %copy-done.7 = bf16[512,256]{1,0:T(8,128)(2,1)S(1)} copy-done((bf16[512,256]{1,0:T(8,128)(2,1)S(1)}, bf16[512,256]{1,0:T(8,128)(2,1)}, u32[]{:S(2)}) %copy-start.7) | copy-done | bytes 262168
  40.6 1.8 %shard_map.94 = (f32[512,256]{1,0:T(8,128)S(1)}, f32[512,256]{1,0:T(8,128)S(1)}) custom-call(s32[2]{0:T(128)S(1)} %pad_add_fusion.where, bf16[2,2,512,512]{3,2,1,0:T(8,128)(2,1)S(1)} %copy-done.1, f32[2,2,512,128]{3,2,1,0:T(8,128)S(1)} %bitcast.32, f32[2,2,512]{2,1,0:T(2,128)S(1)} %bitcast.35, bf16[512,256]{1,0:T(8,128)(2,1)S(1)} %get-tuple-element.34.states_a, ...), custom_call_target="tpu_custom_call" | custom-call | flops 536870912 | bytes 4718592 | tf_op jit(solution)/shard_map/pallas_call | solution.py:148
  42.3 0.0 collective-permute-done.6.arrived
  42.4 0.0 copy-done.3
  42.4 2.2 %shard_map.96.own = bf16[512,256]{1,0:T(8,128)(2,1)S(1)} custom-call(s32[2]{0:T(128)S(1)} %pad_add_fusion.where, bf16[2,2,512,512]{3,2,1,0:T(8,128)(2,1)S(1)} %bitcast.26, bf16[2,2,512,512]{3,2,1,0:T(8,128)(2,1)S(1)} %copy-done.1, f32[512,256]{1,0:T(8,128)S(1)} %get-tuple-element.40.base, bf16[512,256]{1,0:T(8,128)(2,1)} %collective-permute-done.6.arrived), custom_call_target="tpu_custom_call" | custom-call | flops 805306368 | bytes 3407872 | tf_op jit(solution)/shard_map/pallas_call | solution.py:148
  44.6 9.0 %collective-permute-start.7 = (bf16[512,256]{1,0:T(8,128)(2,1)S(1)}, bf16[512,256]{1,0:T(8,128)(2,1)S(1)}, u32[]{:S(2)}, u32[]{:S(2)}) collective-permute-start(bf16[512,256]{1,0:T(8,128)(2,1)S(1)} %shard_map.96.own), channel_id=1, source_target_pairs={{0,16},{1,17},{2,18},{3,19},{4,20},{5,21},{6,22},{7,23},{8,24},{9,... | collective-permute-start | bytes 786440 | tf_op jit(solution)/shard_map/ppermute | solution.py:257
  53.6 0.0 collective-permute-done.4.arrived
  53.6 0.0 copy-start.9
  53.6 1.4 %shard_map.95.own = bf16[512,256]{1,0:T(8,128)(2,1)S(1)} custom-call(s32[2]{0:T(128)S(1)} %pad_add_fusion.where, bf16[2,2,512,512]{3,2,1,0:T(8,128)(2,1)S(1)} %bitcast.27, bf16[2,2,512,512]{3,2,1,0:T(8,128)(2,1)S(1)} %copy-done.1, f32[512,256]{1,0:T(8,128)S(1)} %get-tuple-element.38.base, bf16[512,256]{1,0:T(8,128)(2,1)} %collective-permute-done.4.arrived), custom_call_target="tpu_custom_call" | custom-call | flops 805306368 | bytes 3407872 | tf_op jit(solution)/shard_map/pallas_call | solution.py:148
  55.0 0.1 collective-permute-start.5
  55.1 0.0 copy-done.9
  55.1 1.3 %multiply_bitcast_fusion.3 = (f32[128]{0:T(128)S(1)}, f32[128]{0:T(128)S(1)}, f32[128]{0:T(128)S(1)}, f32[128]{0:T(128)S(1)}) fusion(f32[]{:T(128)} %get-tuple-element.46, f32[2,128]{1,0:T(2,128)S(1)} %copy-done.9, s32[]{:T(128)S(6)} %select_n.20, s32[]{:T(128)S(6)} %select_n.23, f32[]{:T(128)} %get-tuple-element.47), kind=kLoop, calls=%fused_computation.15 | loop fusion | flops 768 | bytes 3088 | tf_op jit(solution)/shard_map/tile | solution.py:253
  56.4 0.0 collective-permute-done.7.other
  56.5 2.7 %shard_map.97 = (bf16[2,2,512,512]{3,2,1,0:T(8,128)(2,1)}, bf16[2,2,512,512]{3,2,1,0:T(8,128)(2,1)}) custom-call(s32[1]{0:T(128)} %bitcast.13.where, bf16[512,256]{1,0:T(8,128)(2,1)S(1)} %shard_map.96.own, bf16[512,256]{1,0:T(8,128)(2,1)S(1)} %collective-permute-done.7.other, f32[4,256]{1,0:T(4,128)S(1)} %pad_maximum_fusion.scales), custom_call_target="tpu_custom_call" | custom-call | flops 1073741824 | bytes 2097152 | tf_op jit(solution)/shard_map/pallas_call | solution.py:165
  59.2 0.0 collective-permute-done.5.other
  59.2 2.7 %shard_map.98 = (bf16[2,2,512,512]{3,2,1,0:T(8,128)(2,1)}, bf16[2,2,512,512]{3,2,1,0:T(8,128)(2,1)}) custom-call(s32[1]{0:T(128)} %bitcast.where, bf16[512,256]{1,0:T(8,128)(2,1)S(1)} %shard_map.95.own, bf16[512,256]{1,0:T(8,128)(2,1)S(1)} %collective-permute-done.5.other, ...), custom_call_target="tpu_custom_call", output_to_operand_aliasing={{0}: (4, {}), {1}: (5, {})} | custom-call | flops 1073741824 | bytes 2097152 | tf_op jit(solution)/shard_map/pallas_call | solution.py:165
  (5 shorter events, 0.0 us)
Async XLA Ops:
  0.7 1.6 %copy-start = (bf16[2,2,512,512]{3,2,1,0:T(8,128)(2,1)S(1)}, bf16[2,2,512,512]{3,2,1,0:T(8,128)(2,1)}, u32[]{:S(2)}) copy-start(bf16[2,2,512,512]{3,2,1,0:T(8,128)(2,1)} %coupling.21) | copy-start | bytes 6291460
  2.3 1.6 %copy-start.2 = (bf16[1,2,2,512,512]{4,3,2,1,0:T(8,128)(2,1)S(1)}, bf16[1,2,2,512,512]{4,3,2,1,0:T(8,128)(2,1)}, u32[]{:S(2)}) copy-start(bf16[1,2,2,512,512]{4,3,2,1,0:T(8,128)(2,1)} %param.7) | copy-start | bytes 6291460
  3.9 1.2 %copy-start.4 = (f32[1,2,2,512,128]{4,3,2,1,0:T(8,128)S(1)}, f32[1,2,2,512,128]{4,3,2,1,0:T(8,128)}, u32[]{:S(2)}) copy-start(f32[1,2,2,512,128]{4,3,2,1,0:T(8,128)} %param.9) | copy-start | bytes 3145732
  6.6 3.1 %copy-start.1 = (bf16[2,2,512,512]{3,2,1,0:T(8,128)(2,1)S(1)}, bf16[2,2,512,512]{3,2,1,0:T(8,128)(2,1)}, u32[]{:S(2)}) copy-start(bf16[2,2,512,512]{3,2,1,0:T(8,128)(2,1)} %coupling.21) | copy-start | bytes 6291460
  6.6 3.0 %copy-start.5 = (f32[1,2,2,512,128]{4,3,2,1,0:T(8,128)S(1)}, f32[1,2,2,512,128]{4,3,2,1,0:T(8,128)}, u32[]{:S(2)}) copy-start(f32[1,2,2,512,128]{4,3,2,1,0:T(8,128)} %param.9) | copy-start | bytes 3145732
  6.6 3.0 %copy-start.8 = (f32[1,2,2,512]{3,2,1,0:T(2,128)S(1)}, f32[1,2,2,512]{3,2,1,0:T(2,128)}, u32[]{:S(2)}) copy-start(f32[1,2,2,512]{3,2,1,0:T(2,128)} %param.10) | copy-start | bytes 24580
  6.6 12.9 %collective-permute-start = (bf16[512,256]{1,0:T(8,128)(2,1)S(1)}, bf16[512,256]{1,0:T(8,128)(2,1)S(1)}, u32[]{:S(2)}, u32[]{:S(2)}) collective-permute-start(bf16[512,256]{1,0:T(8,128)(2,1)S(1)} %get-tuple-element.27), channel_id=1, source_target_pairs={{0,1},{1,0},{2,3},{3,2},{4,5},{5,4},{6,7},{7,6},{8,9},{9,8},{10,11... | collective-permute-start | bytes 786440 | tf_op jit(solution)/shard_map/ppermute | solution.py:223
  8.5 13.3 %collective-permute-start.1 = (bf16[512,256]{1,0:T(8,128)(2,1)S(1)}, bf16[512,256]{1,0:T(8,128)(2,1)S(1)}, u32[]{:S(2)}, u32[]{:S(2)}) collective-permute-start(bf16[512,256]{1,0:T(8,128)(2,1)S(1)} %get-tuple-element.30), channel_id=1, source_target_pairs={{0,16},{1,2},{2,1},{3,4},{4,3},{5,6},{6,5},{7,8},{8,7},{9,10},{10,... | collective-permute-start | bytes 786440 | tf_op jit(solution)/shard_map/ppermute | solution.py:223
  21.7 11.9 %collective-permute-start.2 = (bf16[512,256]{1,0:T(8,128)(2,1)S(1)}, bf16[512,256]{1,0:T(8,128)(2,1)S(1)}, u32[]{:S(2)}, u32[]{:S(2)}) collective-permute-start(bf16[512,256]{1,0:T(8,128)(2,1)S(1)} %get-tuple-element.33), channel_id=1, source_target_pairs={{0,1},{1,0},{2,3},{3,2},{4,5},{5,4},{6,7},{7,6},{8,9},{9,8},{10,11... | collective-permute-start | bytes 786440 | tf_op jit(solution)/shard_map/ppermute | solution.py:244
  22.8 13.7 %collective-permute-start.3 = (bf16[512,256]{1,0:T(8,128)(2,1)S(1)}, bf16[512,256]{1,0:T(8,128)(2,1)S(1)}, u32[]{:S(2)}, u32[]{:S(2)}) collective-permute-start(bf16[512,256]{1,0:T(8,128)(2,1)S(1)} %get-tuple-element.36), channel_id=1, source_target_pairs={{0,16},{1,2},{2,1},{3,4},{4,3},{5,6},{6,5},{7,8},{8,7},{9,10},{10,... | collective-permute-start | bytes 786440 | tf_op jit(solution)/shard_map/ppermute | solution.py:244
  36.5 5.9 %collective-permute-start.6 = (bf16[512,256]{1,0:T(8,128)(2,1)}, bf16[512,256]{1,0:T(8,128)(2,1)}, u32[]{:S(2)}, u32[]{:S(2)}) collective-permute-start(bf16[512,256]{1,0:T(8,128)(2,1)} %get-tuple-element.41), channel_id=1, source_target_pairs={{0,1},{1,0},{2,3},{3,2},{4,5},{5,4},{6,7},{7,6},{8,9},{9,8},{10,11... | collective-permute-start | bytes 786440 | tf_op jit(solution)/shard_map/ppermute | solution.py:244
  36.5 2.4 %copy-start.10 = (f32[2,4]{1,0:T(2,128)S(1)}, f32[2,4]{1,0:T(2,128)}, u32[]{:S(2)}) copy-start(f32[2,4]{1,0:T(2,128)} %param.13) | copy-start | bytes 100
  36.5 2.4 %copy-start.11 = (s32[2,4]{1,0:T(2,128)S(1)}, s32[2,4]{1,0:T(2,128)}, u32[]{:S(2)}) copy-start(s32[2,4]{1,0:T(2,128)} %param.12) | copy-start | bytes 100
  38.2 0.7 %copy-start.6 = (bf16[512,256]{1,0:T(8,128)(2,1)}, bf16[512,256]{1,0:T(8,128)(2,1)S(1)}, u32[]{:S(2)}) copy-start(bf16[512,256]{1,0:T(8,128)(2,1)S(1)} %get-tuple-element.37.states_b) | copy-start | bytes 786436
  38.9 14.7 %collective-permute-start.4 = (bf16[512,256]{1,0:T(8,128)(2,1)}, bf16[512,256]{1,0:T(8,128)(2,1)}, u32[]{:S(2)}, u32[]{:S(2)}) collective-permute-start(bf16[512,256]{1,0:T(8,128)(2,1)} %get-tuple-element.39), channel_id=1, source_target_pairs={{0,16},{1,2},{2,1},{3,4},{4,3},{5,6},{6,5},{7,8},{8,7},{9,10},{10,... | collective-permute-start | bytes 786440 | tf_op jit(solution)/shard_map/ppermute | solution.py:244
  38.9 3.4 %copy-start.3 = (bf16[1,2,2,512,512]{4,3,2,1,0:T(8,128)(2,1)S(1)}, bf16[1,2,2,512,512]{4,3,2,1,0:T(8,128)(2,1)}, u32[]{:S(2)}) copy-start(bf16[1,2,2,512,512]{4,3,2,1,0:T(8,128)(2,1)} %param.7) | copy-start | bytes 6291460
  39.6 0.9 %copy-start.7 = (bf16[512,256]{1,0:T(8,128)(2,1)S(1)}, bf16[512,256]{1,0:T(8,128)(2,1)}, u32[]{:S(2)}) copy-start(bf16[512,256]{1,0:T(8,128)(2,1)} %copy-done.6) | copy-start | bytes 786436
  44.6 11.8 %collective-permute-start.7 = (bf16[512,256]{1,0:T(8,128)(2,1)S(1)}, bf16[512,256]{1,0:T(8,128)(2,1)S(1)}, u32[]{:S(2)}, u32[]{:S(2)}) collective-permute-start(bf16[512,256]{1,0:T(8,128)(2,1)S(1)} %shard_map.96.own), channel_id=1, source_target_pairs={{0,16},{1,17},{2,18},{3,19},{4,20},{5,21},{6,22},{7,23},{8,24},{9,... | collective-permute-start | bytes 786440 | tf_op jit(solution)/shard_map/ppermute | solution.py:257
  53.6 1.5 %copy-start.9 = (f32[2,128]{1,0:T(2,128)S(1)}, f32[2,128]{1,0:T(2,128)}, u32[]{:S(2)}) copy-start(f32[2,128]{1,0:T(2,128)} %param.11) | copy-start | bytes 3076
  55.0 4.1 %collective-permute-start.5 = (bf16[512,256]{1,0:T(8,128)(2,1)S(1)}, bf16[512,256]{1,0:T(8,128)(2,1)S(1)}, u32[]{:S(2)}, u32[]{:S(2)}) collective-permute-start(bf16[512,256]{1,0:T(8,128)(2,1)S(1)} %shard_map.95.own), channel_id=1, source_target_pairs={{0,16},{1,17},{2,18},{3,19},{4,20},{5,21},{6,22},{7,23},{8,24},{9,... | collective-permute-start | bytes 786440 | tf_op jit(solution)/shard_map/ppermute | solution.py:257

commit v2 on v1

v2 whole, which is shorter than its diff:
```python
import functools

import jax
import jax.numpy as jnp
from jax import lax
from jax.experimental import pallas as pl
from jax.experimental.pallas import tpu as pltpu
from jax.sharding import PartitionSpec as P

SWEEPS = 4
F32 = jnp.float32
BF16 = jnp.bfloat16
AXES = ("energy", "space")


def times_i(pair, sign):
    half = pair.shape[1] // 2
    real, imag = pair[:, :half], pair[:, half:]
    if sign > 0:
        return jnp.concatenate([-imag, real], axis=1)
    return jnp.concatenate([imag, -real], axis=1)


def product(matrix, pair):
    out = jnp.dot(matrix[0], pair, preferred_element_type=F32)
    return out + jnp.dot(matrix[1], times_i(pair, 1), preferred_element_type=F32)


def transposed_dot(matrix, pair):
    return lax.dot_general(matrix, pair, (((0,), (0,)), ((), ())), preferred_element_type=F32)


def adjoint(matrix, pair):
    out = transposed_dot(matrix[0], pair)
    return out + transposed_dot(matrix[1], times_i(pair, -1))


def joined(ref, slab):
    return jnp.concatenate([ref[slab, 0], ref[slab, 1]], axis=1)


def load(source, held, sem):
    copy = pltpu.make_async_copy(source, held, sem)
    copy.start()
    return copy


def lead_kernel(where, precond, coupling, source, states, send, own, link, drive, sems):
    slab = where[0]
    copies = [
        load(source.at[slab], drive, sems.at[0]),
        load(precond.at[slab, 0], own.at[0], sems.at[1]),
        load(precond.at[slab, 1], own.at[1], sems.at[2]),
        load(coupling.at[1, 0], link.at[0], sems.at[3]),
        load(coupling.at[1, 1], link.at[1], sems.at[4]),
    ]
    copies[0].wait()
    pair = jnp.concatenate([drive[0], drive[1]], axis=1).astype(BF16)
    copies[1].wait()
    partial = jnp.dot(own[0], pair, preferred_element_type=F32)
    copies[2].wait()
    partial = partial + jnp.dot(own[1], times_i(pair, 1), preferred_element_type=F32)
    fresh = partial.astype(BF16)
    states[...] = fresh
    copies[3].wait()
    copies[4].wait()
    send_fresh(slab, link, fresh, send)


def trail_kernel(where, precond, coupling, source, link, states, send, own, inner, drive, sems):
    slab = 1 - where[0]
    copies = [
        load(source.at[slab], drive, sems.at[0]),
        load(precond.at[slab, 0], own.at[0], sems.at[1]),
        load(precond.at[slab, 1], own.at[1], sems.at[2]),
        load(coupling.at[0], inner, sems.at[3]),
    ]
    copies[0].wait()
    pair = jnp.concatenate([drive[0], drive[1]], axis=1).astype(BF16)
    copies[1].wait()
    partial = jnp.dot(own[0], pair, preferred_element_type=F32)
    copies[2].wait()
    partial = partial + jnp.dot(own[1], times_i(pair, 1), preferred_element_type=F32)
    fresh = partial.astype(BF16)
    states[...] = fresh
    send_fresh(slab, link, fresh, send)
    copies[3].wait()


def send_fresh(slab, link, fresh, send):
    @pl.when(slab == 1)
    def _():
        send[...] = adjoint(link, fresh).astype(BF16)

    @pl.when(slab == 0)
    def _():
        send[...] = fresh


def chain_kernel(where, own_a, own_b, link, chain):
    def write(own):
        rows = jnp.concatenate([link[0], link[1]], axis=1)
        both = product(own, rows)
        half = both.shape[1] // 2
        chain[0] = both[:, :half].astype(BF16)
        chain[1] = both[:, half:].astype(BF16)

    @pl.when(where[0] != 0)
    def _():
        write(own_a)

    @pl.when(where[0] == 0)
    def _():
        write(own_b)


def base_kernel(first, where, inner, sigma, own_a, own_b, source_a, source_b, states_a, states_b, *rest):
    base_a, base_b = rest[-2:]
    if first:
        occupation, offsets, weights, scales, base_a, base_b = rest
        write_scales(where[2], occupation, offsets, weights, scales)

    def local(slab, source, states):
        rows = states.shape[0]
        padded = jnp.concatenate([sigma[slab], jnp.zeros((6, rows), F32)], axis=0)
        columns = jnp.transpose(padded)
        real, imag = columns[:, 0:1], columns[:, 1:2]
        wide = states.astype(F32)
        half = wide.shape[1] // 2
        turned = jnp.concatenate([-wide[:, half:], wide[:, :half]], axis=1)
        drive = jnp.concatenate([source[0], source[1]], axis=1)
        return drive + (real * wide + imag * turned)

    def both(own, source_left, source_right, states_left, states_right, base_left, base_right):
        left, right = states_left[...], states_right[...]
        handed = adjoint(inner, left).astype(BF16).astype(F32)
        driven = (local(1, source_right, right) + handed).astype(BF16)
        base_right[...] = product(own, driven)
        base_left[...] = local(0, source_left, left) + product(inner, right)

    @pl.when(where[0] != 0)
    def _():
        both(own_a, source_b, source_a, states_b, states_a, base_b, base_a)

    @pl.when(where[0] == 0)
    def _():
        both(own_b, source_a, source_b, states_a, states_b, base_a, base_b)


def write_scales(energy, occupation, offsets, weights, scales):
    modes = occupation.shape[1]
    rows = []
    for at, target in ((0, energy), (1, 1 - energy)):
        total = jnp.float32(0)
        for shift in range(offsets.shape[1]):
            reached = energy + offsets[energy, shift] == target
            total = total + jnp.where(reached, weights[energy, shift], jnp.float32(0))
        weight = jnp.full((1, modes), total, F32) / modes
        filled = occupation[pl.ds(target, 1), :]
        for kind, share in ((0, filled), (1, 1.0 - filled)):
            row = weight * share
            rows.append(jnp.concatenate([row, row], axis=1))
    rows = jnp.concatenate(rows + [jnp.zeros((8 - len(rows), 2 * modes), F32)], axis=0)
    scales[...] = jnp.transpose(rows)


def step_kernel(side, last, where, own, chain, link, base, arrived, *rest):
    states = rest[-1] if last else rest[-2]
    odd, inner = where[0], where[1]
    slab = 1 - odd if side else odd

    def message():
        if side:
            return arrived[...]
        return jnp.where(inner != 0, arrived[...], jnp.zeros_like(arrived))

    @pl.when(slab == 1)
    def _():
        fresh = (base[...] + product(chain, message())).astype(BF16)
        states[...] = fresh
        if not last:
            rest[-1][...] = adjoint(link, fresh).astype(BF16)

    @pl.when(slab == 0)
    def _():
        driven = (base[...] + message().astype(F32)).astype(BF16)
        fresh = product(own, driven).astype(BF16)
        states[...] = fresh
        if not last:
            rest[-1][...] = fresh


def sigma_kernel(where, own, other, scales, *rest):
    lesser, greater, left, right, held, sems = rest[-6:]
    rows, width = own.shape
    half = rows // 2
    for at, states in ((0, own), (1, other)):
        columns = slice(at * width, (at + 1) * width)
        pair = states[...]
        left[:rows, columns] = pair
        left[rows:, columns] = times_i(pair, -1)
        wide = jnp.transpose(pair).astype(F32)
        for kind in range(2):
            scale = scales[:, 2 * at + kind : 2 * at + kind + 1]
            right[kind, columns, :] = (wide * scale).astype(BF16)
    copies = []
    for kind, out in ((0, lesser), (1, greater)):
        for part in range(2):
            columns = slice(part * half, (part + 1) * half)
            block = jnp.dot(left[...], right[kind, :, columns], preferred_element_type=F32)
            held[kind, part, 0] = block[:rows].astype(BF16)
            held[kind, part, 1] = block[rows:].astype(BF16)
            copies.append(
                load(held.at[kind, part], out.at[where[0], :, :, columns], sems.at[kind, part])
            )
    for copy in copies:
        copy.wait()


def whole(count):
    return [pl.BlockSpec(memory_space=pltpu.VMEM)] * count


SCALAR = pl.BlockSpec(memory_space=pltpu.SMEM)
FAR = pl.BlockSpec(memory_space=pltpu.HBM)
NEAR = pl.BlockSpec(memory_space=pltpu.VMEM)


def call(kernel, outs, specs, args, scratch=()):
    return pl.pallas_call(
        kernel,
        out_shape=outs,
        in_specs=specs,
        out_specs=[NEAR] * len(outs),
        scratch_shapes=list(scratch),
        compiler_params=pltpu.CompilerParams(vmem_limit_bytes=24 * 2**20),
        cost_estimate=pl.CostEstimate(flops=1000, bytes_accessed=1000, transcendentals=0),
    )(*args)


def self_blocks(where, own, other, scales, blocks, after, previous):
    rows, width = own.shape
    extra = [after] if previous is None else previous
    kept = [NEAR] if previous is None else [pl.BlockSpec(memory_space=pl.ANY)] * 2
    return pl.pallas_call(
        sigma_kernel,
        out_shape=[jax.ShapeDtypeStruct(blocks, BF16)] * 2,
        in_specs=[SCALAR, NEAR, NEAR, NEAR] + kept,
        out_specs=[pl.BlockSpec(memory_space=pl.ANY)] * 2,
        scratch_shapes=[
            pltpu.VMEM((2 * rows, 2 * width), BF16),
            pltpu.VMEM((2, 2 * width, rows), BF16),
            pltpu.VMEM((2, 2, 2, rows, rows // 2), BF16),
            pltpu.SemaphoreType.DMA((2, 2)),
        ],
        input_output_aliases={} if previous is None else {4: 0, 5: 1},
        compiler_params=pltpu.CompilerParams(vmem_limit_bytes=24 * 2**20),
        cost_estimate=pl.CostEstimate(flops=1000, bytes_accessed=1000, transcendentals=0),
    )(where, own, other, scales, *extra)


def body(energies, chips, precond, coupling, source, sigma_ret, occupation, shift_offsets, shift_weights):
    _, slabs, _, rows, modes = source.shape
    width = 2 * modes
    energy, chip = lax.axis_index("energy"), lax.axis_index("space")
    odd = lax.rem(chip, 2)
    inner = jnp.logical_and(chip > 0, chip < chips - 1).astype(jnp.int32)
    where = jnp.stack([odd, inner, energy]).astype(jnp.int32)

    def at(e, c):
        return e * chips + c

    pairing_a, pairing_b = [], []
    for e in range(energies):
        for c in range(chips):
            pairing_a.append((at(e, c), at(e, c ^ 1)))
            if 0 < c < chips - 1:
                pairing_b.append((at(e, c), at(e, ((c + 1) ^ 1) - 1)))
            else:
                pairing_b.append((at(e, c), at(e ^ 1, c)))
    swap = [(at(e, c), at(e ^ 1, c)) for e in range(energies) for c in range(chips)]

    precond, source, sigma = precond[0], source[0], sigma_ret[0]
    pair = jax.ShapeDtypeStruct((rows, width), BF16)
    total = jax.ShapeDtypeStruct((rows, width), F32)
    matrix = jax.ShapeDtypeStruct((2, rows, rows), BF16)
    drive = jax.ShapeDtypeStruct((2, rows, modes), F32)
    states, arrived = [None, None], [None, None]
    owns, drives = [None, None], [None, None]

    precond, coupling, source = [
        pltpu.with_memory_space_constraint(array, pltpu.HBM) for array in (precond, coupling, source)
    ]
    states[0], send, owns[0], link, drives[0] = call(
        lead_kernel,
        [pair, pair, matrix, matrix, drive],
        [SCALAR, FAR, FAR, FAR],
        (where, precond, coupling, source),
        [pltpu.SemaphoreType.DMA((5,))],
    )
    arrived[0] = lax.ppermute(send, AXES, pairing_b)
    states[1], send, owns[1], within, drives[1] = call(
        trail_kernel,
        [pair, pair, matrix, matrix, drive],
        [SCALAR, FAR, FAR, FAR, NEAR],
        (where, precond, coupling, source, link),
        [pltpu.SemaphoreType.DMA((4,))],
    )
    arrived[1] = lax.ppermute(send, AXES, pairing_a)
    for sweep in range(1, SWEEPS):
        first, last = sweep == 1, sweep == SWEEPS - 1
        bases = call(
            functools.partial(base_kernel, first),
            [jax.ShapeDtypeStruct((width, 8), F32)] * first + [total, total],
            [SCALAR] + [NEAR] * 8 + [NEAR, SCALAR, SCALAR] * first,
            (where, within, sigma, *owns, *drives, *states) + (occupation, shift_offsets, shift_weights) * first,
        )
        if first:
            scales, bases = bases[0], bases[1:]
            (chain,) = call(
                chain_kernel, [matrix], [SCALAR] + [NEAR] * 3, (where, *owns, link)
            )
        states = list(states)
        for side in range(2):
            results = call(
                functools.partial(step_kernel, side, last),
                [pair] if last else [pair, pair],
                [SCALAR] + [NEAR] * 5,
                (where, owns[side], chain, link, bases[side], arrived[side]),
            )
            states[side] = results[0]
            if not last:
                arrived[side] = lax.ppermute(results[1], AXES, (pairing_b, pairing_a)[side])
    others = [lax.ppermute(states[side], AXES, swap) for side in range(2)]
    blocks = None
    for side in range(2):
        slab = 1 - odd if side else odd
        blocks = self_blocks(
            slab[None].astype(jnp.int32),
            states[side],
            others[side],
            scales,
            (slabs, 2, rows, rows),
            states[1] if blocks is None else None,
            blocks,
        )
    return tuple(block[None] for block in blocks)


def solution(mesh):
    energies, chips = mesh.shape["energy"], mesh.shape["space"]
    placed = (
        P("energy", "space", None, None, None),
        P("space", None, None, None),
        P("energy", "space", None, None, None),
        P("energy", "space", None, None),
        P(),
        P(),
        P(),
    )
    return jax.shard_map(
        functools.partial(body, energies, chips),
        mesh=mesh,
        in_specs=placed,
        out_specs=(P("energy", "space", None, None, None), P("energy", "space", None, None, None)),
        check_vma=False,
    )
```

time: 62.1 us -> 56 us (0.902)
  the two profiles are of different devices: /device:TPU:29 before, /device:TPU:1 now
where the time goes in v2:
time: 56 us; the launch traced here: 55.8 us
  Pallas kernels  25.9 us (46%)
  starting transfers between devices  17.8 us (32%)
  waiting for transfers between devices  11.1 us (20%)
  between operations  0.96 us (2%)
    pallas_call x12, Pallas kernels, call(): pl.pallas_call(kernel, out_shape=outs, in_specs=specs, out_specs=[NEAR] *...  20.9 us
    ppermute x4, starting transfers between devices, body(): arrived[side] = lax.ppermute(results[1], AXES, (pairing_b, pairing_a)[side])  10.8 us
    ppermute x4, waiting for transfers between devices, body(): arrived[side] = lax.ppermute(results[1], AXES, (pairing_b, pairing_a)[side])  7.05 us
    pallas_call x2, Pallas kernels, self_blocks(): pl.pallas_call(sigma_kernel, out_shape=[jax.ShapeDtypeStruct(blocks, BF16...  4.98 us
    ppermute x2, starting transfers between devices, body(): others = [lax.ppermute(states[side], AXES, swap) for side in range(2)]  4.12 us
    ppermute x1, waiting for transfers between devices, body(): arrived[1] = lax.ppermute(send, AXES, pairing_a)  4 us
    ppermute x1, starting transfers between devices, body(): arrived[1] = lax.ppermute(send, AXES, pairing_a)  2.79 us
  transfers between devices with their start and end apart: 8, of which 3 were waited for; matrix products, arithmetic and copies ran while one was open for 0% of the time, Pallas kernels for 38%

profile of v2, /device:TPU:1, one launch (start us, length us, event | category | flops | bytes accessed | tf_op | source)
XLA Modules:
  0.0 55.8 jit_solution(5763845031265317957)
XLA Ops:
  0.6 0.1 pad_add_fusion.where
  0.7 2.4 %shard_map.86 = (bf16[512,256]{1,0:T(8,128)(2,1)S(1)}, bf16[512,256]{1,0:T(8,128)(2,1)S(1)}, bf16[2,512,512]{2,1,0:T(8,128)(2,1)S(1)}, bf16[2,512,512]{2,1,0:T(8,128)(2,1)S(1)}, f32[2,512,128]{2,1,0:T(8,128)S(1)}) custom-call(s32[3]{0:T(128)S(1)} %pad_add_fusion.where, bf16[2,2,512,512]{3,2,1,0:T(8,128)(2,1)} %bitcast.12, bf16[2,2,512,512]{3,2,1,0:T(8,128)(2,1)} %coupling.3, ...), custom_call_target="tpu_custom_call" | custom-call | flops 1000 | bytes 1000 | tf_op jit(solution)/shard_map/pallas_call | solution.py:230
  3.1 0.1 collective-permute-start
  3.3 2.9 %shard_map.87 = (bf16[512,256]{1,0:T(8,128)(2,1)S(1)}, bf16[512,256]{1,0:T(8,128)(2,1)S(1)}, bf16[2,512,512]{2,1,0:T(8,128)(2,1)S(1)}, bf16[2,512,512]{2,1,0:T(8,128)(2,1)S(1)}, f32[2,512,128]{2,1,0:T(8,128)S(1)}) custom-call(s32[3]{0:T(128)S(1)} %pad_add_fusion.where, bf16[2,2,512,512]{3,2,1,0:T(8,128)(2,1)} %bitcast.13, bf16[2,2,512,512]{3,2,1,0:T(8,128)(2,1)} %coupling.3, ...), custom_call_target="tpu_custom_call" | custom-call | flops 1000 | bytes 1000 | tf_op jit(solution)/shard_map/pallas_call | solution.py:230
  6.1 2.8 %collective-permute-start.1 = (bf16[512,256]{1,0:T(8,128)(2,1)S(1)}, bf16[512,256]{1,0:T(8,128)(2,1)S(1)}, u32[]{:S(2)}, u32[]{:S(2)}) collective-permute-start(bf16[512,256]{1,0:T(8,128)(2,1)S(1)} %get-tuple-element.43), channel_id=1, source_target_pairs={{0,1},{1,0},{2,3},{3,2},{4,5},{5,4},{6,7},{7,6},{8,9},{9,8},{10,11... | collective-permute-start | bytes 786440 | tf_op jit(solution)/shard_map/ppermute | solution.py:309
  8.9 0.0 copy-start
  8.9 0.0 copy-start.1
  8.9 0.0 copy-start.2
  8.9 0.0 copy-start.3
  8.9 1.8 %shard_map.88.chain = bf16[2,512,512]{2,1,0:T(8,128)(2,1)S(1)} custom-call(s32[3]{0:T(128)S(1)} %pad_add_fusion.where, bf16[2,512,512]{2,1,0:T(8,128)(2,1)S(1)} %get-tuple-element.33.own_a.own, bf16[2,512,512]{2,1,0:T(8,128)(2,1)S(1)} %get-tuple-element.32.own_b.own, bf16[2,512,512]{2,1,0:T(8,128)(2,1)S(1)} %get-tuple-element.31.link), custom_call_target="tpu_custom_call" | custom-call | flops 1000 | bytes 1000 | tf_op jit(solution)/shard_map/pallas_call | solution.py:230
  10.7 0.0 copy-done
  10.7 0.0 copy-done.1
  10.7 0.0 copy-done.2
  10.8 0.0 copy-done.3
  10.8 2.1 %shard_map.89 = (f32[256,8]{1,0:T(8,128)S(1)}, f32[512,256]{1,0:T(8,128)S(1)}, f32[512,256]{1,0:T(8,128)S(1)}) custom-call(s32[3]{0:T(128)S(1)} %pad_add_fusion.where, bf16[2,512,512]{2,1,0:T(8,128)(2,1)S(1)} %get-tuple-element.34.inner, f32[2,2,512]{2,1,0:T(2,128)S(1)} %bitcast.9, bf16[2,512,512]{2,1,0:T(8,128)(2,1)S(1)} %get-tuple-element.33.own_a.own, ...), custom_call_target="tpu_custom_call" | custom-call | flops 1000 | bytes 1000 | tf_op jit(solution)/shard_map/pallas_call | solution.py:230
  12.9 0.0 collective-permute-done.arrived
  12.9 1.0 %shard_map.90 = (bf16[512,256]{1,0:T(8,128)(2,1)S(1)}, bf16[512,256]{1,0:T(8,128)(2,1)S(1)}) custom-call(s32[3]{0:T(128)S(1)} %pad_add_fusion.where, bf16[2,512,512]{2,1,0:T(8,128)(2,1)S(1)} %get-tuple-element.33.own_a.own, bf16[2,512,512]{2,1,0:T(8,128)(2,1)S(1)} %shard_map.88.chain, bf16[2,512,512]{2,1,0:T(8,128)(2,1)S(1)} %get-tuple-element.31.link, ...), custom_call_target="tpu_custom_call" | custom-call | flops 1000 | bytes 1000 | tf_op jit(solution)/shard_map/pallas_call | solution.py:230
  13.9 1.3 %collective-permute-start.2 = (bf16[512,256]{1,0:T(8,128)(2,1)S(1)}, bf16[512,256]{1,0:T(8,128)(2,1)S(1)}, u32[]{:S(2)}, u32[]{:S(2)}) collective-permute-start(bf16[512,256]{1,0:T(8,128)(2,1)S(1)} %get-tuple-element.46), channel_id=1, source_target_pairs={{0,16},{1,2},{2,1},{3,4},{4,3},{5,6},{6,5},{7,8},{8,7},{9,10},{10,... | collective-permute-start | bytes 786440 | tf_op jit(solution)/shard_map/ppermute | solution.py:333
  15.2 4.0 %collective-permute-done.1.arrived = bf16[512,256]{1,0:T(8,128)(2,1)S(1)} collective-permute-done((bf16[512,256]{1,0:T(8,128)(2,1)S(1)}, bf16[512,256]{1,0:T(8,128)(2,1)S(1)}, u32[]{:S(2)}, u32[]{:S(2)}) %collective-permute-start.1) | collective-permute-done | bytes 262176 | tf_op jit(solution)/shard_map/ppermute | solution.py:309
  19.2 1.8 %shard_map.91 = (bf16[512,256]{1,0:T(8,128)(2,1)S(1)}, bf16[512,256]{1,0:T(8,128)(2,1)S(1)}) custom-call(s32[3]{0:T(128)S(1)} %pad_add_fusion.where, bf16[2,512,512]{2,1,0:T(8,128)(2,1)S(1)} %get-tuple-element.32.own_b.own, bf16[2,512,512]{2,1,0:T(8,128)(2,1)S(1)} %shard_map.88.chain, bf16[2,512,512]{2,1,0:T(8,128)(2,1)S(1)} %get-tuple-element.31.link, ...), custom_call_target="tpu_custom_call" | custom-call | flops 1000 | bytes 1000 | tf_op jit(solution)/shard_map/pallas_call | solution.py:230
  21.0 7.0 %collective-permute-start.3 = (bf16[512,256]{1,0:T(8,128)(2,1)S(1)}, bf16[512,256]{1,0:T(8,128)(2,1)S(1)}, u32[]{:S(2)}, u32[]{:S(2)}) collective-permute-start(bf16[512,256]{1,0:T(8,128)(2,1)S(1)} %get-tuple-element.49), channel_id=1, source_target_pairs={{0,1},{1,0},{2,3},{3,2},{4,5},{5,4},{6,7},{7,6},{8,9},{9,8},{10,11... | collective-permute-start | bytes 786440 | tf_op jit(solution)/shard_map/ppermute | solution.py:333
  28.1 2.0 %shard_map.92 = (f32[512,256]{1,0:T(8,128)S(1)}, f32[512,256]{1,0:T(8,128)S(1)}) custom-call(s32[3]{0:T(128)S(1)} %pad_add_fusion.where, bf16[2,512,512]{2,1,0:T(8,128)(2,1)S(1)} %get-tuple-element.34.inner, f32[2,2,512]{2,1,0:T(2,128)S(1)} %bitcast.10, bf16[2,512,512]{2,1,0:T(8,128)(2,1)S(1)} %get-tuple-element.33.own_a.own, ...), custom_call_target="tpu_custom_call" | custom-call | flops 1000 | bytes 1000 | tf_op jit(solution)/shard_map/pallas_call | solution.py:230
  30.0 0.0 collective-permute-done.2.arrived
  30.0 1.0 %shard_map.93 = (bf16[512,256]{1,0:T(8,128)(2,1)S(1)}, bf16[512,256]{1,0:T(8,128)(2,1)S(1)}) custom-call(s32[3]{0:T(128)S(1)} %pad_add_fusion.where, bf16[2,512,512]{2,1,0:T(8,128)(2,1)S(1)} %get-tuple-element.33.own_a.own, bf16[2,512,512]{2,1,0:T(8,128)(2,1)S(1)} %shard_map.88.chain, bf16[2,512,512]{2,1,0:T(8,128)(2,1)S(1)} %get-tuple-element.31.link, ...), custom_call_target="tpu_custom_call" | custom-call | flops 1000 | bytes 1000 | tf_op jit(solution)/shard_map/pallas_call | solution.py:230
  31.1 0.9 %collective-permute-start.6 = (bf16[512,256]{1,0:T(8,128)(2,1)S(1)}, bf16[512,256]{1,0:T(8,128)(2,1)S(1)}, u32[]{:S(2)}, u32[]{:S(2)}) collective-permute-start(bf16[512,256]{1,0:T(8,128)(2,1)S(1)} %get-tuple-element.55), channel_id=1, source_target_pairs={{0,16},{1,2},{2,1},{3,4},{4,3},{5,6},{6,5},{7,8},{8,7},{9,10},{10,... | collective-permute-start | bytes 786440 | tf_op jit(solution)/shard_map/ppermute | solution.py:333
  31.9 6.8 %collective-permute-done.3.arrived = bf16[512,256]{1,0:T(8,128)(2,1)S(1)} collective-permute-done((bf16[512,256]{1,0:T(8,128)(2,1)S(1)}, bf16[512,256]{1,0:T(8,128)(2,1)S(1)}, u32[]{:S(2)}, u32[]{:S(2)}) %collective-permute-start.3) | collective-permute-done | bytes 262176 | tf_op jit(solution)/shard_map/ppermute | solution.py:333
  38.7 2.0 %shard_map.94 = (bf16[512,256]{1,0:T(8,128)(2,1)S(1)}, bf16[512,256]{1,0:T(8,128)(2,1)S(1)}) custom-call(s32[3]{0:T(128)S(1)} %pad_add_fusion.where, bf16[2,512,512]{2,1,0:T(8,128)(2,1)S(1)} %get-tuple-element.32.own_b.own, bf16[2,512,512]{2,1,0:T(8,128)(2,1)S(1)} %shard_map.88.chain, bf16[2,512,512]{2,1,0:T(8,128)(2,1)S(1)} %get-tuple-element.31.link, ...), custom_call_target="tpu_custom_call" | custom-call | flops 1000 | bytes 1000 | tf_op jit(solution)/shard_map/pallas_call | solution.py:230
  40.8 1.6 %collective-permute-start.4 = (bf16[512,256]{1,0:T(8,128)(2,1)S(1)}, bf16[512,256]{1,0:T(8,128)(2,1)S(1)}, u32[]{:S(2)}, u32[]{:S(2)}) collective-permute-start(bf16[512,256]{1,0:T(8,128)(2,1)S(1)} %get-tuple-element.52), channel_id=1, source_target_pairs={{0,1},{1,0},{2,3},{3,2},{4,5},{5,4},{6,7},{7,6},{8,9},{9,8},{10,11... | collective-permute-start | bytes 786440 | tf_op jit(solution)/shard_map/ppermute | solution.py:333
  42.3 2.0 %shard_map.95 = (f32[512,256]{1,0:T(8,128)S(1)}, f32[512,256]{1,0:T(8,128)S(1)}) custom-call(s32[3]{0:T(128)S(1)} %pad_add_fusion.where, bf16[2,512,512]{2,1,0:T(8,128)(2,1)S(1)} %get-tuple-element.34.inner, f32[2,2,512]{2,1,0:T(2,128)S(1)} %bitcast.11, bf16[2,512,512]{2,1,0:T(8,128)(2,1)S(1)} %get-tuple-element.33.own_a.own, ...), custom_call_target="tpu_custom_call" | custom-call | flops 1000 | bytes 1000 | tf_op jit(solution)/shard_map/pallas_call | solution.py:230
  44.3 0.0 collective-permute-done.6.arrived
  44.3 1.0 %shard_map.97.own = bf16[512,256]{1,0:T(8,128)(2,1)S(1)} custom-call(s32[3]{0:T(128)S(1)} %pad_add_fusion.where, bf16[2,512,512]{2,1,0:T(8,128)(2,1)S(1)} %get-tuple-element.33.own_a.own, bf16[2,512,512]{2,1,0:T(8,128)(2,1)S(1)} %shard_map.88.chain, bf16[2,512,512]{2,1,0:T(8,128)(2,1)S(1)} %get-tuple-element.31.link, f32[512,256]{1,0:T(8,128)S(1)} %get-tuple-element.54.base, ...), custom_call_target="tpu_custom_call" | custom-call | flops 1000 | bytes 1000 | tf_op jit(solution)/shard_map/pallas_call | solution.py:230
  45.3 1.7 %collective-permute-start.7 = (bf16[512,256]{1,0:T(8,128)(2,1)S(1)}, bf16[512,256]{1,0:T(8,128)(2,1)S(1)}, u32[]{:S(2)}, u32[]{:S(2)}) collective-permute-start(bf16[512,256]{1,0:T(8,128)(2,1)S(1)} %shard_map.97.own), channel_id=1, source_target_pairs={{0,16},{1,17},{2,18},{3,19},{4,20},{5,21},{6,22},{7,23},{8,24},{9,... | collective-permute-start | bytes 786440 | tf_op jit(solution)/shard_map/ppermute | solution.py:334
  47.0 0.2 collective-permute-done.4.arrived
  47.2 1.0 %shard_map.96.rest_0_.own = bf16[512,256]{1,0:T(8,128)(2,1)S(1)} custom-call(s32[3]{0:T(128)S(1)} %pad_add_fusion.where, bf16[2,512,512]{2,1,0:T(8,128)(2,1)S(1)} %get-tuple-element.32.own_b.own, bf16[2,512,512]{2,1,0:T(8,128)(2,1)S(1)} %shard_map.88.chain, bf16[2,512,512]{2,1,0:T(8,128)(2,1)S(1)} %get-tuple-element.31.link, ...), custom_call_target="tpu_custom_call" | custom-call | flops 1000 | bytes 1000 | tf_op jit(solution)/shard_map/pallas_call | solution.py:230
  48.2 2.4 %collective-permute-start.5 = (bf16[512,256]{1,0:T(8,128)(2,1)S(1)}, bf16[512,256]{1,0:T(8,128)(2,1)S(1)}, u32[]{:S(2)}, u32[]{:S(2)}) collective-permute-start(bf16[512,256]{1,0:T(8,128)(2,1)S(1)} %shard_map.96.rest_0_.own), channel_id=1, source_target_pairs={{0,16},{1,17},{2,18},{3,19},{4,20},{5,21},{6,22},{7,23},{8,24},{9,... | collective-permute-start | bytes 786440 | tf_op jit(solution)/shard_map/ppermute | solution.py:334
  50.7 0.0 collective-permute-done.7.other
  50.7 2.5 %shard_map.98 = (bf16[2,2,512,512]{3,2,1,0:T(8,128)(2,1)}, bf16[2,2,512,512]{3,2,1,0:T(8,128)(2,1)}) custom-call(s32[1]{0:T(128)} %bitcast.1.where, bf16[512,256]{1,0:T(8,128)(2,1)S(1)} %shard_map.97.own, bf16[512,256]{1,0:T(8,128)(2,1)S(1)} %collective-permute-done.7.other, f32[256,8]{1,0:T(8,128)S(1)} %get-tuple-element.53.scales, ...), custom_call_target="tpu_custom_call" | custom-call | flops 1000 | bytes 1000 | tf_op jit(solution)/shard_map/pallas_call | solution.py:245
  53.2 0.0 collective-permute-done.5.other
  53.2 2.5 %shard_map.99 = (bf16[2,2,512,512]{3,2,1,0:T(8,128)(2,1)}, bf16[2,2,512,512]{3,2,1,0:T(8,128)(2,1)}) custom-call(s32[1]{0:T(128)} %bitcast.where, bf16[512,256]{1,0:T(8,128)(2,1)S(1)} %shard_map.96.rest_0_.own, bf16[512,256]{1,0:T(8,128)(2,1)S(1)} %collective-permute-done.5.other, ...), custom_call_target="tpu_custom_call", output_to_operand_aliasing={{0}: (4, {}), {1}: (5, {})} | custom-call | flops 1000 | bytes 1000 | tf_op jit(solution)/shard_map/pallas_call | solution.py:245
Async XLA Ops:
  3.1 9.7 %collective-permute-start = (bf16[512,256]{1,0:T(8,128)(2,1)S(1)}, bf16[512,256]{1,0:T(8,128)(2,1)S(1)}, u32[]{:S(2)}, u32[]{:S(2)}) collective-permute-start(bf16[512,256]{1,0:T(8,128)(2,1)S(1)} %get-tuple-element.40), channel_id=1, source_target_pairs={{0,16},{1,2},{2,1},{3,4},{4,3},{5,6},{6,5},{7,8},{8,7},{9,10},{10,... | collective-permute-start | bytes 786440 | tf_op jit(solution)/shard_map/ppermute | solution.py:301
  6.1 13.1 %collective-permute-start.1 = (bf16[512,256]{1,0:T(8,128)(2,1)S(1)}, bf16[512,256]{1,0:T(8,128)(2,1)S(1)}, u32[]{:S(2)}, u32[]{:S(2)}) collective-permute-start(bf16[512,256]{1,0:T(8,128)(2,1)S(1)} %get-tuple-element.43), channel_id=1, source_target_pairs={{0,1},{1,0},{2,3},{3,2},{4,5},{5,4},{6,7},{7,6},{8,9},{9,8},{10,11... | collective-permute-start | bytes 786440 | tf_op jit(solution)/shard_map/ppermute | solution.py:309
  8.9 1.8 %copy-start = (f32[1,2,2,512]{3,2,1,0:T(2,128)S(1)}, f32[1,2,2,512]{3,2,1,0:T(2,128)}, u32[]{:S(2)}) copy-start(f32[1,2,2,512]{3,2,1,0:T(2,128)} %param.10) | copy-start | bytes 24580
  8.9 1.8 %copy-start.1 = (f32[2,128]{1,0:T(2,128)S(1)}, f32[2,128]{1,0:T(2,128)}, u32[]{:S(2)}) copy-start(f32[2,128]{1,0:T(2,128)} %rest_0_.1) | copy-start | bytes 3076
  8.9 1.8 %copy-start.2 = (s32[2,4]{1,0:T(2,128)S(1)}, s32[2,4]{1,0:T(2,128)}, u32[]{:S(2)}) copy-start(s32[2,4]{1,0:T(2,128)} %rest_1_.1) | copy-start | bytes 100
  8.9 1.8 %copy-start.3 = (f32[2,4]{1,0:T(2,128)S(1)}, f32[2,4]{1,0:T(2,128)}, u32[]{:S(2)}) copy-start(f32[2,4]{1,0:T(2,128)} %rest_2_.1) | copy-start | bytes 100
  13.9 16.2 %collective-permute-start.2 = (bf16[512,256]{1,0:T(8,128)(2,1)S(1)}, bf16[512,256]{1,0:T(8,128)(2,1)S(1)}, u32[]{:S(2)}, u32[]{:S(2)}) collective-permute-start(bf16[512,256]{1,0:T(8,128)(2,1)S(1)} %get-tuple-element.46), channel_id=1, source_target_pairs={{0,16},{1,2},{2,1},{3,4},{4,3},{5,6},{6,5},{7,8},{8,7},{9,10},{10,... | collective-permute-start | bytes 786440 | tf_op jit(solution)/shard_map/ppermute | solution.py:333
  21.0 17.7 %collective-permute-start.3 = (bf16[512,256]{1,0:T(8,128)(2,1)S(1)}, bf16[512,256]{1,0:T(8,128)(2,1)S(1)}, u32[]{:S(2)}, u32[]{:S(2)}) collective-permute-start(bf16[512,256]{1,0:T(8,128)(2,1)S(1)} %get-tuple-element.49), channel_id=1, source_target_pairs={{0,1},{1,0},{2,3},{3,2},{4,5},{5,4},{6,7},{7,6},{8,9},{9,8},{10,11... | collective-permute-start | bytes 786440 | tf_op jit(solution)/shard_map/ppermute | solution.py:333
  31.1 13.2 %collective-permute-start.6 = (bf16[512,256]{1,0:T(8,128)(2,1)S(1)}, bf16[512,256]{1,0:T(8,128)(2,1)S(1)}, u32[]{:S(2)}, u32[]{:S(2)}) collective-permute-start(bf16[512,256]{1,0:T(8,128)(2,1)S(1)} %get-tuple-element.55), channel_id=1, source_target_pairs={{0,16},{1,2},{2,1},{3,4},{4,3},{5,6},{6,5},{7,8},{8,7},{9,10},{10,... | collective-permute-start | bytes 786440 | tf_op jit(solution)/shard_map/ppermute | solution.py:333
  40.8 6.5 %collective-permute-start.4 = (bf16[512,256]{1,0:T(8,128)(2,1)S(1)}, bf16[512,256]{1,0:T(8,128)(2,1)S(1)}, u32[]{:S(2)}, u32[]{:S(2)}) collective-permute-start(bf16[512,256]{1,0:T(8,128)(2,1)S(1)} %get-tuple-element.52), channel_id=1, source_target_pairs={{0,1},{1,0},{2,3},{3,2},{4,5},{5,4},{6,7},{7,6},{8,9},{9,8},{10,11... | collective-permute-start | bytes 786440 | tf_op jit(solution)/shard_map/ppermute | solution.py:333
  45.3 5.3 %collective-permute-start.7 = (bf16[512,256]{1,0:T(8,128)(2,1)S(1)}, bf16[512,256]{1,0:T(8,128)(2,1)S(1)}, u32[]{:S(2)}, u32[]{:S(2)}) collective-permute-start(bf16[512,256]{1,0:T(8,128)(2,1)S(1)} %shard_map.97.own), channel_id=1, source_target_pairs={{0,16},{1,17},{2,18},{3,19},{4,20},{5,21},{6,22},{7,23},{8,24},{9,... | collective-permute-start | bytes 786440 | tf_op jit(solution)/shard_map/ppermute | solution.py:334
  48.2 4.9 %collective-permute-start.5 = (bf16[512,256]{1,0:T(8,128)(2,1)S(1)}, bf16[512,256]{1,0:T(8,128)(2,1)S(1)}, u32[]{:S(2)}, u32[]{:S(2)}) collective-permute-start(bf16[512,256]{1,0:T(8,128)(2,1)S(1)} %shard_map.96.rest_0_.own), channel_id=1, source_target_pairs={{0,16},{1,17},{2,18},{3,19},{4,20},{5,21},{6,22},{7,23},{8,24},{9,... | collective-permute-start | bytes 786440 | tf_op jit(solution)/shard_map/ppermute | solution.py:334

commit v3 on v2

v3 whole, which is shorter than its diff:
```python
import functools

import jax
import jax.numpy as jnp
from jax import lax
from jax.experimental import pallas as pl
from jax.experimental.pallas import tpu as pltpu
from jax.sharding import PartitionSpec as P

SWEEPS = 4
F32 = jnp.float32
BF16 = jnp.bfloat16
AXES = ("energy", "space")
LEAD_A = True
LEAD_PIECES = 2
HOLD = True


def times_i(pair, sign):
    half = pair.shape[1] // 2
    real, imag = pair[:, :half], pair[:, half:]
    if sign > 0:
        return jnp.concatenate([-imag, real], axis=1)
    return jnp.concatenate([imag, -real], axis=1)


def product(matrix, pair):
    out = jnp.dot(matrix[0], pair, preferred_element_type=F32)
    return out + jnp.dot(matrix[1], times_i(pair, 1), preferred_element_type=F32)


def transposed_dot(matrix, pair):
    return lax.dot_general(matrix, pair, (((0,), (0,)), ((), ())), preferred_element_type=F32)


def adjoint(matrix, pair):
    out = transposed_dot(matrix[0], pair)
    return out + transposed_dot(matrix[1], times_i(pair, -1))


def joined(ref, slab):
    return jnp.concatenate([ref[slab, 0], ref[slab, 1]], axis=1)


def load(source, held, sem):
    copy = pltpu.make_async_copy(source, held, sem)
    copy.start()
    return copy


def lead_kernel(where, precond, coupling, source, states, send, own, link, drive, sems):
    slab = where[0]
    copies = [
        load(source.at[slab], drive, sems.at[0]),
        load(precond.at[slab, 0], own.at[0], sems.at[1]),
        load(precond.at[slab, 1], own.at[1], sems.at[2]),
        load(coupling.at[1, 0], link.at[0], sems.at[3]),
        load(coupling.at[1, 1], link.at[1], sems.at[4]),
    ]
    copies[0].wait()
    pair = jnp.concatenate([drive[0], drive[1]], axis=1).astype(BF16)
    copies[1].wait()
    partial = jnp.dot(own[0], pair, preferred_element_type=F32)
    copies[2].wait()
    partial = partial + jnp.dot(own[1], times_i(pair, 1), preferred_element_type=F32)
    fresh = partial.astype(BF16)
    states[...] = fresh
    copies[3].wait()
    copies[4].wait()
    send_fresh(slab, link, fresh, send)


def trail_kernel(
    where, precond, coupling, source, link, lead, lead_states,
    states, send, own, inner, drive, chain, term, sems,
):
    slab = 1 - where[0]
    copies = [
        load(source.at[slab], drive, sems.at[0]),
        load(precond.at[slab, 0], own.at[0], sems.at[1]),
        load(precond.at[slab, 1], own.at[1], sems.at[2]),
        load(coupling.at[0], inner, sems.at[3]),
    ]
    copies[0].wait()
    pair = jnp.concatenate([drive[0], drive[1]], axis=1).astype(BF16)
    copies[1].wait()
    partial = jnp.dot(own[0], pair, preferred_element_type=F32)
    copies[2].wait()
    partial = partial + jnp.dot(own[1], times_i(pair, 1), preferred_element_type=F32)
    fresh = partial.astype(BF16)
    states[...] = fresh
    send_fresh(slab, link, fresh, send)

    def write_chain(matrix):
        both = product(matrix, jnp.concatenate([link[0], link[1]], axis=1))
        half = both.shape[1] // 2
        chain[0] = both[:, :half].astype(BF16)
        chain[1] = both[:, half:].astype(BF16)

    @pl.when(slab == 1)
    def _():
        write_chain(own)

    @pl.when(slab == 0)
    def _():
        write_chain(lead)

    copies[3].wait()
    write_term(slab, inner, lead_states, term)


def send_fresh(slab, link, fresh, send):
    @pl.when(slab == 1)
    def _():
        send[...] = adjoint(link, fresh).astype(BF16)

    @pl.when(slab == 0)
    def _():
        send[...] = fresh


def write_term(slab, inner, states, term):
    @pl.when(slab == 0)
    def _():
        term[...] = product(inner, states[...])

    @pl.when(slab == 1)
    def _():
        term[...] = adjoint(inner, states[...]).astype(BF16).astype(F32)


def term_kernel(where, inner, states, term):
    write_term(1 - where[0], inner, states, term)


def base_kernel(kind, where, inner, sigma, own_a, own_b, source_a, source_b, states_a, states_b, term, *rest):
    if kind == "first":
        occupation, offsets, weights, base_a, base_b, scales = rest
        write_scales(where[3], occupation, offsets, weights, scales)
    elif kind == "holding":
        waiting, base_a, base_b, send = rest
        send[...] = waiting[...]
    else:
        base_a, base_b = rest

    def local(slab, source, states):
        rows = states.shape[0]
        padded = jnp.concatenate([sigma[slab], jnp.zeros((6, rows), F32)], axis=0)
        columns = jnp.transpose(padded)
        real, imag = columns[:, 0:1], columns[:, 1:2]
        wide = states[...].astype(F32)
        half = wide.shape[1] // 2
        turned = jnp.concatenate([-wide[:, half:], wide[:, :half]], axis=1)
        drive = jnp.concatenate([source[0], source[1]], axis=1)
        return drive + (real * wide + imag * turned)

    @pl.when(where[0] == 1)
    def _():
        handed = adjoint(inner, states_b[...]).astype(BF16).astype(F32)
        base_a[...] = product(own_a, (local(1, source_a, states_a) + handed).astype(BF16))
        base_b[...] = local(0, source_b, states_b) + term[...]

    @pl.when(where[0] == 0)
    def _():
        base_a[...] = local(0, source_a, states_a) + product(inner, states_b[...])
        driven = (local(1, source_b, states_b) + term[...]).astype(BF16)
        base_b[...] = product(own_b, driven)


def write_scales(energy, occupation, offsets, weights, scales):
    modes = occupation.shape[1]
    rows = []
    for at, target in ((0, energy), (1, 1 - energy)):
        total = jnp.float32(0)
        for shift in range(offsets.shape[1]):
            reached = energy + offsets[energy, shift] == target
            total = total + jnp.where(reached, weights[energy, shift], jnp.float32(0))
        weight = jnp.full((1, modes), total, F32) / modes
        filled = occupation[pl.ds(target, 1), :]
        for kind, share in ((0, filled), (1, 1.0 - filled)):
            row = weight * share
            rows.append(jnp.concatenate([row, row], axis=1))
    rows = jnp.concatenate(rows + [jnp.zeros((8 - len(rows), 2 * modes), F32)], axis=0)
    scales[...] = jnp.transpose(rows)


def step_kernel(side, last, outs, where, own, chain, link, base, arrived, *rest):
    results = rest[len(rest) - outs :]
    slab = 1 - where[0] if side else where[0]

    def message():
        return jnp.where(where[1 + side] != 0, arrived[...], jnp.zeros_like(arrived))

    def keep(fresh):
        if not last:
            results[0][...] = fresh
            return
        rows = fresh.shape[0] // outs
        for at, piece in enumerate(results):
            piece[...] = fresh[at * rows : (at + 1) * rows]

    @pl.when(slab == 1)
    def _():
        fresh = (base[...] + product(chain, message())).astype(BF16)
        keep(fresh)
        if not last:
            results[1][...] = adjoint(link, fresh).astype(BF16)

    @pl.when(slab == 0)
    def _():
        driven = (base[...] + message().astype(F32)).astype(BF16)
        fresh = product(own, driven).astype(BF16)
        keep(fresh)
        if not last:
            results[1][...] = fresh


def weighted_squares(parts, scales, at):
    pair = jnp.concatenate([part[...] for part in parts], axis=0)
    half = pair.shape[0] // 2
    turned = times_i(pair, -1)
    upper = jnp.concatenate([pair[:half], turned[:half]], axis=0)
    lower = jnp.concatenate([pair[half:], turned[half:]], axis=0)
    wide = jnp.transpose(pair).astype(F32)
    for kind in range(2):
        weighted = (wide * scales[:, 2 * at + kind : 2 * at + kind + 1]).astype(BF16)
        yield (
            kind,
            jnp.dot(upper, weighted, preferred_element_type=F32),
            jnp.dot(lower, weighted[:, half:], preferred_element_type=F32),
        )


def own_sigma_kernel(pieces, scales, *rest):
    tops, lows = rest[pieces:]
    for kind, top, low in weighted_squares(rest[:pieces], scales, 0):
        tops[kind] = top
        lows[kind] = low


def sigma_kernel(pieces, where, scales, tops, lows, *rest):
    lesser, greater, token, held, sems = rest[-5:]
    token[...] = jnp.zeros_like(token)
    copies = []
    for kind, top, low in weighted_squares(rest[:pieces], scales, 1):
        out = greater if kind else lesser
        top = (top + tops[kind]).astype(BF16)
        low = (low + lows[kind]).astype(BF16)
        half = low.shape[1]
        held[kind, 0, :half] = top[:half]
        held[kind, 1, :half] = top[half:]
        rows = slice(0, half)
        copies.append(load(held.at[kind, :, rows], out.at[where[0], :, rows], sems.at[kind, 0]))
        held[kind, 0, half:, half:] = low[:half]
        held[kind, 1, half:, half:] = low[half:]
        held[kind, 0, half:, :half] = jnp.transpose(top[:half, half:])
        held[kind, 1, half:, :half] = -jnp.transpose(top[half:, half:])
        rows = slice(half, 2 * half)
        copies.append(load(held.at[kind, :, rows], out.at[where[0], :, rows], sems.at[kind, 1]))
    for copy in copies:
        copy.wait()


def whole(count):
    return [pl.BlockSpec(memory_space=pltpu.VMEM)] * count


SCALAR = pl.BlockSpec(memory_space=pltpu.SMEM)
FAR = pl.BlockSpec(memory_space=pltpu.HBM)
NEAR = pl.BlockSpec(memory_space=pltpu.VMEM)


def call(kernel, outs, specs, args, scratch=()):
    return pl.pallas_call(
        kernel,
        out_shape=outs,
        in_specs=specs,
        out_specs=[NEAR] * len(outs),
        scratch_shapes=list(scratch),
        compiler_params=pltpu.CompilerParams(vmem_limit_bytes=24 * 2**20),
        cost_estimate=pl.CostEstimate(flops=1000, bytes_accessed=1000, transcendentals=0),
    )(*args)


def self_blocks(where, scales, own, other, blocks, previous):
    rows = sum(part.shape[0] for part in own)
    pieces = len(own)
    sums = call(
        functools.partial(own_sigma_kernel, pieces),
        [
            jax.ShapeDtypeStruct((2, rows, rows), F32),
            jax.ShapeDtypeStruct((2, rows, rows // 2), F32),
        ],
        [NEAR] * (1 + pieces),
        (scales, *own),
    )
    return pl.pallas_call(
        functools.partial(sigma_kernel, pieces),
        out_shape=[jax.ShapeDtypeStruct(blocks, BF16)] * 2 + [jax.ShapeDtypeStruct((8, 128), F32)],
        in_specs=[SCALAR] + [NEAR] * (3 + pieces) + [pl.BlockSpec(memory_space=pl.ANY)] * len(previous),
        out_specs=[pl.BlockSpec(memory_space=pl.ANY)] * 2 + [NEAR],
        scratch_shapes=[
            pltpu.VMEM((2, 2, rows, rows), BF16),
            pltpu.SemaphoreType.DMA((2, 2)),
        ],
        input_output_aliases={4 + pieces + at: at for at in range(len(previous))},
        compiler_params=pltpu.CompilerParams(vmem_limit_bytes=24 * 2**20),
        cost_estimate=pl.CostEstimate(flops=1000, bytes_accessed=1000, transcendentals=0),
    )(where, scales, *sums, *other, *previous)


def body(energies, chips, precond, coupling, source, sigma_ret, occupation, shift_offsets, shift_weights):
    _, slabs, _, rows, modes = source.shape
    width = 2 * modes
    energy, chip = lax.axis_index("energy"), lax.axis_index("space")
    odd = lax.rem(chip, 2)
    inner = jnp.logical_and(chip > 0, chip < chips - 1).astype(jnp.int32)
    if LEAD_A:
        lead, valid = 1 - odd, [jnp.ones_like(inner), inner]
    else:
        lead, valid = odd, [inner, jnp.ones_like(inner)]
    where = jnp.stack([lead, *valid, energy]).astype(jnp.int32)

    def at(e, c):
        return e * chips + c

    pairing_a, pairing_b = [], []
    for e in range(energies):
        for c in range(chips):
            pairing_a.append((at(e, c), at(e, c ^ 1)))
            if 0 < c < chips - 1:
                pairing_b.append((at(e, c), at(e, ((c + 1) ^ 1) - 1)))
            else:
                pairing_b.append((at(e, c), at(e ^ 1, c)))
    pairings = (pairing_a, pairing_b) if LEAD_A else (pairing_b, pairing_a)
    swap = [(at(e, c), at(e ^ 1, c)) for e in range(energies) for c in range(chips)]

    precond, source, sigma = precond[0], source[0], sigma_ret[0]
    pair = jax.ShapeDtypeStruct((rows, width), BF16)
    total = jax.ShapeDtypeStruct((rows, width), F32)
    matrix = jax.ShapeDtypeStruct((2, rows, rows), BF16)
    drive = jax.ShapeDtypeStruct((2, rows, modes), F32)
    states, arrived = [None, None], [None, None]
    owns, drives = [None, None], [None, None]

    precond, coupling, source = [
        pltpu.with_memory_space_constraint(array, pltpu.HBM) for array in (precond, coupling, source)
    ]
    states[0], send, owns[0], link, drives[0] = call(
        lead_kernel,
        [pair, pair, matrix, matrix, drive],
        [SCALAR, FAR, FAR, FAR],
        (where, precond, coupling, source),
        [pltpu.SemaphoreType.DMA((5,))],
    )
    arrived[0] = lax.ppermute(send, AXES, pairings[0])
    states[1], send, owns[1], within, drives[1], chain, term = call(
        trail_kernel,
        [pair, pair, matrix, matrix, drive, matrix, total],
        [SCALAR, FAR, FAR, FAR] + [NEAR] * 3,
        (where, precond, coupling, source, link, owns[0], states[0]),
        [pltpu.SemaphoreType.DMA((4,))],
    )
    arrived[1] = lax.ppermute(send, AXES, pairings[1])
    for sweep in range(1, SWEEPS):
        first, last = sweep == 1, sweep == SWEEPS - 1
        kind = "first" if first else "holding" if HOLD else "plain"
        extra_out = {"first": [jax.ShapeDtypeStruct((width, 8), F32)], "holding": [pair], "plain": []}
        extra_in = {"first": (occupation, shift_offsets, shift_weights), "holding": (send,) if not first else (), "plain": ()}
        if kind == "plain":
            arrived[1] = lax.ppermute(send, AXES, pairings[1])
        bases = call(
            functools.partial(base_kernel, kind),
            [total, total] + extra_out[kind],
            [SCALAR] + [NEAR] * 9 + [NEAR, SCALAR, SCALAR][: len(extra_in[kind])],
            (where, within, sigma, *owns, *drives, *states, term) + extra_in[kind],
        )
        if first:
            scales = bases[2]
        elif kind == "holding":
            arrived[1] = lax.ppermute(bases[2], AXES, pairings[1])
        states, blocks, token = list(states), [], []
        for side in range(2):
            if last:
                pieces = 1 if side else LEAD_PIECES
                outs = [jax.ShapeDtypeStruct((rows // pieces, width), BF16)] * pieces
            else:
                outs = [pair, pair]
            extra = token if last else [term] * side
            results = call(
                functools.partial(step_kernel, side, last, len(outs)),
                outs,
                [SCALAR] + [NEAR] * (5 + len(extra)),
                (where, owns[side], chain, link, bases[side], arrived[side], *extra),
            )
            if last:
                others = [lax.ppermute(result, AXES, swap) for result in results]
                slab = (1 - lead if side else lead)[None].astype(jnp.int32)
                *blocks, after = self_blocks(
                    slab, scales, results, others, (slabs, 2, rows, rows), blocks
                )
                token = [after]
                continue
            states[side], send = results
            if not side:
                arrived[0] = lax.ppermute(send, AXES, pairings[0])
                (term,) = call(
                    term_kernel, [total], [SCALAR, NEAR, NEAR], (where, within, states[0])
                )
    return tuple(block[None] for block in blocks)


def solution(mesh):
    energies, chips = mesh.shape["energy"], mesh.shape["space"]
    placed = (
        P("energy", "space", None, None, None),
        P("space", None, None, None),
        P("energy", "space", None, None, None),
        P("energy", "space", None, None),
        P(),
        P(),
        P(),
    )
    return jax.shard_map(
        functools.partial(body, energies, chips),
        mesh=mesh,
        in_specs=placed,
        out_specs=(P("energy", "space", None, None, None), P("energy", "space", None, None, None)),
        check_vma=False,
    )
```

time: 56 us -> 49.3 us (0.88)
  the two profiles are of different devices: /device:TPU:1 before, /device:TPU:27 now
where the time goes in v3:
time: 49.3 us; the launch traced here: 49.1 us
  Pallas kernels  28.1 us (57%)
  starting transfers between devices  17.4 us (35%)
  waiting for transfers between devices  2.62 us (5%)
  between operations  0.94 us (2%)
    pallas_call x15, Pallas kernels, call(): pl.pallas_call(kernel, out_shape=outs, in_specs=specs, out_specs=[NEAR] *...  23.9 us
    ppermute x3, starting transfers between devices, body(): others = [lax.ppermute(result, AXES, swap) for result in results]  8.94 us
    ppermute x3, starting transfers between devices, body(): arrived[0] = lax.ppermute(send, AXES, pairings[0])  6.55 us
    pallas_call x2, Pallas kernels, self_blocks(): pl.pallas_call(functools.partial(sigma_kernel, pieces), out_shape=[jax.Sh...  4.22 us
    ppermute x1, starting transfers between devices, body(): arrived[1] = lax.ppermute(send, AXES, pairings[1])  1.26 us
  transfers between devices with their start and end apart: 9, of which 6 were waited for; matrix products, arithmetic and copies ran while one was open for 0% of the time, Pallas kernels for 45%

profile of v3, /device:TPU:27, one launch (start us, length us, event | category | flops | bytes accessed | tf_op | source)
XLA Modules:
  0.0 49.1 jit_solution(12107324150388556281)
XLA Ops:
  0.6 0.1 pad_add_fusion.where
  0.7 2.4 %shard_map.86 = (bf16[512,256]{1,0:T(8,128)(2,1)S(1)}, bf16[512,256]{1,0:T(8,128)(2,1)S(1)}, bf16[2,512,512]{2,1,0:T(8,128)(2,1)S(1)}, bf16[2,512,512]{2,1,0:T(8,128)(2,1)S(1)}, f32[2,512,128]{2,1,0:T(8,128)S(1)}) custom-call(s32[4]{0:T(128)S(1)} %pad_add_fusion.where, bf16[2,2,512,512]{3,2,1,0:T(8,128)(2,1)} %bitcast.12, bf16[2,2,512,512]{3,2,1,0:T(8,128)(2,1)} %coupling.3, ...), custom_call_target="tpu_custom_call" | custom-call | flops 1000 | bytes 1000 | tf_op jit(solution)/shard_map/pallas_call | solution.py:274
  3.1 0.8 %collective-permute-start = (bf16[512,256]{1,0:T(8,128)(2,1)S(1)}, bf16[512,256]{1,0:T(8,128)(2,1)S(1)}, u32[]{:S(2)}, u32[]{:S(2)}) collective-permute-start(bf16[512,256]{1,0:T(8,128)(2,1)S(1)} %get-tuple-element.54), channel_id=1, source_target_pairs={{0,1},{1,0},{2,3},{3,2},{4,5},{5,4},{6,7},{7,6},{8,9},{9,8},{10,11... | collective-permute-start | bytes 786440 | tf_op jit(solution)/shard_map/ppermute | solution.py:356
  3.9 0.0 copy-start
  3.9 0.0 copy-start.1
  3.9 0.0 copy-start.2
  3.9 0.0 copy-start.3
  3.9 4.6 %shard_map.87 = (bf16[512,256]{1,0:T(8,128)(2,1)S(1)}, bf16[512,256]{1,0:T(8,128)(2,1)S(1)}, bf16[2,512,512]{2,1,0:T(8,128)(2,1)S(1)}, bf16[2,512,512]{2,1,0:T(8...) custom-call(s32[4]{0:T(128)S(1)} %pad_add_fusion.where, ...), custom_call_target="tpu_custom_call" | custom-call | flops 1000 | bytes 1000 | tf_op jit(solution)/shard_map/pallas_call | solution.py:274
  8.6 1.3 %collective-permute-start.1 = (bf16[512,256]{1,0:T(8,128)(2,1)S(1)}, bf16[512,256]{1,0:T(8,128)(2,1)S(1)}, u32[]{:S(2)}, u32[]{:S(2)}) collective-permute-start(bf16[512,256]{1,0:T(8,128)(2,1)S(1)} %get-tuple-element.57), channel_id=1, source_target_pairs={{0,16},{1,2},{2,1},{3,4},{4,3},{5,6},{6,5},{7,8},{8,7},{9,10},{10,... | collective-permute-start | bytes 786440 | tf_op jit(solution)/shard_map/ppermute | solution.py:364
  9.8 0.0 copy-done
  9.8 0.0 copy-done.1
  9.8 0.0 copy-done.2
  9.8 0.0 copy-done.3
  9.8 1.9 %shard_map.88 = (f32[512,256]{1,0:T(8,128)S(1)}, f32[512,256]{1,0:T(8,128)S(1)}, f32[256,8]{1,0:T(8,128)S(1)}) custom-call(s32[4]{0:T(128)S(1)} %pad_add_fusion.where, bf16[2,512,512]{2,1,0:T(8,128)(2,1)S(1)} %get-tuple-element.45.inner, f32[2,2,512]{2,1,0:T(2,128)S(1)} %bitcast.9, bf16[2,512,512]{2,1,0:T(8,128)(2,1)S(1)} %get-tuple-element.43.lead.own_a.own, ...), custom_call_target="tpu_custom_call" | custom-call | flops 1000 | bytes 1000 | tf_op jit(solution)/shard_map/pallas_call | solution.py:274
  11.8 0.0 collective-permute-done.arrived
  11.8 1.0 %shard_map.89 = (bf16[512,256]{1,0:T(8,128)(2,1)S(1)}, bf16[512,256]{1,0:T(8,128)(2,1)S(1)}) custom-call(s32[4]{0:T(128)S(1)} %pad_add_fusion.where, bf16[2,512,512]{2,1,0:T(8,128)(2,1)S(1)} %get-tuple-element.43.lead.own_a.own, bf16[2,512,512]{2,1,0:T(8,128)(2,1)S(1)} %get-tuple-element.52.chain, bf16[2,512,512]{2,1,0:T(8,128)(2,1)S(1)} %get-tuple-element.42.link, ...), custom_call_target="tpu_custom_call" | custom-call | flops 1000 | bytes 1000 | tf_op jit(solution)/shard_map/pallas_call | solution.py:274
  12.8 2.3 %collective-permute-start.2 = (bf16[512,256]{1,0:T(8,128)(2,1)S(1)}, bf16[512,256]{1,0:T(8,128)(2,1)S(1)}, u32[]{:S(2)}, u32[]{:S(2)}) collective-permute-start(bf16[512,256]{1,0:T(8,128)(2,1)S(1)} %get-tuple-element.61), channel_id=1, source_target_pairs={{0,1},{1,0},{2,3},{3,2},{4,5},{5,4},{6,7},{7,6},{8,9},{9,8},{10,11... | collective-permute-start | bytes 786440 | tf_op jit(solution)/shard_map/ppermute | solution.py:406
  15.0 1.0 %shard_map.90.rest_0_.term = f32[512,256]{1,0:T(8,128)S(1)} custom-call(s32[4]{0:T(128)S(1)} %pad_add_fusion.where, bf16[2,512,512]{2,1,0:T(8,128)(2,1)S(1)} %get-tuple-element.45.inner, bf16[512,256]{1,0:T(8,128)(2,1)S(1)} %get-tuple-element.55.states.states_a), custom_call_target="tpu_custom_call" | custom-call | flops 1000 | bytes 1000 | tf_op jit(solution)/shard_map/pallas_call | solution.py:274
  16.1 0.8 %collective-permute-done.1.arrived = bf16[512,256]{1,0:T(8,128)(2,1)S(1)} collective-permute-done((bf16[512,256]{1,0:T(8,128)(2,1)S(1)}, bf16[512,256]{1,0:T(8,128)(2,1)S(1)}, u32[]{:S(2)}, u32[]{:S(2)}) %collective-permute-start.1) | collective-permute-done | bytes 262176 | tf_op jit(solution)/shard_map/ppermute | solution.py:364
  16.9 1.8 %shard_map.91 = (bf16[512,256]{1,0:T(8,128)(2,1)S(1)}, bf16[512,256]{1,0:T(8,128)(2,1)S(1)}) custom-call(s32[4]{0:T(128)S(1)} %pad_add_fusion.where, bf16[2,512,512]{2,1,0:T(8,128)(2,1)S(1)} %get-tuple-element.46.own_b.own, bf16[2,512,512]{2,1,0:T(8,128)(2,1)S(1)} %get-tuple-element.52.chain, bf16[2,512,512]{2,1,0:T(8,128)(2,1)S(1)} %get-tuple-element.42.link, ...), custom_call_target="tpu_custom_call" | custom-call | flops 1000 | bytes 1000 | tf_op jit(solution)/shard_map/pallas_call | solution.py:274
  18.7 1.8 %shard_map.92 = (f32[512,256]{1,0:T(8,128)S(1)}, f32[512,256]{1,0:T(8,128)S(1)}, bf16[512,256]{1,0:T(8,128)(2,1)S(1)}) custom-call(s32[4]{0:T(128)S(1)} %pad_add_fusion.where, bf16[2,512,512]{2,1,0:T(8,128)(2,1)S(1)} %get-tuple-element.45.inner, f32[2,2,512]{2,1,0:T(2,128)S(1)} %bitcast.10, bf16[2,512,512]{2,1,0:T(8,128)(2,1)S(1)} %get-tuple-element.43.lead.own_a.own, ...), custom_call_target="tpu_custom_call" | custom-call | flops 1000 | bytes 1000 | tf_op jit(solution)/shard_map/pallas_call | solution.py:274
  20.5 0.2 collective-permute-start.3
  20.7 0.0 collective-permute-done.2.arrived
  20.7 1.2 %shard_map.93 = (bf16[512,256]{1,0:T(8,128)(2,1)S(1)}, bf16[512,256]{1,0:T(8,128)(2,1)S(1)}) custom-call(s32[4]{0:T(128)S(1)} %pad_add_fusion.where, bf16[2,512,512]{2,1,0:T(8,128)(2,1)S(1)} %get-tuple-element.43.lead.own_a.own, bf16[2,512,512]{2,1,0:T(8,128)(2,1)S(1)} %get-tuple-element.52.chain, bf16[2,512,512]{2,1,0:T(8,128)(2,1)S(1)} %get-tuple-element.42.link, ...), custom_call_target="tpu_custom_call" | custom-call | flops 1000 | bytes 1000 | tf_op jit(solution)/shard_map/pallas_call | solution.py:274
  21.9 3.5 %collective-permute-start.5 = (bf16[512,256]{1,0:T(8,128)(2,1)S(1)}, bf16[512,256]{1,0:T(8,128)(2,1)S(1)}, u32[]{:S(2)}, u32[]{:S(2)}) collective-permute-start(bf16[512,256]{1,0:T(8,128)(2,1)S(1)} %get-tuple-element.70), channel_id=1, source_target_pairs={{0,1},{1,0},{2,3},{3,2},{4,5},{5,4},{6,7},{7,6},{8,9},{9,8},{10,11... | collective-permute-start | bytes 786440 | tf_op jit(solution)/shard_map/ppermute | solution.py:406
  25.4 1.0 %shard_map.94.rest_0_.term = f32[512,256]{1,0:T(8,128)S(1)} custom-call(s32[4]{0:T(128)S(1)} %pad_add_fusion.where, bf16[2,512,512]{2,1,0:T(8,128)(2,1)S(1)} %get-tuple-element.45.inner, bf16[512,256]{1,0:T(8,128)(2,1)S(1)} %get-tuple-element.62.states.states_a), custom_call_target="tpu_custom_call" | custom-call | flops 1000 | bytes 1000 | tf_op jit(solution)/shard_map/pallas_call | solution.py:274
  26.4 0.3 collective-permute-done.3.arrived
  26.7 1.8 %shard_map.95 = (bf16[512,256]{1,0:T(8,128)(2,1)S(1)}, bf16[512,256]{1,0:T(8,128)(2,1)S(1)}) custom-call(s32[4]{0:T(128)S(1)} %pad_add_fusion.where, bf16[2,512,512]{2,1,0:T(8,128)(2,1)S(1)} %get-tuple-element.46.own_b.own, bf16[2,512,512]{2,1,0:T(8,128)(2,1)S(1)} %get-tuple-element.52.chain, bf16[2,512,512]{2,1,0:T(8,128)(2,1)S(1)} %get-tuple-element.42.link, ...), custom_call_target="tpu_custom_call" | custom-call | flops 1000 | bytes 1000 | tf_op jit(solution)/shard_map/pallas_call | solution.py:274
  28.5 1.8 %shard_map.96 = (f32[512,256]{1,0:T(8,128)S(1)}, f32[512,256]{1,0:T(8,128)S(1)}, bf16[512,256]{1,0:T(8,128)(2,1)S(1)}) custom-call(s32[4]{0:T(128)S(1)} %pad_add_fusion.where, bf16[2,512,512]{2,1,0:T(8,128)(2,1)S(1)} %get-tuple-element.45.inner, f32[2,2,512]{2,1,0:T(2,128)S(1)} %bitcast.11, bf16[2,512,512]{2,1,0:T(8,128)(2,1)S(1)} %get-tuple-element.43.lead.own_a.own, ...), custom_call_target="tpu_custom_call" | custom-call | flops 1000 | bytes 1000 | tf_op jit(solution)/shard_map/pallas_call | solution.py:274
  30.3 0.5 collective-permute-start.4
  30.8 0.6 %collective-permute-done.5.arrived = bf16[512,256]{1,0:T(8,128)(2,1)S(1)} collective-permute-done((bf16[512,256]{1,0:T(8,128)(2,1)S(1)}, bf16[512,256]{1,0:T(8,128)(2,1)S(1)}, u32[]{:S(2)}, u32[]{:S(2)}) %collective-permute-start.5) | collective-permute-done | bytes 262176 | tf_op jit(solution)/shard_map/ppermute | solution.py:406
  31.3 1.0 %shard_map.97 = (bf16[256,256]{1,0:T(8,128)(2,1)S(1)}, bf16[256,256]{1,0:T(8,128)(2,1)S(1)}) custom-call(s32[4]{0:T(128)S(1)} %pad_add_fusion.where, bf16[2,512,512]{2,1,0:T(8,128)(2,1)S(1)} %get-tuple-element.43.lead.own_a.own, bf16[2,512,512]{2,1,0:T(8,128)(2,1)S(1)} %get-tuple-element.52.chain, bf16[2,512,512]{2,1,0:T(8,128)(2,1)S(1)} %get-tuple-element.42.link, ...), custom_call_target="tpu_custom_call" | custom-call | flops 1000 | bytes 1000 | tf_op jit(solution)/shard_map/pallas_call | solution.py:274
  32.3 5.8 %collective-permute-start.6 = (bf16[256,256]{1,0:T(8,128)(2,1)S(1)}, bf16[256,256]{1,0:T(8,128)(2,1)S(1)}, u32[]{:S(2)}, u32[]{:S(2)}) collective-permute-start(bf16[256,256]{1,0:T(8,128)(2,1)S(1)} %get-tuple-element.71.rest_0_), channel_id=1, source_target_pairs={{0,16},{1,17},{2,18},{3,19},{4,20},{5,21},{6,22},{7,23},{8,24},{9,... | collective-permute-start | bytes 393224 | tf_op jit(solution)/shard_map/ppermute | solution.py:397
  38.1 0.1 collective-permute-start.7
  38.2 0.7 %shard_map.98 = (f32[2,512,512]{2,1,0:T(8,128)S(1)}, f32[2,512,256]{2,1,0:T(8,128)S(1)}) custom-call(f32[256,8]{1,0:T(8,128)S(1)} %get-tuple-element.51.scales, bf16[256,256]{1,0:T(8,128)(2,1)S(1)} %get-tuple-element.71.rest_0_, bf16[256,256]{1,0:T(8,128)(2,1)S(1)} %get-tuple-element.72.rest_1_), custom_call_target="tpu_custom_call" | custom-call | flops 1000 | bytes 1000 | tf_op jit(solution)/shard_map/pallas_call | solution.py:274
  39.0 0.2 collective-permute-done.6.rest_0_
  39.1 0.4 collective-permute-done.7.rest_1_
  39.5 1.8 %shard_map.99 = (bf16[2,2,512,512]{3,2,1,0:T(8,128)(2,1)}, bf16[2,2,512,512]{3,2,1,0:T(8,128)(2,1)}, f32[8,128]{1,0:T(8,128)S(1)}) custom-call(s32[1]{0:T(128)} %bitcast.1.where, f32[256,8]{1,0:T(8,128)S(1)} %get-tuple-element.51.scales, f32[2,512,512]{2,1,0:T(8,128)S(1)} %get-tuple-element.73.tops, f32[2,512,256]{2,1,0:T(8,128)S(1)} %get-tuple-element.74.lows, ...), custom_call_target="tpu_custom_call" | custom-call | flops 1000 | bytes 1000 | tf_op jit(solution)/shard_map/pallas_call | solution.py:297
  41.3 0.0 collective-permute-done.4.arrived
  41.3 1.0 %shard_map.100.rest_0_ = bf16[512,256]{1,0:T(8,128)(2,1)S(1)} custom-call(s32[4]{0:T(128)S(1)} %pad_add_fusion.where, bf16[2,512,512]{2,1,0:T(8,128)(2,1)S(1)} %get-tuple-element.46.own_b.own, bf16[2,512,512]{2,1,0:T(8,128)(2,1)S(1)} %get-tuple-element.52.chain, bf16[2,512,512]{2,1,0:T(8,128)(2,1)S(1)} %get-tuple-element.42.link, ...), custom_call_target="tpu_custom_call" | custom-call | flops 1000 | bytes 1000 | tf_op jit(solution)/shard_map/pallas_call | solution.py:274
  42.3 3.1 %collective-permute-start.8 = (bf16[512,256]{1,0:T(8,128)(2,1)S(1)}, bf16[512,256]{1,0:T(8,128)(2,1)S(1)}, u32[]{:S(2)}, u32[]{:S(2)}) collective-permute-start(bf16[512,256]{1,0:T(8,128)(2,1)S(1)} %shard_map.100.rest_0_), channel_id=1, source_target_pairs={{0,16},{1,17},{2,18},{3,19},{4,20},{5,21},{6,22},{7,23},{8,24},{9,... | collective-permute-start | bytes 786440 | tf_op jit(solution)/shard_map/ppermute | solution.py:397
  45.4 0.8 %shard_map.101 = (f32[2,512,512]{2,1,0:T(8,128)S(1)}, f32[2,512,256]{2,1,0:T(8,128)S(1)}) custom-call(f32[256,8]{1,0:T(8,128)S(1)} %get-tuple-element.51.scales, bf16[512,256]{1,0:T(8,128)(2,1)S(1)} %shard_map.100.rest_0_), custom_call_target="tpu_custom_call" | custom-call | flops 1000 | bytes 1000 | tf_op jit(solution)/shard_map/pallas_call | solution.py:274
  46.1 0.4 collective-permute-done.8.rest_0_
  46.5 2.4 %shard_map.102 = (bf16[2,2,512,512]{3,2,1,0:T(8,128)(2,1)}, bf16[2,2,512,512]{3,2,1,0:T(8,128)(2,1)}, f32[8,128]{1,0:T(8,128)}) custom-call(s32[1]{0:T(128)} %bitcast.where, f32[256,8]{1,0:T(8,128)S(1)} %get-tuple-element.51.scales, f32[2,512,512]{2,1,0:T(8,128)S(1)} %get-tuple-element.76.tops, ...), custom_call_target="tpu_custom_call", output_to_operand_aliasing={{0}: (5, {}), {1}: (6, {})} | custom-call | flops 1000 | bytes 1000 | tf_op jit(solution)/shard_map/pallas_call | solution.py:297
Async XLA Ops:
  3.1 8.6 %collective-permute-start = (bf16[512,256]{1,0:T(8,128)(2,1)S(1)}, bf16[512,256]{1,0:T(8,128)(2,1)S(1)}, u32[]{:S(2)}, u32[]{:S(2)}) collective-permute-start(bf16[512,256]{1,0:T(8,128)(2,1)S(1)} %get-tuple-element.54), channel_id=1, source_target_pairs={{0,1},{1,0},{2,3},{3,2},{4,5},{5,4},{6,7},{7,6},{8,9},{9,8},{10,11... | collective-permute-start | bytes 786440 | tf_op jit(solution)/shard_map/ppermute | solution.py:356
  3.9 5.9 %copy-start = (f32[1,2,2,512]{3,2,1,0:T(2,128)S(1)}, f32[1,2,2,512]{3,2,1,0:T(2,128)}, u32[]{:S(2)}) copy-start(f32[1,2,2,512]{3,2,1,0:T(2,128)} %param.10) | copy-start | bytes 24580
  3.9 5.9 %copy-start.1 = (f32[2,128]{1,0:T(2,128)S(1)}, f32[2,128]{1,0:T(2,128)}, u32[]{:S(2)}) copy-start(f32[2,128]{1,0:T(2,128)} %rest_0_.1) | copy-start | bytes 3076
  3.9 5.9 %copy-start.2 = (s32[2,4]{1,0:T(2,128)S(1)}, s32[2,4]{1,0:T(2,128)}, u32[]{:S(2)}) copy-start(s32[2,4]{1,0:T(2,128)} %rest_1_.1) | copy-start | bytes 100
  3.9 5.9 %copy-start.3 = (f32[2,4]{1,0:T(2,128)S(1)}, f32[2,4]{1,0:T(2,128)}, u32[]{:S(2)}) copy-start(f32[2,4]{1,0:T(2,128)} %rest_2_.1) | copy-start | bytes 100
  8.6 8.3 %collective-permute-start.1 = (bf16[512,256]{1,0:T(8,128)(2,1)S(1)}, bf16[512,256]{1,0:T(8,128)(2,1)S(1)}, u32[]{:S(2)}, u32[]{:S(2)}) collective-permute-start(bf16[512,256]{1,0:T(8,128)(2,1)S(1)} %get-tuple-element.57), channel_id=1, source_target_pairs={{0,16},{1,2},{2,1},{3,4},{4,3},{5,6},{6,5},{7,8},{8,7},{9,10},{10,... | collective-permute-start | bytes 786440 | tf_op jit(solution)/shard_map/ppermute | solution.py:364
  12.8 7.9 %collective-permute-start.2 = (bf16[512,256]{1,0:T(8,128)(2,1)S(1)}, bf16[512,256]{1,0:T(8,128)(2,1)S(1)}, u32[]{:S(2)}, u32[]{:S(2)}) collective-permute-start(bf16[512,256]{1,0:T(8,128)(2,1)S(1)} %get-tuple-element.61), channel_id=1, source_target_pairs={{0,1},{1,0},{2,3},{3,2},{4,5},{5,4},{6,7},{7,6},{8,9},{9,8},{10,11... | collective-permute-start | bytes 786440 | tf_op jit(solution)/shard_map/ppermute | solution.py:406
  20.5 6.2 %collective-permute-start.3 = (bf16[512,256]{1,0:T(8,128)(2,1)S(1)}, bf16[512,256]{1,0:T(8,128)(2,1)S(1)}, u32[]{:S(2)}, u32[]{:S(2)}) collective-permute-start(bf16[512,256]{1,0:T(8,128)(2,1)S(1)} %get-tuple-element.64), channel_id=1, source_target_pairs={{0,16},{1,2},{2,1},{3,4},{4,3},{5,6},{6,5},{7,8},{8,7},{9,10},{10,... | collective-permute-start | bytes 786440 | tf_op jit(solution)/shard_map/ppermute | solution.py:381
  21.9 9.5 %collective-permute-start.5 = (bf16[512,256]{1,0:T(8,128)(2,1)S(1)}, bf16[512,256]{1,0:T(8,128)(2,1)S(1)}, u32[]{:S(2)}, u32[]{:S(2)}) collective-permute-start(bf16[512,256]{1,0:T(8,128)(2,1)S(1)} %get-tuple-element.70), channel_id=1, source_target_pairs={{0,1},{1,0},{2,3},{3,2},{4,5},{5,4},{6,7},{7,6},{8,9},{9,8},{10,11... | collective-permute-start | bytes 786440 | tf_op jit(solution)/shard_map/ppermute | solution.py:406
  30.3 11.0 %collective-permute-start.4 = (bf16[512,256]{1,0:T(8,128)(2,1)S(1)}, bf16[512,256]{1,0:T(8,128)(2,1)S(1)}, u32[]{:S(2)}, u32[]{:S(2)}) collective-permute-start(bf16[512,256]{1,0:T(8,128)(2,1)S(1)} %get-tuple-element.68), channel_id=1, source_target_pairs={{0,16},{1,2},{2,1},{3,4},{4,3},{5,6},{6,5},{7,8},{8,7},{9,10},{10,... | collective-permute-start | bytes 786440 | tf_op jit(solution)/shard_map/ppermute | solution.py:381
  32.3 6.8 %collective-permute-start.6 = (bf16[256,256]{1,0:T(8,128)(2,1)S(1)}, bf16[256,256]{1,0:T(8,128)(2,1)S(1)}, u32[]{:S(2)}, u32[]{:S(2)}) collective-permute-start(bf16[256,256]{1,0:T(8,128)(2,1)S(1)} %get-tuple-element.71.rest_0_), channel_id=1, source_target_pairs={{0,16},{1,17},{2,18},{3,19},{4,20},{5,21},{6,22},{7,23},{8,24},{9,... | collective-permute-start | bytes 393224 | tf_op jit(solution)/shard_map/ppermute | solution.py:397
  38.1 1.3 %collective-permute-start.7 = (bf16[256,256]{1,0:T(8,128)(2,1)S(1)}, bf16[256,256]{1,0:T(8,128)(2,1)S(1)}, u32[]{:S(2)}, u32[]{:S(2)}) collective-permute-start(bf16[256,256]{1,0:T(8,128)(2,1)S(1)} %get-tuple-element.72.rest_1_), channel_id=1, source_target_pairs={{0,16},{1,17},{2,18},{3,19},{4,20},{5,21},{6,22},{7,23},{8,24},{9,... | collective-permute-start | bytes 393224 | tf_op jit(solution)/shard_map/ppermute | solution.py:397
  42.3 4.2 %collective-permute-start.8 = (bf16[512,256]{1,0:T(8,128)(2,1)S(1)}, bf16[512,256]{1,0:T(8,128)(2,1)S(1)}, u32[]{:S(2)}, u32[]{:S(2)}) collective-permute-start(bf16[512,256]{1,0:T(8,128)(2,1)S(1)} %shard_map.100.rest_0_), channel_id=1, source_target_pairs={{0,16},{1,17},{2,18},{3,19},{4,20},{5,21},{6,22},{7,23},{8,24},{9,... | collective-permute-start | bytes 786440 | tf_op jit(solution)/shard_map/ppermute | solution.py:397

commit v4 on v3

--- a/solution.py
+++ b/solution.py
@@ -13,7 +13,7 @@
 AXES = ("energy", "space")
 LEAD_A = True
 LEAD_PIECES = 2
-HOLD = True
+HELD = {1: (0, 2), 2: (0, 2), 3: (2, 2)}
 
 
 def times_i(pair, sign):
@@ -66,8 +66,17 @@
     fresh = partial.astype(BF16)
     states[...] = fresh
     copies[3].wait()
-    copies[4].wait()
-    send_fresh(slab, link, fresh, send)
+
+    @pl.when(slab == 0)
+    def _():
+        send[...] = fresh
+        copies[4].wait()
+
+    @pl.when(slab == 1)
+    def _():
+        handed = transposed_dot(link[0], fresh)
+        copies[4].wait()
+        send[...] = (handed + transposed_dot(link[1], times_i(fresh, -1))).astype(BF16)
 
 
 def trail_kernel(
@@ -129,19 +138,27 @@
         term[...] = adjoint(inner, states[...]).astype(BF16).astype(F32)
 
 
-def term_kernel(where, inner, states, term):
-    write_term(1 - where[0], inner, states, term)
-
-
-def base_kernel(kind, where, inner, sigma, own_a, own_b, source_a, source_b, states_a, states_b, term, *rest):
-    if kind == "first":
-        occupation, offsets, weights, base_a, base_b, scales = rest
-        write_scales(where[3], occupation, offsets, weights, scales)
-    elif kind == "holding":
-        waiting, base_a, base_b, send = rest
-        send[...] = waiting[...]
+def hand_kernel(where, chain, link, hand):
+    @pl.when(where[0] == 0)
+    def _():
+        both = adjoint(link, jnp.concatenate([chain[0], chain[1]], axis=1))
+        half = both.shape[1] // 2
+        hand[0] = both[:, :half].astype(BF16)
+        hand[1] = both[:, half:].astype(BF16)
+
+
+def base_kernel(
+    kind, held, last, where, inner, link, sigma, own_a, own_b, source_a, source_b, states_a, states_b, term, *rest
+):
+    if kind == "before":
+        base_a, base_b, base_send, send = rest[-4:]
+        send[...] = rest[0][...]
     else:
-        base_a, base_b = rest
+        base_a, base_b, base_send = rest[-3:]
+    parts = jnp.where(lax.rem(where[3], 2) == 0, held[0], held[1])
+    here_a, here_b = parts > 0, parts > 1
+    if kind == "after":
+        here_a, here_b = jnp.logical_not(here_a), jnp.logical_not(here_b)
 
     def local(slab, source, states):
         rows = states.shape[0]
@@ -154,20 +171,30 @@
         drive = jnp.concatenate([source[0], source[1]], axis=1)
         return drive + (real * wide + imag * turned)
 
-    @pl.when(where[0] == 1)
+    @pl.when(jnp.logical_and(here_a, where[0] == 1))
     def _():
         handed = adjoint(inner, states_b[...]).astype(BF16).astype(F32)
         base_a[...] = product(own_a, (local(1, source_a, states_a) + handed).astype(BF16))
+
+    @pl.when(jnp.logical_and(here_a, where[0] == 0))
+    def _():
+        base_a[...] = local(0, source_a, states_a) + product(inner, states_b[...])
+
+    @pl.when(jnp.logical_and(here_b, where[0] == 1))
+    def _():
         base_b[...] = local(0, source_b, states_b) + term[...]
 
-    @pl.when(where[0] == 0)
-    def _():
-        base_a[...] = local(0, source_a, states_a) + product(inner, states_b[...])
+    @pl.when(jnp.logical_and(here_b, where[0] == 0))
+    def _():
         driven = (local(1, source_b, states_b) + term[...]).astype(BF16)
-        base_b[...] = product(own_b, driven)
-
-
-def write_scales(energy, occupation, offsets, weights, scales):
+        solved = product(own_b, driven)
+        base_b[...] = solved
+        if not last:
+            base_send[...] = adjoint(link, solved.astype(BF16))
+
+
+def scales_kernel(where, occupation, offsets, weights, scales):
+    energy = where[3]
     modes = occupation.shape[1]
     rows = []
     for at, target in ((0, energy), (1, 1 - energy)):
@@ -203,7 +230,10 @@
     def _():
         fresh = (base[...] + product(chain, message())).astype(BF16)
         keep(fresh)
-        if not last:
+        if side and not last:
+            hand, base_send = rest[:2]
+            results[1][...] = (base_send[...] + product(hand, message())).astype(BF16)
+        elif not last:
             results[1][...] = adjoint(link, fresh).astype(BF16)
 
     @pl.when(slab == 0)
@@ -213,6 +243,9 @@
         keep(fresh)
         if not last:
             results[1][...] = fresh
+
+    if not side and not last:
+        write_term(1 - slab, rest[0], results[0], results[2])
 
 
 def weighted_squares(parts, scales, at):
@@ -270,13 +303,25 @@
 NEAR = pl.BlockSpec(memory_space=pltpu.VMEM)
 
 
-def call(kernel, outs, specs, args, scratch=()):
+def call(kernel, outs, specs, args, scratch=(), aliases=None):
+    scalars, specs, args = (args[0], specs[1:], args[1:]) if specs[0] is SCALAR else ((), specs, args)
+    count = len(scalars)
+    aliases = {count - 1 + source: target for source, target in (aliases or {}).items()}
+
+    def unpacked(*refs):
+        if count:
+            kernel([ref[0] for ref in refs[:count]], *refs[count:])
+        else:
+            kernel(*refs)
+
+    specs, args = [SCALAR] * count + list(specs), (*scalars, *args)
     return pl.pallas_call(
-        kernel,
+        unpacked,
         out_shape=outs,
         in_specs=specs,
         out_specs=[NEAR] * len(outs),
         scratch_shapes=list(scratch),
+        input_output_aliases=aliases,
         compiler_params=pltpu.CompilerParams(vmem_limit_bytes=24 * 2**20),
         cost_estimate=pl.CostEstimate(flops=1000, bytes_accessed=1000, transcendentals=0),
     )(*args)
@@ -319,7 +364,7 @@
         lead, valid = 1 - odd, [jnp.ones_like(inner), inner]
     else:
         lead, valid = odd, [inner, jnp.ones_like(inner)]
-    where = jnp.stack([lead, *valid, energy]).astype(jnp.int32)
+    where = [jnp.reshape(value, (1,)).astype(jnp.int32) for value in (lead, *valid, energy)]
 
     def at(e, c):
         return e * chips + c
@@ -361,32 +406,37 @@
         (where, precond, coupling, source, link, owns[0], states[0]),
         [pltpu.SemaphoreType.DMA((4,))],
     )
-    arrived[1] = lax.ppermute(send, AXES, pairings[1])
     for sweep in range(1, SWEEPS):
         first, last = sweep == 1, sweep == SWEEPS - 1
-        kind = "first" if first else "holding" if HOLD else "plain"
-        extra_out = {"first": [jax.ShapeDtypeStruct((width, 8), F32)], "holding": [pair], "plain": []}
-        extra_in = {"first": (occupation, shift_offsets, shift_weights), "holding": (send,) if not first else (), "plain": ()}
-        if kind == "plain":
-            arrived[1] = lax.ppermute(send, AXES, pairings[1])
+        common = (where, within, link, sigma, *owns, *drives, *states, term)
+        near = [SCALAR] + [NEAR] * 10
+        *bases, send = call(
+            functools.partial(base_kernel, "before", HELD[sweep], last),
+            [total, total, total, pair],
+            near + [NEAR],
+            common + (send,),
+        )
+        arrived[1] = lax.ppermute(send, AXES, pairings[1])
         bases = call(
-            functools.partial(base_kernel, kind),
-            [total, total] + extra_out[kind],
-            [SCALAR] + [NEAR] * 9 + [NEAR, SCALAR, SCALAR][: len(extra_in[kind])],
-            (where, within, sigma, *owns, *drives, *states, term) + extra_in[kind],
+            functools.partial(base_kernel, "after", HELD[sweep], last),
+            [total, total, total],
+            near + [NEAR] * 3,
+            common + tuple(bases),
+            aliases={11: 0, 12: 1, 13: 2},
         )
-        if first:
-            scales = bases[2]
-        elif kind == "holding":
-            arrived[1] = lax.ppermute(bases[2], AXES, pairings[1])
         states, blocks, token = list(states), [], []
         for side in range(2):
             if last:
                 pieces = 1 if side else LEAD_PIECES
                 outs = [jax.ShapeDtypeStruct((rows // pieces, width), BF16)] * pieces
             else:
-                outs = [pair, pair]
-            extra = token if last else [term] * side
+                outs = [pair, pair] if side else [pair, pair, total]
+            if last:
+                extra = token
+            elif side:
+                extra = [hand, bases[2]]
+            else:
+                extra = [within]
             results = call(
                 functools.partial(step_kernel, side, last, len(outs)),
                 outs,
@@ -401,12 +451,21 @@
                 )
                 token = [after]
                 continue
-            states[side], send = results
+            states[side], send = results[:2]
             if not side:
                 arrived[0] = lax.ppermute(send, AXES, pairings[0])
-                (term,) = call(
-                    term_kernel, [total], [SCALAR, NEAR, NEAR], (where, within, states[0])
-                )
+                term = results[2]
+                if first:
+                    (hand,) = call(
+                        hand_kernel, [matrix], [SCALAR, NEAR, NEAR], (where, chain, link)
+                    )
+                else:
+                    (scales,) = call(
+                        scales_kernel,
+                        [jax.ShapeDtypeStruct((width, 8), F32)],
+                        [SCALAR, NEAR, SCALAR, SCALAR],
+                        (where, occupation, shift_offsets, shift_weights),
+                    )
     return tuple(block[None] for block in blocks)
 
 

time: 49.3 us -> 47.4 us (0.961)
  the two profiles are of different devices: /device:TPU:27 before, /device:TPU:25 now
where the time goes in v4:
time: 47.4 us; the launch traced here: 47.2 us
  Pallas kernels  23.1 us (49%)
  waiting for transfers between devices  13.8 us (29%)
  starting transfers between devices  9.4 us (20%)
  between operations  0.98 us (2%)
    pallas_call x18, Pallas kernels, call(): pl.pallas_call(unpacked, out_shape=outs, in_specs=specs, out_specs=[NEAR]...  18.9 us
    ppermute x3, waiting for transfers between devices, body(): arrived[1] = lax.ppermute(send, AXES, pairings[1])  12.9 us
    ppermute x3, starting transfers between devices, body(): arrived[1] = lax.ppermute(send, AXES, pairings[1])  7.23 us
    pallas_call x2, Pallas kernels, self_blocks(): pl.pallas_call(functools.partial(sigma_kernel, pieces), out_shape=[jax.Sh...  4.2 us
    ppermute x3, starting transfers between devices, body(): others = [lax.ppermute(result, AXES, swap) for result in results]  1.25 us
  transfers between devices with their start and end apart: 9, of which 5 were waited for; matrix products, arithmetic and copies ran while one was open for 0% of the time, Pallas kernels for 38%

profile of v4, /device:TPU:25, one launch (start us, length us, event | category | flops | bytes accessed | tf_op | source)
XLA Modules:
  0.0 47.2 jit_solution(11691867653326056014)
XLA Ops:
  0.6 2.4 %shard_map.87 = (bf16[512,256]{1,0:T(8,128)(2,1)S(1)}, bf16[512,256]{1,0:T(8,128)(2,1)S(1)}, bf16[2,512,512]{2,1,0:T(8,128)(2,1)S(1)}, bf16[2,512,512]{2,1,0:T(8,128)(2,1)S(1)}, f32[2,512,128]{2,1,0:T(8,128)S(1)}) custom-call(s32[1]{0:T(128)} %bitcast.1.refs_0_.where, s32[1]{0:T(128)} %constant.16.clone.1.refs_1_, s32[1]{0:T(128)} %bitcast.2.refs_2_, ...), custom_call_target="tpu_custom_call" | custom-call | flops 1000 | bytes 1000 | tf_op jit(solution)/shard_map/pallas_call | solution.py:318
  3.0 0.8 %collective-permute-start = (bf16[512,256]{1,0:T(8,128)(2,1)S(1)}, bf16[512,256]{1,0:T(8,128)(2,1)S(1)}, u32[]{:S(2)}, u32[]{:S(2)}) collective-permute-start(bf16[512,256]{1,0:T(8,128)(2,1)S(1)} %get-tuple-element.70), channel_id=1, source_target_pairs={{0,1},{1,0},{2,3},{3,2},{4,5},{5,4},{6,7},{7,6},{8,9},{9,8},{10,11... | collective-permute-start | bytes 786440 | tf_op jit(solution)/shard_map/ppermute | solution.py:401
  3.8 0.0 copy-start
  3.8 3.6 %shard_map.88 = (bf16[512,256]{1,0:T(8,128)(2,1)S(1)}, bf16[512,256]{1,0:T(8,128)(2,1)S(1)}, bf16[2,512,512]{2,1,0:T(8,128)(2,1)S(1)}, bf16[2,512,512]{2,1,0:T(8...) custom-call(s32[1]{0:T(128)} %bitcast.1.refs_0_.where, ...), custom_call_target="tpu_custom_call" | custom-call | flops 1000 | bytes 1000 | tf_op jit(solution)/shard_map/pallas_call | solution.py:318
  7.4 0.0 copy-done
  7.4 1.8 %shard_map.89 = (f32[512,256]{1,0:T(8,128)S(1)}, f32[512,256]{1,0:T(8,128)S(1)}, f32[512,256]{1,0:T(8,128)S(1)}, bf16[512,256]{1,0:T(8,128)(2,1)S(1)}) custom-call(s32[1]{0:T(128)} %bitcast.1.refs_0_.where, s32[1]{0:T(128)} %constant.16.clone.1.refs_1_, s32[1]{0:T(128)} %bitcast.2.refs_2_, s32[1]{0:T(128)} %bitcast.3.refs_3_, ...), custom_call_target="tpu_custom_call" | custom-call | flops 1000 | bytes 1000 | tf_op jit(solution)/shard_map/pallas_call | solution.py:318
  9.1 2.5 %collective-permute-start.1 = (bf16[512,256]{1,0:T(8,128)(2,1)S(1)}, bf16[512,256]{1,0:T(8,128)(2,1)S(1)}, u32[]{:S(2)}, u32[]{:S(2)}) collective-permute-start(bf16[512,256]{1,0:T(8,128)(2,1)S(1)} %get-tuple-element.73), channel_id=1, source_target_pairs={{0,16},{1,2},{2,1},{3,4},{4,3},{5,6},{6,5},{7,8},{8,7},{9,10},{10,... | collective-permute-start | bytes 786440 | tf_op jit(solution)/shard_map/ppermute | solution.py:419
  11.7 0.0 collective-permute-done.refs_8_
  11.7 1.7 %shard_map.91 = (bf16[512,256]{1,0:T(8,128)(2,1)S(1)}, bf16[512,256]{1,0:T(8,128)(2,1)S(1)}, f32[512,256]{1,0:T(8,128)S(1)}) custom-call(s32[1]{0:T(128)} %bitcast.1.refs_0_.where, s32[1]{0:T(128)} %constant.16.clone.1.refs_1_, s32[1]{0:T(128)} %bitcast.2.refs_2_, s32[1]{0:T(128)} %bitcast.3.refs_3_, ...), custom_call_target="tpu_custom_call" | custom-call | flops 1000 | bytes 1000 | tf_op jit(solution)/shard_map/pallas_call | solution.py:318
  13.4 0.1 collective-permute-start.2
  13.5 5.3 %collective-permute-done.1.refs_8_ = bf16[512,256]{1,0:T(8,128)(2,1)S(1)} collective-permute-done((bf16[512,256]{1,0:T(8,128)(2,1)S(1)}, bf16[512,256]{1,0:T(8,128)(2,1)S(1)}, u32[]{:S(2)}, u32[]{:S(2)}) %collective-permute-start.1) | collective-permute-done | bytes 262176 | tf_op jit(solution)/shard_map/ppermute | solution.py:419
  18.8 0.4 shard_map.93
  19.3 1.8 %shard_map.94 = (f32[512,256]{1,0:T(8,128)S(1)}, f32[512,256]{1,0:T(8,128)S(1)}, f32[512,256]{1,0:T(8,128)S(1)}, bf16[512,256]{1,0:T(8,128)(2,1)S(1)}) custom-call(s32[1]{0:T(128)} %bitcast.1.refs_0_.where, s32[1]{0:T(128)} %constant.16.clone.1.refs_1_, s32[1]{0:T(128)} %bitcast.2.refs_2_, s32[1]{0:T(128)} %bitcast.3.refs_3_, ...), custom_call_target="tpu_custom_call" | custom-call | flops 1000 | bytes 1000 | tf_op jit(solution)/shard_map/pallas_call | solution.py:318
  21.1 2.8 %collective-permute-start.3 = (bf16[512,256]{1,0:T(8,128)(2,1)S(1)}, bf16[512,256]{1,0:T(8,128)(2,1)S(1)}, u32[]{:S(2)}, u32[]{:S(2)}) collective-permute-start(bf16[512,256]{1,0:T(8,128)(2,1)S(1)} %get-tuple-element.85), channel_id=1, source_target_pairs={{0,16},{1,2},{2,1},{3,4},{4,3},{5,6},{6,5},{7,8},{8,7},{9,10},{10,... | collective-permute-start | bytes 786440 | tf_op jit(solution)/shard_map/ppermute | solution.py:419
  23.8 0.0 collective-permute-done.2.refs_8_
  23.8 1.7 %shard_map.96 = (bf16[512,256]{1,0:T(8,128)(2,1)S(1)}, bf16[512,256]{1,0:T(8,128)(2,1)S(1)}, f32[512,256]{1,0:T(8,128)S(1)}) custom-call(s32[1]{0:T(128)} %bitcast.1.refs_0_.where, s32[1]{0:T(128)} %constant.16.clone.1.refs_1_, s32[1]{0:T(128)} %bitcast.2.refs_2_, s32[1]{0:T(128)} %bitcast.3.refs_3_, ...), custom_call_target="tpu_custom_call" | custom-call | flops 1000 | bytes 1000 | tf_op jit(solution)/shard_map/pallas_call | solution.py:318
  25.6 0.1 collective-permute-start.5
  25.7 4.5 %collective-permute-done.3.refs_8_ = bf16[512,256]{1,0:T(8,128)(2,1)S(1)} collective-permute-done((bf16[512,256]{1,0:T(8,128)(2,1)S(1)}, bf16[512,256]{1,0:T(8,128)(2,1)S(1)}, u32[]{:S(2)}, u32[]{:S(2)}) %collective-permute-start.3) | collective-permute-done | bytes 262176 | tf_op jit(solution)/shard_map/ppermute | solution.py:419
  30.2 0.4 shard_map.97
  30.6 1.8 %shard_map.98 = (f32[512,256]{1,0:T(8,128)S(1)}, f32[512,256]{1,0:T(8,128)S(1)}, f32[512,256]{1,0:T(8,128)S(1)}, bf16[512,256]{1,0:T(8,128)(2,1)S(1)}) custom-call(s32[1]{0:T(128)} %bitcast.1.refs_0_.where, s32[1]{0:T(128)} %constant.16.clone.1.refs_1_, s32[1]{0:T(128)} %bitcast.2.refs_2_, s32[1]{0:T(128)} %bitcast.3.refs_3_, ...), custom_call_target="tpu_custom_call" | custom-call | flops 1000 | bytes 1000 | tf_op jit(solution)/shard_map/pallas_call | solution.py:318
  32.4 1.9 %collective-permute-start.4 = (bf16[512,256]{1,0:T(8,128)(2,1)S(1)}, bf16[512,256]{1,0:T(8,128)(2,1)S(1)}, u32[]{:S(2)}, u32[]{:S(2)}) collective-permute-start(bf16[512,256]{1,0:T(8,128)(2,1)S(1)} %get-tuple-element.94), channel_id=1, source_target_pairs={{0,16},{1,2},{2,1},{3,4},{4,3},{5,6},{6,5},{7,8},{8,7},{9,10},{10,... | collective-permute-start | bytes 786440 | tf_op jit(solution)/shard_map/ppermute | solution.py:419
  34.3 0.0 copy-start.1
  34.3 0.0 copy-start.2
  34.3 0.0 copy-start.3
  34.3 0.4 collective-permute-done.5.refs_8_
  34.7 0.7 %shard_map.100 = (bf16[256,256]{1,0:T(8,128)(2,1)S(1)}, bf16[256,256]{1,0:T(8,128)(2,1)S(1)}) custom-call(s32[1]{0:T(128)} %bitcast.1.refs_0_.where, s32[1]{0:T(128)} %constant.16.clone.1.refs_1_, s32[1]{0:T(128)} %bitcast.2.refs_2_, s32[1]{0:T(128)} %bitcast.3.refs_3_, bf16[2,512,512]{2,1,0:T(8,128)(2,1)S(1)} %get-tuple-element.56.refs_8_.refs_7_.refs_4_, ...), custom_call_target="tpu_custom_call" | custom-call | flops 1000 | bytes 1000 | tf_op jit(solution)/shard_map/pallas_call | solution.py:318
  35.4 0.4 collective-permute-start.6
  35.9 0.1 collective-permute-start.7
  36.0 0.0 copy-done.1
  36.0 0.0 copy-done.2
  36.0 0.0 copy-done.3
  36.0 0.7 %shard_map.86.refs_0_.scales = f32[256,8]{1,0:T(8,128)S(1)} custom-call(s32[1]{0:T(128)} %bitcast.1.refs_0_.where, s32[1]{0:T(128)} %constant.16.clone.1.refs_1_, s32[1]{0:T(128)} %bitcast.2.refs_2_, s32[1]{0:T(128)} %bitcast.3.refs_3_, f32[2,128]{1,0:T(2,128)S(1)} %copy-done.1, s32[2,4]{1,0:T(2,128)S(1)} %copy-done.2, f32[2,4]{1,0:T(2,128)S(1)} %copy-done.3), custom_call_target="tpu_custom_call" | custom-call | flops 1000 | bytes 1000 | tf_op jit(solution)/shard_map/pallas_call | solution.py:318
  36.7 0.7 %shard_map.101 = (f32[2,512,512]{2,1,0:T(8,128)S(1)}, f32[2,512,256]{2,1,0:T(8,128)S(1)}) custom-call(f32[256,8]{1,0:T(8,128)S(1)} %shard_map.86.refs_0_.scales, bf16[256,256]{1,0:T(8,128)(2,1)S(1)} %get-tuple-element.97.refs_1_, bf16[256,256]{1,0:T(8,128)(2,1)S(1)} %get-tuple-element.98.refs_2_), custom_call_target="tpu_custom_call" | custom-call | flops 1000 | bytes 1000 | tf_op jit(solution)/shard_map/pallas_call | solution.py:318
  37.4 0.0 collective-permute-done.6.rest_0_
  37.4 0.0 collective-permute-done.7.rest_1_
  37.4 1.8 %shard_map.102 = (bf16[2,2,512,512]{3,2,1,0:T(8,128)(2,1)}, bf16[2,2,512,512]{3,2,1,0:T(8,128)(2,1)}, f32[8,128]{1,0:T(8,128)S(1)}) custom-call(s32[1]{0:T(128)} %bitcast.1.refs_0_.where, f32[256,8]{1,0:T(8,128)S(1)} %shard_map.86.refs_0_.scales, f32[2,512,512]{2,1,0:T(8,128)S(1)} %get-tuple-element.99.tops, f32[2,512,256]{2,1,0:T(8,128)S(1)} %get-tuple-element.100.lows, ...), custom_call_target="tpu_custom_call" | custom-call | flops 1000 | bytes 1000 | tf_op jit(solution)/shard_map/pallas_call | solution.py:342
  39.3 3.1 %collective-permute-done.4.refs_8_ = bf16[512,256]{1,0:T(8,128)(2,1)S(1)} collective-permute-done((bf16[512,256]{1,0:T(8,128)(2,1)S(1)}, bf16[512,256]{1,0:T(8,128)(2,1)S(1)}, u32[]{:S(2)}, u32[]{:S(2)}) %collective-permute-start.4) | collective-permute-done | bytes 262176 | tf_op jit(solution)/shard_map/ppermute | solution.py:419
  42.4 0.5 shard_map.103.refs_1_
  42.8 0.7 %collective-permute-start.8 = (bf16[512,256]{1,0:T(8,128)(2,1)S(1)}, bf16[512,256]{1,0:T(8,128)(2,1)S(1)}, u32[]{:S(2)}, u32[]{:S(2)}) collective-permute-start(bf16[512,256]{1,0:T(8,128)(2,1)S(1)} %shard_map.103.refs_1_), channel_id=1, source_target_pairs={{0,16},{1,17},{2,18},{3,19},{4,20},{5,21},{6,22},{7,23},{8,24},{9,... | collective-permute-start | bytes 786440 | tf_op jit(solution)/shard_map/ppermute | solution.py:447
  43.5 0.7 %shard_map.104 = (f32[2,512,512]{2,1,0:T(8,128)S(1)}, f32[2,512,256]{2,1,0:T(8,128)S(1)}) custom-call(f32[256,8]{1,0:T(8,128)S(1)} %shard_map.86.refs_0_.scales, bf16[512,256]{1,0:T(8,128)(2,1)S(1)} %shard_map.103.refs_1_), custom_call_target="tpu_custom_call" | custom-call | flops 1000 | bytes 1000 | tf_op jit(solution)/shard_map/pallas_call | solution.py:318
  44.2 0.4 collective-permute-done.8.rest_0_
  44.7 2.4 %shard_map.105 = (bf16[2,2,512,512]{3,2,1,0:T(8,128)(2,1)}, bf16[2,2,512,512]{3,2,1,0:T(8,128)(2,1)}, f32[8,128]{1,0:T(8,128)}) custom-call(s32[1]{0:T(128)} %bitcast.where, f32[256,8]{1,0:T(8,128)S(1)} %shard_map.86.refs_0_.scales, f32[2,512,512]{2,1,0:T(8,128)S(1)} %get-tuple-element.102.tops, ...), custom_call_target="tpu_custom_call", output_to_operand_aliasing={{0}: (5, {}), {1}: (6, {})} | custom-call | flops 1000 | bytes 1000 | tf_op jit(solution)/shard_map/pallas_call | solution.py:342
  (4 shorter events, 0.0 us)
Async XLA Ops:
  3.0 8.7 %collective-permute-start = (bf16[512,256]{1,0:T(8,128)(2,1)S(1)}, bf16[512,256]{1,0:T(8,128)(2,1)S(1)}, u32[]{:S(2)}, u32[]{:S(2)}) collective-permute-start(bf16[512,256]{1,0:T(8,128)(2,1)S(1)} %get-tuple-element.70), channel_id=1, source_target_pairs={{0,1},{1,0},{2,3},{3,2},{4,5},{5,4},{6,7},{7,6},{8,9},{9,8},{10,11... | collective-permute-start | bytes 786440 | tf_op jit(solution)/shard_map/ppermute | solution.py:401
  3.8 3.6 %copy-start = (f32[1,2,2,512]{3,2,1,0:T(2,128)S(1)}, f32[1,2,2,512]{3,2,1,0:T(2,128)}, u32[]{:S(2)}) copy-start(f32[1,2,2,512]{3,2,1,0:T(2,128)} %param.10) | copy-start | bytes 24580
  9.1 9.7 %collective-permute-start.1 = (bf16[512,256]{1,0:T(8,128)(2,1)S(1)}, bf16[512,256]{1,0:T(8,128)(2,1)S(1)}, u32[]{:S(2)}, u32[]{:S(2)}) collective-permute-start(bf16[512,256]{1,0:T(8,128)(2,1)S(1)} %get-tuple-element.73), channel_id=1, source_target_pairs={{0,16},{1,2},{2,1},{3,4},{4,3},{5,6},{6,5},{7,8},{8,7},{9,10},{10,... | collective-permute-start | bytes 786440 | tf_op jit(solution)/shard_map/ppermute | solution.py:419
  13.4 10.4 %collective-permute-start.2 = (bf16[512,256]{1,0:T(8,128)(2,1)S(1)}, bf16[512,256]{1,0:T(8,128)(2,1)S(1)}, u32[]{:S(2)}, u32[]{:S(2)}) collective-permute-start(bf16[512,256]{1,0:T(8,128)(2,1)S(1)} %get-tuple-element.82), channel_id=1, source_target_pairs={{0,1},{1,0},{2,3},{3,2},{4,5},{5,4},{6,7},{7,6},{8,9},{9,8},{10,11... | collective-permute-start | bytes 786440 | tf_op jit(solution)/shard_map/ppermute | solution.py:456
  21.1 9.1 %collective-permute-start.3 = (bf16[512,256]{1,0:T(8,128)(2,1)S(1)}, bf16[512,256]{1,0:T(8,128)(2,1)S(1)}, u32[]{:S(2)}, u32[]{:S(2)}) collective-permute-start(bf16[512,256]{1,0:T(8,128)(2,1)S(1)} %get-tuple-element.85), channel_id=1, source_target_pairs={{0,16},{1,2},{2,1},{3,4},{4,3},{5,6},{6,5},{7,8},{8,7},{9,10},{10,... | collective-permute-start | bytes 786440 | tf_op jit(solution)/shard_map/ppermute | solution.py:419
  25.6 9.2 %collective-permute-start.5 = (bf16[512,256]{1,0:T(8,128)(2,1)S(1)}, bf16[512,256]{1,0:T(8,128)(2,1)S(1)}, u32[]{:S(2)}, u32[]{:S(2)}) collective-permute-start(bf16[512,256]{1,0:T(8,128)(2,1)S(1)} %get-tuple-element.96), channel_id=1, source_target_pairs={{0,1},{1,0},{2,3},{3,2},{4,5},{5,4},{6,7},{7,6},{8,9},{9,8},{10,11... | collective-permute-start | bytes 786440 | tf_op jit(solution)/shard_map/ppermute | solution.py:456
  32.4 10.0 %collective-permute-start.4 = (bf16[512,256]{1,0:T(8,128)(2,1)S(1)}, bf16[512,256]{1,0:T(8,128)(2,1)S(1)}, u32[]{:S(2)}, u32[]{:S(2)}) collective-permute-start(bf16[512,256]{1,0:T(8,128)(2,1)S(1)} %get-tuple-element.94), channel_id=1, source_target_pairs={{0,16},{1,2},{2,1},{3,4},{4,3},{5,6},{6,5},{7,8},{8,7},{9,10},{10,... | collective-permute-start | bytes 786440 | tf_op jit(solution)/shard_map/ppermute | solution.py:419
  34.3 1.7 %copy-start.1 = (f32[2,128]{1,0:T(2,128)S(1)}, f32[2,128]{1,0:T(2,128)}, u32[]{:S(2)}) copy-start(f32[2,128]{1,0:T(2,128)} %refs_4_.1) | copy-start | bytes 3076
  34.3 1.7 %copy-start.2 = (s32[2,4]{1,0:T(2,128)S(1)}, s32[2,4]{1,0:T(2,128)}, u32[]{:S(2)}) copy-start(s32[2,4]{1,0:T(2,128)} %refs_5_.3) | copy-start | bytes 100
  34.3 1.7 %copy-start.3 = (f32[2,4]{1,0:T(2,128)S(1)}, f32[2,4]{1,0:T(2,128)}, u32[]{:S(2)}) copy-start(f32[2,4]{1,0:T(2,128)} %refs_6_.1) | copy-start | bytes 100
  35.4 2.0 %collective-permute-start.6 = (bf16[256,256]{1,0:T(8,128)(2,1)S(1)}, bf16[256,256]{1,0:T(8,128)(2,1)S(1)}, u32[]{:S(2)}, u32[]{:S(2)}) collective-permute-start(bf16[256,256]{1,0:T(8,128)(2,1)S(1)} %get-tuple-element.97.refs_1_), channel_id=1, source_target_pairs={{0,16},{1,17},{2,18},{3,19},{4,20},{5,21},{6,22},{7,23},{8,24},{9,... | collective-permute-start | bytes 393224 | tf_op jit(solution)/shard_map/ppermute | solution.py:447
  35.9 1.6 %collective-permute-start.7 = (bf16[256,256]{1,0:T(8,128)(2,1)S(1)}, bf16[256,256]{1,0:T(8,128)(2,1)S(1)}, u32[]{:S(2)}, u32[]{:S(2)}) collective-permute-start(bf16[256,256]{1,0:T(8,128)(2,1)S(1)} %get-tuple-element.98.refs_2_), channel_id=1, source_target_pairs={{0,16},{1,17},{2,18},{3,19},{4,20},{5,21},{6,22},{7,23},{8,24},{9,... | collective-permute-start | bytes 393224 | tf_op jit(solution)/shard_map/ppermute | solution.py:447
  42.8 1.8 %collective-permute-start.8 = (bf16[512,256]{1,0:T(8,128)(2,1)S(1)}, bf16[512,256]{1,0:T(8,128)(2,1)S(1)}, u32[]{:S(2)}, u32[]{:S(2)}) collective-permute-start(bf16[512,256]{1,0:T(8,128)(2,1)S(1)} %shard_map.103.refs_1_), channel_id=1, source_target_pairs={{0,16},{1,17},{2,18},{3,19},{4,20},{5,21},{6,22},{7,23},{8,24},{9,... | collective-permute-start | bytes 786440 | tf_op jit(solution)/shard_map/ppermute | solution.py:447

commit v5 on v4

--- a/solution.py
+++ b/solution.py
@@ -13,7 +13,7 @@
 AXES = ("energy", "space")
 LEAD_A = True
 LEAD_PIECES = 2
-HELD = {1: (0, 2), 2: (0, 2), 3: (2, 2)}
+HELD = {1: (0, 2), 2: (0, 2), 3: (2, 1)}
 
 
 def times_i(pair, sign):
@@ -248,48 +248,54 @@
         write_term(1 - slab, rest[0], results[0], results[2])
 
 
-def weighted_squares(parts, scales, at):
+def squares_inputs(parts):
     pair = jnp.concatenate([part[...] for part in parts], axis=0)
-    half = pair.shape[0] // 2
-    turned = times_i(pair, -1)
-    upper = jnp.concatenate([pair[:half], turned[:half]], axis=0)
-    lower = jnp.concatenate([pair[half:], turned[half:]], axis=0)
-    wide = jnp.transpose(pair).astype(F32)
-    for kind in range(2):
-        weighted = (wide * scales[:, 2 * at + kind : 2 * at + kind + 1]).astype(BF16)
-        yield (
-            kind,
-            jnp.dot(upper, weighted, preferred_element_type=F32),
-            jnp.dot(lower, weighted[:, half:], preferred_element_type=F32),
-        )
+    return (pair, times_i(pair, -1)), jnp.transpose(pair).astype(F32)
 
 
 def own_sigma_kernel(pieces, scales, *rest):
     tops, lows = rest[pieces:]
-    for kind, top, low in weighted_squares(rest[:pieces], scales, 0):
-        tops[kind] = top
-        lows[kind] = low
-
-
-def sigma_kernel(pieces, where, scales, tops, lows, *rest):
-    lesser, greater, token, held, sems = rest[-5:]
-    token[...] = jnp.zeros_like(token)
+    lefts, wide = squares_inputs(rest[:pieces])
+    half = wide.shape[1] // 2
+    upper = jnp.concatenate([left[:half] for left in lefts], axis=0)
+    lower = jnp.concatenate([left[half:] for left in lefts], axis=0)
+    for kind in range(2):
+        weighted = (wide * scales[:, kind : kind + 1]).astype(BF16)
+        tops[kind] = jnp.dot(upper, weighted, preferred_element_type=F32)
+        lows[kind] = jnp.dot(lower, weighted[:, half:], preferred_element_type=F32)
+
+
+def sigma_kernel(pieces, aliased, where, scales, tops, lows, *rest):
+    lesser, greater, *token, held, sems = rest[pieces + aliased :]
+    for ref in token:
+        ref[...] = jnp.zeros_like(ref)
+    lefts, wide = squares_inputs(rest[:pieces])
+    half = wide.shape[1] // 2
     copies = []
-    for kind, top, low in weighted_squares(rest[:pieces], scales, 1):
-        out = greater if kind else lesser
-        top = (top + tops[kind]).astype(BF16)
-        low = (low + lows[kind]).astype(BF16)
-        half = low.shape[1]
-        held[kind, 0, :half] = top[:half]
-        held[kind, 1, :half] = top[half:]
-        rows = slice(0, half)
-        copies.append(load(held.at[kind, :, rows], out.at[where[0], :, rows], sems.at[kind, 0]))
-        held[kind, 0, half:, half:] = low[:half]
-        held[kind, 1, half:, half:] = low[half:]
-        held[kind, 0, half:, :half] = jnp.transpose(top[:half, half:])
-        held[kind, 1, half:, :half] = -jnp.transpose(top[half:, half:])
-        rows = slice(half, 2 * half)
-        copies.append(load(held.at[kind, :, rows], out.at[where[0], :, rows], sems.at[kind, 1]))
+
+    def send(kind, out, part, at):
+        rows = slice(at * half, (at + 1) * half)
+        copies.append(
+            load(held.at[kind, part, rows], out.at[where[0], part, rows], sems.at[kind, 2 * part + at])
+        )
+
+    for kind, out in ((0, lesser), (1, greater)):
+        weighted = (wide * scales[:, 2 + kind : 3 + kind]).astype(BF16)
+        corners = []
+        for part, left in enumerate(lefts):
+            rows = slice(part * half, (part + 1) * half)
+            top = jnp.dot(left[:half], weighted, preferred_element_type=F32) + tops[kind, rows]
+            top = top.astype(BF16)
+            held[kind, part, :half] = top
+            send(kind, out, part, 0)
+            corners.append(top[:, half:])
+        for part, left in enumerate(lefts):
+            rows = slice(part * half, (part + 1) * half)
+            low = jnp.dot(left[half:], weighted[:, half:], preferred_element_type=F32)
+            held[kind, part, half:, half:] = (low + lows[kind, rows]).astype(BF16)
+            turned = jnp.transpose(corners[part])
+            held[kind, part, half:, :half] = -turned if part else turned
+            send(kind, out, part, 1)
     for copy in copies:
         copy.wait()
 
@@ -330,6 +336,7 @@
 def self_blocks(where, scales, own, other, blocks, previous):
     rows = sum(part.shape[0] for part in own)
     pieces = len(own)
+    token = [] if previous else [jax.ShapeDtypeStruct((8, 128), F32)]
     sums = call(
         functools.partial(own_sigma_kernel, pieces),
         [
@@ -340,13 +347,13 @@
         (scales, *own),
     )
     return pl.pallas_call(
-        functools.partial(sigma_kernel, pieces),
-        out_shape=[jax.ShapeDtypeStruct(blocks, BF16)] * 2 + [jax.ShapeDtypeStruct((8, 128), F32)],
+        functools.partial(sigma_kernel, pieces, len(previous)),
+        out_shape=[jax.ShapeDtypeStruct(blocks, BF16)] * 2 + token,
         in_specs=[SCALAR] + [NEAR] * (3 + pieces) + [pl.BlockSpec(memory_space=pl.ANY)] * len(previous),
-        out_specs=[pl.BlockSpec(memory_space=pl.ANY)] * 2 + [NEAR],
+        out_specs=[pl.BlockSpec(memory_space=pl.ANY)] * 2 + [NEAR] * len(token),
         scratch_shapes=[
             pltpu.VMEM((2, 2, rows, rows), BF16),
-            pltpu.SemaphoreType.DMA((2, 2)),
+            pltpu.SemaphoreType.DMA((2, 4)),
         ],
         input_output_aliases={4 + pieces + at: at for at in range(len(previous))},
         compiler_params=pltpu.CompilerParams(vmem_limit_bytes=24 * 2**20),
@@ -446,10 +453,8 @@
             if last:
                 others = [lax.ppermute(result, AXES, swap) for result in results]
                 slab = (1 - lead if side else lead)[None].astype(jnp.int32)
-                *blocks, after = self_blocks(
-                    slab, scales, results, others, (slabs, 2, rows, rows), blocks
-                )
-                token = [after]
+                blocks = self_blocks(slab, scales, results, others, (slabs, 2, rows, rows), blocks)
+                blocks, token = blocks[:2], blocks[2:]
                 continue
             states[side], send = results[:2]
             if not side:

time: 47.4 us -> 46.4 us (0.979)
  Pallas kernels: 23.1 us -> 22.5 us
    ppermute x3, waiting for transfers between devices: 12.9 us -> 12.2 us  [body(): arrived[1] = lax.ppermute(send, AXES, pairings[1])]
    pallas_call x2, Pallas kernels: 4.2 us -> 3.61 us  [self_blocks(): pl.pallas_call(functools.partial(sigma_kernel, pieces, len(previous)), ou...]
  transfers between devices with their start and end apart: 9 -> 9, of which waited for: 5 -> 5; matrix products, arithmetic and copies ran while one was open for 0% -> 0% of each run, Pallas kernels for 38% -> 39%
where the time goes in v5:
time: 46.4 us; the launch traced here: 46.3 us
  Pallas kernels  22.5 us (48%)
  waiting for transfers between devices  13.4 us (29%)
  starting transfers between devices  9.34 us (20%)
  between operations  1.01 us (2%)
    pallas_call x18, Pallas kernels, call(): pl.pallas_call(unpacked, out_shape=outs, in_specs=specs, out_specs=[NEAR]...  18.9 us
    ppermute x3, waiting for transfers between devices, body(): arrived[1] = lax.ppermute(send, AXES, pairings[1])  12.2 us
    ppermute x3, starting transfers between devices, body(): arrived[1] = lax.ppermute(send, AXES, pairings[1])  6.83 us
    pallas_call x2, Pallas kernels, self_blocks(): pl.pallas_call(functools.partial(sigma_kernel, pieces, len(previous)), ou...  3.61 us
    ppermute x3, starting transfers between devices, body(): others = [lax.ppermute(result, AXES, swap) for result in results]  1.59 us
  transfers between devices with their start and end apart: 9, of which 5 were waited for; matrix products, arithmetic and copies ran while one was open for 0% of the time, Pallas kernels for 39%

profile of v5, /device:TPU:25, one launch (start us, length us, event | category | flops | bytes accessed | tf_op | source)
XLA Modules:
  0.0 46.3 jit_solution(8948114294861125158)
XLA Ops:
  0.6 2.4 %shard_map.87 = (bf16[512,256]{1,0:T(8,128)(2,1)S(1)}, bf16[512,256]{1,0:T(8,128)(2,1)S(1)}, bf16[2,512,512]{2,1,0:T(8,128)(2,1)S(1)}, bf16[2,512,512]{2,1,0:T(8,128)(2,1)S(1)}, f32[2,512,128]{2,1,0:T(8,128)S(1)}) custom-call(s32[1]{0:T(128)} %bitcast.1.refs_0_.where, s32[1]{0:T(128)} %constant.16.clone.1.refs_1_, s32[1]{0:T(128)} %bitcast.2.refs_2_, ...), custom_call_target="tpu_custom_call" | custom-call | flops 1000 | bytes 1000 | tf_op jit(solution)/shard_map/pallas_call | solution.py:324
  3.0 0.8 %collective-permute-start = (bf16[512,256]{1,0:T(8,128)(2,1)S(1)}, bf16[512,256]{1,0:T(8,128)(2,1)S(1)}, u32[]{:S(2)}, u32[]{:S(2)}) collective-permute-start(bf16[512,256]{1,0:T(8,128)(2,1)S(1)} %get-tuple-element.70), channel_id=1, source_target_pairs={{0,1},{1,0},{2,3},{3,2},{4,5},{5,4},{6,7},{7,6},{8,9},{9,8},{10,11... | collective-permute-start | bytes 786440 | tf_op jit(solution)/shard_map/ppermute | solution.py:408
  3.8 0.0 copy-start
  3.8 3.6 %shard_map.88 = (bf16[512,256]{1,0:T(8,128)(2,1)S(1)}, bf16[512,256]{1,0:T(8,128)(2,1)S(1)}, bf16[2,512,512]{2,1,0:T(8,128)(2,1)S(1)}, bf16[2,512,512]{2,1,0:T(8...) custom-call(s32[1]{0:T(128)} %bitcast.1.refs_0_.where, ...), custom_call_target="tpu_custom_call" | custom-call | flops 1000 | bytes 1000 | tf_op jit(solution)/shard_map/pallas_call | solution.py:324
  7.4 0.0 copy-done
  7.4 1.8 %shard_map.89 = (f32[512,256]{1,0:T(8,128)S(1)}, f32[512,256]{1,0:T(8,128)S(1)}, f32[512,256]{1,0:T(8,128)S(1)}, bf16[512,256]{1,0:T(8,128)(2,1)S(1)}) custom-call(s32[1]{0:T(128)} %bitcast.1.refs_0_.where, s32[1]{0:T(128)} %constant.16.clone.1.refs_1_, s32[1]{0:T(128)} %bitcast.2.refs_2_, s32[1]{0:T(128)} %bitcast.3.refs_3_, ...), custom_call_target="tpu_custom_call" | custom-call | flops 1000 | bytes 1000 | tf_op jit(solution)/shard_map/pallas_call | solution.py:324
  9.1 2.5 %collective-permute-start.1 = (bf16[512,256]{1,0:T(8,128)(2,1)S(1)}, bf16[512,256]{1,0:T(8,128)(2,1)S(1)}, u32[]{:S(2)}, u32[]{:S(2)}) collective-permute-start(bf16[512,256]{1,0:T(8,128)(2,1)S(1)} %get-tuple-element.73), channel_id=1, source_target_pairs={{0,16},{1,2},{2,1},{3,4},{4,3},{5,6},{6,5},{7,8},{8,7},{9,10},{10,... | collective-permute-start | bytes 786440 | tf_op jit(solution)/shard_map/ppermute | solution.py:426
  11.7 0.0 collective-permute-done.refs_8_
  11.7 1.7 %shard_map.91 = (bf16[512,256]{1,0:T(8,128)(2,1)S(1)}, bf16[512,256]{1,0:T(8,128)(2,1)S(1)}, f32[512,256]{1,0:T(8,128)S(1)}) custom-call(s32[1]{0:T(128)} %bitcast.1.refs_0_.where, s32[1]{0:T(128)} %constant.16.clone.1.refs_1_, s32[1]{0:T(128)} %bitcast.2.refs_2_, s32[1]{0:T(128)} %bitcast.3.refs_3_, ...), custom_call_target="tpu_custom_call" | custom-call | flops 1000 | bytes 1000 | tf_op jit(solution)/shard_map/pallas_call | solution.py:324
  13.4 0.1 collective-permute-start.2
  13.5 5.3 %collective-permute-done.1.refs_8_ = bf16[512,256]{1,0:T(8,128)(2,1)S(1)} collective-permute-done((bf16[512,256]{1,0:T(8,128)(2,1)S(1)}, bf16[512,256]{1,0:T(8,128)(2,1)S(1)}, u32[]{:S(2)}, u32[]{:S(2)}) %collective-permute-start.1) | collective-permute-done | bytes 262176 | tf_op jit(solution)/shard_map/ppermute | solution.py:426
  18.8 0.4 shard_map.93
  19.3 1.8 %shard_map.94 = (f32[512,256]{1,0:T(8,128)S(1)}, f32[512,256]{1,0:T(8,128)S(1)}, f32[512,256]{1,0:T(8,128)S(1)}, bf16[512,256]{1,0:T(8,128)(2,1)S(1)}) custom-call(s32[1]{0:T(128)} %bitcast.1.refs_0_.where, s32[1]{0:T(128)} %constant.16.clone.1.refs_1_, s32[1]{0:T(128)} %bitcast.2.refs_2_, s32[1]{0:T(128)} %bitcast.3.refs_3_, ...), custom_call_target="tpu_custom_call" | custom-call | flops 1000 | bytes 1000 | tf_op jit(solution)/shard_map/pallas_call | solution.py:324
  21.1 2.8 %collective-permute-start.3 = (bf16[512,256]{1,0:T(8,128)(2,1)S(1)}, bf16[512,256]{1,0:T(8,128)(2,1)S(1)}, u32[]{:S(2)}, u32[]{:S(2)}) collective-permute-start(bf16[512,256]{1,0:T(8,128)(2,1)S(1)} %get-tuple-element.85), channel_id=1, source_target_pairs={{0,16},{1,2},{2,1},{3,4},{4,3},{5,6},{6,5},{7,8},{8,7},{9,10},{10,... | collective-permute-start | bytes 786440 | tf_op jit(solution)/shard_map/ppermute | solution.py:426
  23.8 0.0 collective-permute-done.2.refs_8_
  23.8 1.7 %shard_map.96 = (bf16[512,256]{1,0:T(8,128)(2,1)S(1)}, bf16[512,256]{1,0:T(8,128)(2,1)S(1)}, f32[512,256]{1,0:T(8,128)S(1)}) custom-call(s32[1]{0:T(128)} %bitcast.1.refs_0_.where, s32[1]{0:T(128)} %constant.16.clone.1.refs_1_, s32[1]{0:T(128)} %bitcast.2.refs_2_, s32[1]{0:T(128)} %bitcast.3.refs_3_, ...), custom_call_target="tpu_custom_call" | custom-call | flops 1000 | bytes 1000 | tf_op jit(solution)/shard_map/pallas_call | solution.py:324
  25.6 0.1 collective-permute-start.5
  25.7 4.5 %collective-permute-done.3.refs_8_ = bf16[512,256]{1,0:T(8,128)(2,1)S(1)} collective-permute-done((bf16[512,256]{1,0:T(8,128)(2,1)S(1)}, bf16[512,256]{1,0:T(8,128)(2,1)S(1)}, u32[]{:S(2)}, u32[]{:S(2)}) %collective-permute-start.3) | collective-permute-done | bytes 262176 | tf_op jit(solution)/shard_map/ppermute | solution.py:426
  30.2 0.4 shard_map.97
  30.6 1.4 %shard_map.98 = (f32[512,256]{1,0:T(8,128)S(1)}, f32[512,256]{1,0:T(8,128)S(1)}, f32[512,256]{1,0:T(8,128)S(1)}, bf16[512,256]{1,0:T(8,128)(2,1)S(1)}) custom-call(s32[1]{0:T(128)} %bitcast.1.refs_0_.where, s32[1]{0:T(128)} %constant.16.clone.1.refs_1_, s32[1]{0:T(128)} %bitcast.2.refs_2_, s32[1]{0:T(128)} %bitcast.3.refs_3_, ...), custom_call_target="tpu_custom_call" | custom-call | flops 1000 | bytes 1000 | tf_op jit(solution)/shard_map/pallas_call | solution.py:324
  32.0 1.5 %collective-permute-start.4 = (bf16[512,256]{1,0:T(8,128)(2,1)S(1)}, bf16[512,256]{1,0:T(8,128)(2,1)S(1)}, u32[]{:S(2)}, u32[]{:S(2)}) collective-permute-start(bf16[512,256]{1,0:T(8,128)(2,1)S(1)} %get-tuple-element.94), channel_id=1, source_target_pairs={{0,16},{1,2},{2,1},{3,4},{4,3},{5,6},{6,5},{7,8},{8,7},{9,10},{10,... | collective-permute-start | bytes 786440 | tf_op jit(solution)/shard_map/ppermute | solution.py:426
  33.5 0.4 shard_map.99
  33.9 0.0 copy-start.1
  33.9 0.0 copy-start.2
  34.0 0.0 copy-start.3
  34.0 0.8 %collective-permute-done.5.refs_8_ = bf16[512,256]{1,0:T(8,128)(2,1)S(1)} collective-permute-done((bf16[512,256]{1,0:T(8,128)(2,1)S(1)}, bf16[512,256]{1,0:T(8,128)(2,1)S(1)}, u32[]{:S(2)}, u32[]{:S(2)}) %collective-permute-start.5) | collective-permute-done | bytes 262176 | tf_op jit(solution)/shard_map/ppermute | solution.py:461
  34.7 0.7 %shard_map.100 = (bf16[256,256]{1,0:T(8,128)(2,1)S(1)}, bf16[256,256]{1,0:T(8,128)(2,1)S(1)}) custom-call(s32[1]{0:T(128)} %bitcast.1.refs_0_.where, s32[1]{0:T(128)} %constant.16.clone.1.refs_1_, s32[1]{0:T(128)} %bitcast.2.refs_2_, s32[1]{0:T(128)} %bitcast.3.refs_3_, bf16[2,512,512]{2,1,0:T(8,128)(2,1)S(1)} %get-tuple-element.56.refs_8_.refs_7_.refs_4_, ...), custom_call_target="tpu_custom_call" | custom-call | flops 1000 | bytes 1000 | tf_op jit(solution)/shard_map/pallas_call | solution.py:324
  35.4 0.4 collective-permute-start.6
  35.9 0.1 collective-permute-start.7
  36.0 0.0 copy-done.1
  36.0 0.0 copy-done.2
  36.0 0.0 copy-done.3
  36.0 0.7 %shard_map.86.refs_0_.scales = f32[256,8]{1,0:T(8,128)S(1)} custom-call(s32[1]{0:T(128)} %bitcast.1.refs_0_.where, s32[1]{0:T(128)} %constant.16.clone.1.refs_1_, s32[1]{0:T(128)} %bitcast.2.refs_2_, s32[1]{0:T(128)} %bitcast.3.refs_3_, f32[2,128]{1,0:T(2,128)S(1)} %copy-done.1, s32[2,4]{1,0:T(2,128)S(1)} %copy-done.2, f32[2,4]{1,0:T(2,128)S(1)} %copy-done.3), custom_call_target="tpu_custom_call" | custom-call | flops 1000 | bytes 1000 | tf_op jit(solution)/shard_map/pallas_call | solution.py:324
  36.7 0.7 %shard_map.101 = (f32[2,512,512]{2,1,0:T(8,128)S(1)}, f32[2,512,256]{2,1,0:T(8,128)S(1)}) custom-call(f32[256,8]{1,0:T(8,128)S(1)} %shard_map.86.refs_0_.scales, bf16[256,256]{1,0:T(8,128)(2,1)S(1)} %get-tuple-element.97.refs_1_, bf16[256,256]{1,0:T(8,128)(2,1)S(1)} %get-tuple-element.98.refs_2_), custom_call_target="tpu_custom_call" | custom-call | flops 1000 | bytes 1000 | tf_op jit(solution)/shard_map/pallas_call | solution.py:324
  37.4 0.0 collective-permute-done.6.rest_0_
  37.4 0.0 collective-permute-done.7.rest_1_
  37.4 1.8 %shard_map.102 = (bf16[2,2,512,512]{3,2,1,0:T(8,128)(2,1)}, bf16[2,2,512,512]{3,2,1,0:T(8,128)(2,1)}, f32[8,128]{1,0:T(8,128)S(1)}) custom-call(s32[1]{0:T(128)} %bitcast.1.refs_0_.where, f32[256,8]{1,0:T(8,128)S(1)} %shard_map.86.refs_0_.scales, f32[2,512,512]{2,1,0:T(8,128)S(1)} %get-tuple-element.99.tops, f32[2,512,256]{2,1,0:T(8,128)S(1)} %get-tuple-element.100.lows, ...), custom_call_target="tpu_custom_call" | custom-call | flops 1000 | bytes 1000 | tf_op jit(solution)/shard_map/pallas_call | solution.py:349
  39.3 2.4 %collective-permute-done.4.refs_8_ = bf16[512,256]{1,0:T(8,128)(2,1)S(1)} collective-permute-done((bf16[512,256]{1,0:T(8,128)(2,1)S(1)}, bf16[512,256]{1,0:T(8,128)(2,1)S(1)}, u32[]{:S(2)}, u32[]{:S(2)}) %collective-permute-start.4) | collective-permute-done | bytes 262176 | tf_op jit(solution)/shard_map/ppermute | solution.py:426
  41.6 0.5 shard_map.103.refs_1_
  42.1 1.0 %collective-permute-start.8 = (bf16[512,256]{1,0:T(8,128)(2,1)S(1)}, bf16[512,256]{1,0:T(8,128)(2,1)S(1)}, u32[]{:S(2)}, u32[]{:S(2)}) collective-permute-start(bf16[512,256]{1,0:T(8,128)(2,1)S(1)} %shard_map.103.refs_1_), channel_id=1, source_target_pairs={{0,16},{1,17},{2,18},{3,19},{4,20},{5,21},{6,22},{7,23},{8,24},{9,... | collective-permute-start | bytes 786440 | tf_op jit(solution)/shard_map/ppermute | solution.py:454
  43.1 0.7 %shard_map.104 = (f32[2,512,512]{2,1,0:T(8,128)S(1)}, f32[2,512,256]{2,1,0:T(8,128)S(1)}) custom-call(f32[256,8]{1,0:T(8,128)S(1)} %shard_map.86.refs_0_.scales, bf16[512,256]{1,0:T(8,128)(2,1)S(1)} %shard_map.103.refs_1_), custom_call_target="tpu_custom_call" | custom-call | flops 1000 | bytes 1000 | tf_op jit(solution)/shard_map/pallas_call | solution.py:324
  43.9 0.4 collective-permute-done.8.rest_0_
  44.3 1.8 %shard_map.105 = (bf16[2,2,512,512]{3,2,1,0:T(8,128)(2,1)}, bf16[2,2,512,512]{3,2,1,0:T(8,128)(2,1)}) custom-call(s32[1]{0:T(128)} %bitcast.where, f32[256,8]{1,0:T(8,128)S(1)} %shard_map.86.refs_0_.scales, f32[2,512,512]{2,1,0:T(8,128)S(1)} %get-tuple-element.102.tops, ...), custom_call_target="tpu_custom_call", output_to_operand_aliasing={{0}: (5, {}), {1}: (6, {})} | custom-call | flops 1000 | bytes 1000 | tf_op jit(solution)/shard_map/pallas_call | solution.py:349
  (3 shorter events, 0.0 us)
Async XLA Ops:
  3.0 8.7 %collective-permute-start = (bf16[512,256]{1,0:T(8,128)(2,1)S(1)}, bf16[512,256]{1,0:T(8,128)(2,1)S(1)}, u32[]{:S(2)}, u32[]{:S(2)}) collective-permute-start(bf16[512,256]{1,0:T(8,128)(2,1)S(1)} %get-tuple-element.70), channel_id=1, source_target_pairs={{0,1},{1,0},{2,3},{3,2},{4,5},{5,4},{6,7},{7,6},{8,9},{9,8},{10,11... | collective-permute-start | bytes 786440 | tf_op jit(solution)/shard_map/ppermute | solution.py:408
  3.8 3.6 %copy-start = (f32[1,2,2,512]{3,2,1,0:T(2,128)S(1)}, f32[1,2,2,512]{3,2,1,0:T(2,128)}, u32[]{:S(2)}) copy-start(f32[1,2,2,512]{3,2,1,0:T(2,128)} %param.10) | copy-start | bytes 24580
  9.1 9.7 %collective-permute-start.1 = (bf16[512,256]{1,0:T(8,128)(2,1)S(1)}, bf16[512,256]{1,0:T(8,128)(2,1)S(1)}, u32[]{:S(2)}, u32[]{:S(2)}) collective-permute-start(bf16[512,256]{1,0:T(8,128)(2,1)S(1)} %get-tuple-element.73), channel_id=1, source_target_pairs={{0,16},{1,2},{2,1},{3,4},{4,3},{5,6},{6,5},{7,8},{8,7},{9,10},{10,... | collective-permute-start | bytes 786440 | tf_op jit(solution)/shard_map/ppermute | solution.py:426
  13.4 10.4 %collective-permute-start.2 = (bf16[512,256]{1,0:T(8,128)(2,1)S(1)}, bf16[512,256]{1,0:T(8,128)(2,1)S(1)}, u32[]{:S(2)}, u32[]{:S(2)}) collective-permute-start(bf16[512,256]{1,0:T(8,128)(2,1)S(1)} %get-tuple-element.82), channel_id=1, source_target_pairs={{0,1},{1,0},{2,3},{3,2},{4,5},{5,4},{6,7},{7,6},{8,9},{9,8},{10,11... | collective-permute-start | bytes 786440 | tf_op jit(solution)/shard_map/ppermute | solution.py:461
  21.1 9.1 %collective-permute-start.3 = (bf16[512,256]{1,0:T(8,128)(2,1)S(1)}, bf16[512,256]{1,0:T(8,128)(2,1)S(1)}, u32[]{:S(2)}, u32[]{:S(2)}) collective-permute-start(bf16[512,256]{1,0:T(8,128)(2,1)S(1)} %get-tuple-element.85), channel_id=1, source_target_pairs={{0,16},{1,2},{2,1},{3,4},{4,3},{5,6},{6,5},{7,8},{8,7},{9,10},{10,... | collective-permute-start | bytes 786440 | tf_op jit(solution)/shard_map/ppermute | solution.py:426
  25.6 9.2 %collective-permute-start.5 = (bf16[512,256]{1,0:T(8,128)(2,1)S(1)}, bf16[512,256]{1,0:T(8,128)(2,1)S(1)}, u32[]{:S(2)}, u32[]{:S(2)}) collective-permute-start(bf16[512,256]{1,0:T(8,128)(2,1)S(1)} %get-tuple-element.96), channel_id=1, source_target_pairs={{0,1},{1,0},{2,3},{3,2},{4,5},{5,4},{6,7},{7,6},{8,9},{9,8},{10,11... | collective-permute-start | bytes 786440 | tf_op jit(solution)/shard_map/ppermute | solution.py:461
  32.0 9.6 %collective-permute-start.4 = (bf16[512,256]{1,0:T(8,128)(2,1)S(1)}, bf16[512,256]{1,0:T(8,128)(2,1)S(1)}, u32[]{:S(2)}, u32[]{:S(2)}) collective-permute-start(bf16[512,256]{1,0:T(8,128)(2,1)S(1)} %get-tuple-element.94), channel_id=1, source_target_pairs={{0,16},{1,2},{2,1},{3,4},{4,3},{5,6},{6,5},{7,8},{8,7},{9,10},{10,... | collective-permute-start | bytes 786440 | tf_op jit(solution)/shard_map/ppermute | solution.py:426
  33.9 2.1 %copy-start.1 = (f32[2,128]{1,0:T(2,128)S(1)}, f32[2,128]{1,0:T(2,128)}, u32[]{:S(2)}) copy-start(f32[2,128]{1,0:T(2,128)} %refs_4_.1) | copy-start | bytes 3076
  33.9 2.0 %copy-start.2 = (s32[2,4]{1,0:T(2,128)S(1)}, s32[2,4]{1,0:T(2,128)}, u32[]{:S(2)}) copy-start(s32[2,4]{1,0:T(2,128)} %refs_5_.3) | copy-start | bytes 100
  34.0 2.0 %copy-start.3 = (f32[2,4]{1,0:T(2,128)S(1)}, f32[2,4]{1,0:T(2,128)}, u32[]{:S(2)}) copy-start(f32[2,4]{1,0:T(2,128)} %refs_6_.1) | copy-start | bytes 100
  35.4 2.0 %collective-permute-start.6 = (bf16[256,256]{1,0:T(8,128)(2,1)S(1)}, bf16[256,256]{1,0:T(8,128)(2,1)S(1)}, u32[]{:S(2)}, u32[]{:S(2)}) collective-permute-start(bf16[256,256]{1,0:T(8,128)(2,1)S(1)} %get-tuple-element.97.refs_1_), channel_id=1, source_target_pairs={{0,16},{1,17},{2,18},{3,19},{4,20},{5,21},{6,22},{7,23},{8,24},{9,... | collective-permute-start | bytes 393224 | tf_op jit(solution)/shard_map/ppermute | solution.py:454
  35.9 1.6 %collective-permute-start.7 = (bf16[256,256]{1,0:T(8,128)(2,1)S(1)}, bf16[256,256]{1,0:T(8,128)(2,1)S(1)}, u32[]{:S(2)}, u32[]{:S(2)}) collective-permute-start(bf16[256,256]{1,0:T(8,128)(2,1)S(1)} %get-tuple-element.98.refs_2_), channel_id=1, source_target_pairs={{0,16},{1,17},{2,18},{3,19},{4,20},{5,21},{6,22},{7,23},{8,24},{9,... | collective-permute-start | bytes 393224 | tf_op jit(solution)/shard_map/ppermute | solution.py:454
  42.1 2.2 %collective-permute-start.8 = (bf16[512,256]{1,0:T(8,128)(2,1)S(1)}, bf16[512,256]{1,0:T(8,128)(2,1)S(1)}, u32[]{:S(2)}, u32[]{:S(2)}) collective-permute-start(bf16[512,256]{1,0:T(8,128)(2,1)S(1)} %shard_map.103.refs_1_), channel_id=1, source_target_pairs={{0,16},{1,17},{2,18},{3,19},{4,20},{5,21},{6,22},{7,23},{8,24},{9,... | collective-permute-start | bytes 786440 | tf_op jit(solution)/shard_map/ppermute | solution.py:454

commit v6 on v5

--- a/solution.py
+++ b/solution.py
@@ -54,9 +54,14 @@
         load(source.at[slab], drive, sems.at[0]),
         load(precond.at[slab, 0], own.at[0], sems.at[1]),
         load(precond.at[slab, 1], own.at[1], sems.at[2]),
-        load(coupling.at[1, 0], link.at[0], sems.at[3]),
-        load(coupling.at[1, 1], link.at[1], sems.at[4]),
     ]
+    links = [pltpu.make_async_copy(coupling.at[1, at], link.at[at], sems.at[3 + at]) for at in range(2)]
+
+    @pl.when(slab == 1)
+    def _():
+        for copy in links:
+            copy.start()
+
     copies[0].wait()
     pair = jnp.concatenate([drive[0], drive[1]], axis=1).astype(BF16)
     copies[1].wait()
@@ -65,31 +70,36 @@
     partial = partial + jnp.dot(own[1], times_i(pair, 1), preferred_element_type=F32)
     fresh = partial.astype(BF16)
     states[...] = fresh
-    copies[3].wait()
 
     @pl.when(slab == 0)
     def _():
         send[...] = fresh
-        copies[4].wait()
-
-    @pl.when(slab == 1)
-    def _():
+
+    @pl.when(slab == 1)
+    def _():
+        links[0].wait()
         handed = transposed_dot(link[0], fresh)
-        copies[4].wait()
+        links[1].wait()
         send[...] = (handed + transposed_dot(link[1], times_i(fresh, -1))).astype(BF16)
 
 
 def trail_kernel(
-    where, precond, coupling, source, link, lead, lead_states,
-    states, send, own, inner, drive, chain, term, sems,
+    where, precond, coupling, source, given, lead, lead_states,
+    states, send, own, inner, drive, chain, term, link, sems,
 ):
     slab = 1 - where[0]
     copies = [
         load(source.at[slab], drive, sems.at[0]),
         load(precond.at[slab, 0], own.at[0], sems.at[1]),
         load(precond.at[slab, 1], own.at[1], sems.at[2]),
-        load(coupling.at[0], inner, sems.at[3]),
     ]
+    missing = pltpu.make_async_copy(coupling.at[1], link, sems.at[4])
+
+    @pl.when(slab == 1)
+    def _():
+        missing.start()
+
+    copies.append(load(coupling.at[0], inner, sems.at[3]))
     copies[0].wait()
     pair = jnp.concatenate([drive[0], drive[1]], axis=1).astype(BF16)
     copies[1].wait()
@@ -98,6 +108,11 @@
     partial = partial + jnp.dot(own[1], times_i(pair, 1), preferred_element_type=F32)
     fresh = partial.astype(BF16)
     states[...] = fresh
+
+    @pl.when(slab == 1)
+    def _():
+        missing.wait()
+
     send_fresh(slab, link, fresh, send)
 
     def write_chain(matrix):
@@ -406,12 +421,13 @@
         [pltpu.SemaphoreType.DMA((5,))],
     )
     arrived[0] = lax.ppermute(send, AXES, pairings[0])
-    states[1], send, owns[1], within, drives[1], chain, term = call(
+    states[1], send, owns[1], within, drives[1], chain, term, link = call(
         trail_kernel,
-        [pair, pair, matrix, matrix, drive, matrix, total],
+        [pair, pair, matrix, matrix, drive, matrix, total, matrix],
         [SCALAR, FAR, FAR, FAR] + [NEAR] * 3,
         (where, precond, coupling, source, link, owns[0], states[0]),
-        [pltpu.SemaphoreType.DMA((4,))],
+        [pltpu.SemaphoreType.DMA((5,))],
+        aliases={4: 7},
     )
     for sweep in range(1, SWEEPS):
         first, last = sweep == 1, sweep == SWEEPS - 1

time: 46.4 us -> 46.4 us (level)
  no operation moved by 1% of the time
where the time goes in v6:
time: 46.4 us; the launch traced here: 46.3 us
  Pallas kernels  22.5 us (48%)
  waiting for transfers between devices  13.4 us (29%)
  starting transfers between devices  9.4 us (20%)
  between operations  1.01 us (2%)
    pallas_call x18, Pallas kernels, call(): pl.pallas_call(unpacked, out_shape=outs, in_specs=specs, out_specs=[NEAR]...  18.9 us
    ppermute x3, waiting for transfers between devices, body(): arrived[1] = lax.ppermute(send, AXES, pairings[1])  12.2 us
    ppermute x3, starting transfers between devices, body(): arrived[1] = lax.ppermute(send, AXES, pairings[1])  6.88 us
    pallas_call x2, Pallas kernels, self_blocks(): pl.pallas_call(functools.partial(sigma_kernel, pieces, len(previous)), ou...  3.61 us
    ppermute x3, starting transfers between devices, body(): others = [lax.ppermute(result, AXES, swap) for result in results]  1.59 us
  transfers between devices with their start and end apart: 9, of which 5 were waited for; matrix products, arithmetic and copies ran while one was open for 0% of the time, Pallas kernels for 39%

profile of v6, /device:TPU:25, one launch (start us, length us, event | category | flops | bytes accessed | tf_op | source)
XLA Modules:
  0.0 46.3 jit_solution(5696711189091336192)
XLA Ops:
  0.6 2.4 %shard_map.87 = (bf16[512,256]{1,0:T(8,128)(2,1)S(1)}, bf16[512,256]{1,0:T(8,128)(2,1)S(1)}, bf16[2,512,512]{2,1,0:T(8,128)(2,1)S(1)}, bf16[2,512,512]{2,1,0:T(8,128)(2,1)S(1)}, f32[2,512,128]{2,1,0:T(8,128)S(1)}) custom-call(s32[1]{0:T(128)} %bitcast.1.refs_0_.where, s32[1]{0:T(128)} %constant.16.clone.1.refs_1_, s32[1]{0:T(128)} %bitcast.2.refs_2_, ...), custom_call_target="tpu_custom_call" | custom-call | flops 1000 | bytes 1000 | tf_op jit(solution)/shard_map/pallas_call | solution.py:339
  3.0 0.8 %collective-permute-start = (bf16[512,256]{1,0:T(8,128)(2,1)S(1)}, bf16[512,256]{1,0:T(8,128)(2,1)S(1)}, u32[]{:S(2)}, u32[]{:S(2)}) collective-permute-start(bf16[512,256]{1,0:T(8,128)(2,1)S(1)} %get-tuple-element.72), channel_id=1, source_target_pairs={{0,1},{1,0},{2,3},{3,2},{4,5},{5,4},{6,7},{7,6},{8,9},{9,8},{10,11... | collective-permute-start | bytes 786440 | tf_op jit(solution)/shard_map/ppermute | solution.py:423
  3.8 0.0 copy-start
  3.8 3.6 %shard_map.88 = (bf16[512,256]{1,0:T(8,128)(2,1)S(1)}, bf16[512,256]{1,0:T(8,128)(2,1)S(1)}, bf16[2,512,512]{2,1,0:T(8,128)(2,1)S(1)}, bf16[2,512,512]{2,1,0:T(8...) custom-call(s32[1]{0:T(128)} %bitcast.1.refs_0_.where, ...), custom_call_target="tpu_custom_call", output_to_operand_aliasing={{7}: (7, {})} | custom-call | flops 1000 | bytes 1000 | tf_op jit(solution)/shard_map/pallas_call | solution.py:339
  7.4 0.0 copy-done
  7.4 1.8 %shard_map.89 = (f32[512,256]{1,0:T(8,128)S(1)}, f32[512,256]{1,0:T(8,128)S(1)}, f32[512,256]{1,0:T(8,128)S(1)}, bf16[512,256]{1,0:T(8,128)(2,1)S(1)}) custom-call(s32[1]{0:T(128)} %bitcast.1.refs_0_.where, s32[1]{0:T(128)} %constant.16.clone.1.refs_1_, s32[1]{0:T(128)} %bitcast.2.refs_2_, s32[1]{0:T(128)} %bitcast.3.refs_3_, ...), custom_call_target="tpu_custom_call" | custom-call | flops 1000 | bytes 1000 | tf_op jit(solution)/shard_map/pallas_call | solution.py:339
  9.1 2.5 %collective-permute-start.1 = (bf16[512,256]{1,0:T(8,128)(2,1)S(1)}, bf16[512,256]{1,0:T(8,128)(2,1)S(1)}, u32[]{:S(2)}, u32[]{:S(2)}) collective-permute-start(bf16[512,256]{1,0:T(8,128)(2,1)S(1)} %get-tuple-element.75), channel_id=1, source_target_pairs={{0,16},{1,2},{2,1},{3,4},{4,3},{5,6},{6,5},{7,8},{8,7},{9,10},{10,... | collective-permute-start | bytes 786440 | tf_op jit(solution)/shard_map/ppermute | solution.py:442
  11.7 0.0 collective-permute-done.refs_8_
  11.7 1.7 %shard_map.91 = (bf16[512,256]{1,0:T(8,128)(2,1)S(1)}, bf16[512,256]{1,0:T(8,128)(2,1)S(1)}, f32[512,256]{1,0:T(8,128)S(1)}) custom-call(s32[1]{0:T(128)} %bitcast.1.refs_0_.where, s32[1]{0:T(128)} %constant.16.clone.1.refs_1_, s32[1]{0:T(128)} %bitcast.2.refs_2_, s32[1]{0:T(128)} %bitcast.3.refs_3_, ...), custom_call_target="tpu_custom_call" | custom-call | flops 1000 | bytes 1000 | tf_op jit(solution)/shard_map/pallas_call | solution.py:339
  13.4 0.1 collective-permute-start.2
  13.5 5.3 %collective-permute-done.1.refs_8_ = bf16[512,256]{1,0:T(8,128)(2,1)S(1)} collective-permute-done((bf16[512,256]{1,0:T(8,128)(2,1)S(1)}, bf16[512,256]{1,0:T(8,128)(2,1)S(1)}, u32[]{:S(2)}, u32[]{:S(2)}) %collective-permute-start.1) | collective-permute-done | bytes 262176 | tf_op jit(solution)/shard_map/ppermute | solution.py:442
  18.8 0.4 shard_map.93
  19.3 1.8 %shard_map.94 = (f32[512,256]{1,0:T(8,128)S(1)}, f32[512,256]{1,0:T(8,128)S(1)}, f32[512,256]{1,0:T(8,128)S(1)}, bf16[512,256]{1,0:T(8,128)(2,1)S(1)}) custom-call(s32[1]{0:T(128)} %bitcast.1.refs_0_.where, s32[1]{0:T(128)} %constant.16.clone.1.refs_1_, s32[1]{0:T(128)} %bitcast.2.refs_2_, s32[1]{0:T(128)} %bitcast.3.refs_3_, ...), custom_call_target="tpu_custom_call" | custom-call | flops 1000 | bytes 1000 | tf_op jit(solution)/shard_map/pallas_call | solution.py:339
  21.1 2.8 %collective-permute-start.3 = (bf16[512,256]{1,0:T(8,128)(2,1)S(1)}, bf16[512,256]{1,0:T(8,128)(2,1)S(1)}, u32[]{:S(2)}, u32[]{:S(2)}) collective-permute-start(bf16[512,256]{1,0:T(8,128)(2,1)S(1)} %get-tuple-element.87), channel_id=1, source_target_pairs={{0,16},{1,2},{2,1},{3,4},{4,3},{5,6},{6,5},{7,8},{8,7},{9,10},{10,... | collective-permute-start | bytes 786440 | tf_op jit(solution)/shard_map/ppermute | solution.py:442
  23.9 0.0 collective-permute-done.2.refs_8_
  23.9 1.7 %shard_map.96 = (bf16[512,256]{1,0:T(8,128)(2,1)S(1)}, bf16[512,256]{1,0:T(8,128)(2,1)S(1)}, f32[512,256]{1,0:T(8,128)S(1)}) custom-call(s32[1]{0:T(128)} %bitcast.1.refs_0_.where, s32[1]{0:T(128)} %constant.16.clone.1.refs_1_, s32[1]{0:T(128)} %bitcast.2.refs_2_, s32[1]{0:T(128)} %bitcast.3.refs_3_, ...), custom_call_target="tpu_custom_call" | custom-call | flops 1000 | bytes 1000 | tf_op jit(solution)/shard_map/pallas_call | solution.py:339
  25.6 0.1 collective-permute-start.5
  25.7 4.5 %collective-permute-done.3.refs_8_ = bf16[512,256]{1,0:T(8,128)(2,1)S(1)} collective-permute-done((bf16[512,256]{1,0:T(8,128)(2,1)S(1)}, bf16[512,256]{1,0:T(8,128)(2,1)S(1)}, u32[]{:S(2)}, u32[]{:S(2)}) %collective-permute-start.3) | collective-permute-done | bytes 262176 | tf_op jit(solution)/shard_map/ppermute | solution.py:442
  30.2 0.4 shard_map.97
  30.6 1.4 %shard_map.98 = (f32[512,256]{1,0:T(8,128)S(1)}, f32[512,256]{1,0:T(8,128)S(1)}, f32[512,256]{1,0:T(8,128)S(1)}, bf16[512,256]{1,0:T(8,128)(2,1)S(1)}) custom-call(s32[1]{0:T(128)} %bitcast.1.refs_0_.where, s32[1]{0:T(128)} %constant.16.clone.1.refs_1_, s32[1]{0:T(128)} %bitcast.2.refs_2_, s32[1]{0:T(128)} %bitcast.3.refs_3_, ...), custom_call_target="tpu_custom_call" | custom-call | flops 1000 | bytes 1000 | tf_op jit(solution)/shard_map/pallas_call | solution.py:339
  32.0 1.5 %collective-permute-start.4 = (bf16[512,256]{1,0:T(8,128)(2,1)S(1)}, bf16[512,256]{1,0:T(8,128)(2,1)S(1)}, u32[]{:S(2)}, u32[]{:S(2)}) collective-permute-start(bf16[512,256]{1,0:T(8,128)(2,1)S(1)} %get-tuple-element.96), channel_id=1, source_target_pairs={{0,16},{1,2},{2,1},{3,4},{4,3},{5,6},{6,5},{7,8},{8,7},{9,10},{10,... | collective-permute-start | bytes 786440 | tf_op jit(solution)/shard_map/ppermute | solution.py:442
  33.6 0.4 shard_map.99
  34.0 0.0 copy-start.1
  34.0 0.0 copy-start.2
  34.0 0.0 copy-start.3
  34.0 0.8 %collective-permute-done.5.refs_8_ = bf16[512,256]{1,0:T(8,128)(2,1)S(1)} collective-permute-done((bf16[512,256]{1,0:T(8,128)(2,1)S(1)}, bf16[512,256]{1,0:T(8,128)(2,1)S(1)}, u32[]{:S(2)}, u32[]{:S(2)}) %collective-permute-start.5) | collective-permute-done | bytes 262176 | tf_op jit(solution)/shard_map/ppermute | solution.py:477
  34.7 0.7 %shard_map.100 = (bf16[256,256]{1,0:T(8,128)(2,1)S(1)}, bf16[256,256]{1,0:T(8,128)(2,1)S(1)}) custom-call(s32[1]{0:T(128)} %bitcast.1.refs_0_.where, s32[1]{0:T(128)} %constant.16.clone.1.refs_1_, s32[1]{0:T(128)} %bitcast.2.refs_2_, s32[1]{0:T(128)} %bitcast.3.refs_3_, bf16[2,512,512]{2,1,0:T(8,128)(2,1)S(1)} %get-tuple-element.57.refs_8_.refs_7_.refs_4_, ...), custom_call_target="tpu_custom_call" | custom-call | flops 1000 | bytes 1000 | tf_op jit(solution)/shard_map/pallas_call | solution.py:339
  35.4 0.4 collective-permute-start.6
  35.9 0.1 collective-permute-start.7
  36.0 0.0 copy-done.1
  36.0 0.0 copy-done.2
  36.0 0.0 copy-done.3
  36.0 0.7 %shard_map.86.refs_0_.scales = f32[256,8]{1,0:T(8,128)S(1)} custom-call(s32[1]{0:T(128)} %bitcast.1.refs_0_.where, s32[1]{0:T(128)} %constant.16.clone.1.refs_1_, s32[1]{0:T(128)} %bitcast.2.refs_2_, s32[1]{0:T(128)} %bitcast.3.refs_3_, f32[2,128]{1,0:T(2,128)S(1)} %copy-done.1, s32[2,4]{1,0:T(2,128)S(1)} %copy-done.2, f32[2,4]{1,0:T(2,128)S(1)} %copy-done.3), custom_call_target="tpu_custom_call" | custom-call | flops 1000 | bytes 1000 | tf_op jit(solution)/shard_map/pallas_call | solution.py:339
  36.7 0.7 %shard_map.101 = (f32[2,512,512]{2,1,0:T(8,128)S(1)}, f32[2,512,256]{2,1,0:T(8,128)S(1)}) custom-call(f32[256,8]{1,0:T(8,128)S(1)} %shard_map.86.refs_0_.scales, bf16[256,256]{1,0:T(8,128)(2,1)S(1)} %get-tuple-element.99.refs_1_, bf16[256,256]{1,0:T(8,128)(2,1)S(1)} %get-tuple-element.100.refs_2_), custom_call_target="tpu_custom_call" | custom-call | flops 1000 | bytes 1000 | tf_op jit(solution)/shard_map/pallas_call | solution.py:339
  37.4 0.0 collective-permute-done.6.rest_0_
  37.4 0.0 collective-permute-done.7.rest_1_
  37.4 1.8 %shard_map.102 = (bf16[2,2,512,512]{3,2,1,0:T(8,128)(2,1)}, bf16[2,2,512,512]{3,2,1,0:T(8,128)(2,1)}, f32[8,128]{1,0:T(8,128)S(1)}) custom-call(s32[1]{0:T(128)} %bitcast.1.refs_0_.where, f32[256,8]{1,0:T(8,128)S(1)} %shard_map.86.refs_0_.scales, f32[2,512,512]{2,1,0:T(8,128)S(1)} %get-tuple-element.101.tops, f32[2,512,256]{2,1,0:T(8,128)S(1)} %get-tuple-element.102.lows, ...), custom_call_target="tpu_custom_call" | custom-call | flops 1000 | bytes 1000 | tf_op jit(solution)/shard_map/pallas_call | solution.py:364
  39.3 2.4 %collective-permute-done.4.refs_8_ = bf16[512,256]{1,0:T(8,128)(2,1)S(1)} collective-permute-done((bf16[512,256]{1,0:T(8,128)(2,1)S(1)}, bf16[512,256]{1,0:T(8,128)(2,1)S(1)}, u32[]{:S(2)}, u32[]{:S(2)}) %collective-permute-start.4) | collective-permute-done | bytes 262176 | tf_op jit(solution)/shard_map/ppermute | solution.py:442
  41.6 0.5 shard_map.103.refs_1_
  42.1 1.0 %collective-permute-start.8 = (bf16[512,256]{1,0:T(8,128)(2,1)S(1)}, bf16[512,256]{1,0:T(8,128)(2,1)S(1)}, u32[]{:S(2)}, u32[]{:S(2)}) collective-permute-start(bf16[512,256]{1,0:T(8,128)(2,1)S(1)} %shard_map.103.refs_1_), channel_id=1, source_target_pairs={{0,16},{1,17},{2,18},{3,19},{4,20},{5,21},{6,22},{7,23},{8,24},{9,... | collective-permute-start | bytes 786440 | tf_op jit(solution)/shard_map/ppermute | solution.py:470
  43.1 0.7 %shard_map.104 = (f32[2,512,512]{2,1,0:T(8,128)S(1)}, f32[2,512,256]{2,1,0:T(8,128)S(1)}) custom-call(f32[256,8]{1,0:T(8,128)S(1)} %shard_map.86.refs_0_.scales, bf16[512,256]{1,0:T(8,128)(2,1)S(1)} %shard_map.103.refs_1_), custom_call_target="tpu_custom_call" | custom-call | flops 1000 | bytes 1000 | tf_op jit(solution)/shard_map/pallas_call | solution.py:339
  43.9 0.4 collective-permute-done.8.rest_0_
  44.3 1.8 %shard_map.105 = (bf16[2,2,512,512]{3,2,1,0:T(8,128)(2,1)}, bf16[2,2,512,512]{3,2,1,0:T(8,128)(2,1)}) custom-call(s32[1]{0:T(128)} %bitcast.where, f32[256,8]{1,0:T(8,128)S(1)} %shard_map.86.refs_0_.scales, f32[2,512,512]{2,1,0:T(8,128)S(1)} %get-tuple-element.104.tops, ...), custom_call_target="tpu_custom_call", output_to_operand_aliasing={{0}: (5, {}), {1}: (6, {})} | custom-call | flops 1000 | bytes 1000 | tf_op jit(solution)/shard_map/pallas_call | solution.py:364
  (3 shorter events, 0.0 us)
Async XLA Ops:
  3.0 8.7 %collective-permute-start = (bf16[512,256]{1,0:T(8,128)(2,1)S(1)}, bf16[512,256]{1,0:T(8,128)(2,1)S(1)}, u32[]{:S(2)}, u32[]{:S(2)}) collective-permute-start(bf16[512,256]{1,0:T(8,128)(2,1)S(1)} %get-tuple-element.72), channel_id=1, source_target_pairs={{0,1},{1,0},{2,3},{3,2},{4,5},{5,4},{6,7},{7,6},{8,9},{9,8},{10,11... | collective-permute-start | bytes 786440 | tf_op jit(solution)/shard_map/ppermute | solution.py:423
  3.8 3.6 %copy-start = (f32[1,2,2,512]{3,2,1,0:T(2,128)S(1)}, f32[1,2,2,512]{3,2,1,0:T(2,128)}, u32[]{:S(2)}) copy-start(f32[1,2,2,512]{3,2,1,0:T(2,128)} %param.10) | copy-start | bytes 24580
  9.1 9.7 %collective-permute-start.1 = (bf16[512,256]{1,0:T(8,128)(2,1)S(1)}, bf16[512,256]{1,0:T(8,128)(2,1)S(1)}, u32[]{:S(2)}, u32[]{:S(2)}) collective-permute-start(bf16[512,256]{1,0:T(8,128)(2,1)S(1)} %get-tuple-element.75), channel_id=1, source_target_pairs={{0,16},{1,2},{2,1},{3,4},{4,3},{5,6},{6,5},{7,8},{8,7},{9,10},{10,... | collective-permute-start | bytes 786440 | tf_op jit(solution)/shard_map/ppermute | solution.py:442
  13.4 10.5 %collective-permute-start.2 = (bf16[512,256]{1,0:T(8,128)(2,1)S(1)}, bf16[512,256]{1,0:T(8,128)(2,1)S(1)}, u32[]{:S(2)}, u32[]{:S(2)}) collective-permute-start(bf16[512,256]{1,0:T(8,128)(2,1)S(1)} %get-tuple-element.84), channel_id=1, source_target_pairs={{0,1},{1,0},{2,3},{3,2},{4,5},{5,4},{6,7},{7,6},{8,9},{9,8},{10,11... | collective-permute-start | bytes 786440 | tf_op jit(solution)/shard_map/ppermute | solution.py:477
  21.1 9.1 %collective-permute-start.3 = (bf16[512,256]{1,0:T(8,128)(2,1)S(1)}, bf16[512,256]{1,0:T(8,128)(2,1)S(1)}, u32[]{:S(2)}, u32[]{:S(2)}) collective-permute-start(bf16[512,256]{1,0:T(8,128)(2,1)S(1)} %get-tuple-element.87), channel_id=1, source_target_pairs={{0,16},{1,2},{2,1},{3,4},{4,3},{5,6},{6,5},{7,8},{8,7},{9,10},{10,... | collective-permute-start | bytes 786440 | tf_op jit(solution)/shard_map/ppermute | solution.py:442
  25.6 9.1 %collective-permute-start.5 = (bf16[512,256]{1,0:T(8,128)(2,1)S(1)}, bf16[512,256]{1,0:T(8,128)(2,1)S(1)}, u32[]{:S(2)}, u32[]{:S(2)}) collective-permute-start(bf16[512,256]{1,0:T(8,128)(2,1)S(1)} %get-tuple-element.98), channel_id=1, source_target_pairs={{0,1},{1,0},{2,3},{3,2},{4,5},{5,4},{6,7},{7,6},{8,9},{9,8},{10,11... | collective-permute-start | bytes 786440 | tf_op jit(solution)/shard_map/ppermute | solution.py:477
  32.0 9.6 %collective-permute-start.4 = (bf16[512,256]{1,0:T(8,128)(2,1)S(1)}, bf16[512,256]{1,0:T(8,128)(2,1)S(1)}, u32[]{:S(2)}, u32[]{:S(2)}) collective-permute-start(bf16[512,256]{1,0:T(8,128)(2,1)S(1)} %get-tuple-element.96), channel_id=1, source_target_pairs={{0,16},{1,2},{2,1},{3,4},{4,3},{5,6},{6,5},{7,8},{8,7},{9,10},{10,... | collective-permute-start | bytes 786440 | tf_op jit(solution)/shard_map/ppermute | solution.py:442
  34.0 2.0 %copy-start.1 = (f32[2,128]{1,0:T(2,128)S(1)}, f32[2,128]{1,0:T(2,128)}, u32[]{:S(2)}) copy-start(f32[2,128]{1,0:T(2,128)} %refs_4_.1) | copy-start | bytes 3076
  34.0 2.0 %copy-start.2 = (s32[2,4]{1,0:T(2,128)S(1)}, s32[2,4]{1,0:T(2,128)}, u32[]{:S(2)}) copy-start(s32[2,4]{1,0:T(2,128)} %refs_5_.3) | copy-start | bytes 100
  34.0 2.0 %copy-start.3 = (f32[2,4]{1,0:T(2,128)S(1)}, f32[2,4]{1,0:T(2,128)}, u32[]{:S(2)}) copy-start(f32[2,4]{1,0:T(2,128)} %refs_6_.1) | copy-start | bytes 100
  35.4 2.0 %collective-permute-start.6 = (bf16[256,256]{1,0:T(8,128)(2,1)S(1)}, bf16[256,256]{1,0:T(8,128)(2,1)S(1)}, u32[]{:S(2)}, u32[]{:S(2)}) collective-permute-start(bf16[256,256]{1,0:T(8,128)(2,1)S(1)} %get-tuple-element.99.refs_1_), channel_id=1, source_target_pairs={{0,16},{1,17},{2,18},{3,19},{4,20},{5,21},{6,22},{7,23},{8,24},{9,... | collective-permute-start | bytes 393224 | tf_op jit(solution)/shard_map/ppermute | solution.py:470
  35.9 1.6 %collective-permute-start.7 = (bf16[256,256]{1,0:T(8,128)(2,1)S(1)}, bf16[256,256]{1,0:T(8,128)(2,1)S(1)}, u32[]{:S(2)}, u32[]{:S(2)}) collective-permute-start(bf16[256,256]{1,0:T(8,128)(2,1)S(1)} %get-tuple-element.100.refs_2_), channel_id=1, source_target_pairs={{0,16},{1,17},{2,18},{3,19},{4,20},{5,21},{6,22},{7,23},{8,24},{9,... | collective-permute-start | bytes 393224 | tf_op jit(solution)/shard_map/ppermute | solution.py:470
  42.1 2.2 %collective-permute-start.8 = (bf16[512,256]{1,0:T(8,128)(2,1)S(1)}, bf16[512,256]{1,0:T(8,128)(2,1)S(1)}, u32[]{:S(2)}, u32[]{:S(2)}) collective-permute-start(bf16[512,256]{1,0:T(8,128)(2,1)S(1)} %shard_map.103.refs_1_), channel_id=1, source_target_pairs={{0,16},{1,17},{2,18},{3,19},{4,20},{5,21},{6,22},{7,23},{8,24},{9,... | collective-permute-start | bytes 786440 | tf_op jit(solution)/shard_map/ppermute | solution.py:470

commit v7 on v6

--- a/solution.py
+++ b/solution.py
@@ -13,7 +13,7 @@
 AXES = ("energy", "space")
 LEAD_A = True
 LEAD_PIECES = 2
-HELD = {1: (0, 2), 2: (0, 2), 3: (2, 1)}
+HELD = {1: (0, 3), 2: (0, 3), 3: (2, 1)}
 
 
 def times_i(pair, sign):
@@ -171,7 +171,8 @@
     else:
         base_a, base_b, base_send = rest[-3:]
     parts = jnp.where(lax.rem(where[3], 2) == 0, held[0], held[1])
-    here_a, here_b = parts > 0, parts > 1
+    here_a = jnp.logical_or(parts == 1, parts == 2)
+    here_b = parts > 1
     if kind == "after":
         here_a, here_b = jnp.logical_not(here_a), jnp.logical_not(here_b)
 

time: 46.4 us -> 46.3 us (level); the launches traced: 46.3 us -> 45.6 us
  waiting for transfers between devices: 13.4 us -> 7.94 us
  starting transfers between devices: 9.4 us -> 14.3 us
    ppermute x3, waiting for transfers between devices: 12.2 us -> 7.05 us  [body(): arrived[1] = lax.ppermute(send, AXES, pairings[1])]
    ppermute x3, starting transfers between devices: 6.88 us -> 11.4 us  [body(): arrived[1] = lax.ppermute(send, AXES, pairings[1])]
where the time goes in v7:
time: 46.3 us; the launch traced here: 45.6 us
  Pallas kernels  22.3 us (48%)
  starting transfers between devices  14.3 us (31%)
  waiting for transfers between devices  7.94 us (17%)
  between operations  1.04 us (2%)
    pallas_call x18, Pallas kernels, call(): pl.pallas_call(unpacked, out_shape=outs, in_specs=specs, out_specs=[NEAR]...  18.7 us
    ppermute x3, starting transfers between devices, body(): arrived[1] = lax.ppermute(send, AXES, pairings[1])  11.4 us
    ppermute x3, waiting for transfers between devices, body(): arrived[1] = lax.ppermute(send, AXES, pairings[1])  7.05 us
    pallas_call x2, Pallas kernels, self_blocks(): pl.pallas_call(functools.partial(sigma_kernel, pieces, len(previous)), ou...  3.61 us
    ppermute x3, starting transfers between devices, body(): others = [lax.ppermute(result, AXES, swap) for result in results]  2.01 us
  transfers between devices with their start and end apart: 9, of which 5 were waited for; matrix products, arithmetic and copies ran while one was open for 0% of the time, Pallas kernels for 39%

profile of v7, /device:TPU:25, one launch (start us, length us, event | category | flops | bytes accessed | tf_op | source)
XLA Modules:
  0.0 45.6 jit_solution(3136479401981894182)
XLA Ops:
  0.6 2.4 %shard_map.87 = (bf16[512,256]{1,0:T(8,128)(2,1)S(1)}, bf16[512,256]{1,0:T(8,128)(2,1)S(1)}, bf16[2,512,512]{2,1,0:T(8,128)(2,1)S(1)}, bf16[2,512,512]{2,1,0:T(8,128)(2,1)S(1)}, f32[2,512,128]{2,1,0:T(8,128)S(1)}) custom-call(s32[1]{0:T(128)} %bitcast.1.refs_0_.where, s32[1]{0:T(128)} %constant.16.clone.1.refs_1_, s32[1]{0:T(128)} %bitcast.2.refs_2_, ...), custom_call_target="tpu_custom_call" | custom-call | flops 1000 | bytes 1000 | tf_op jit(solution)/shard_map/pallas_call | solution.py:340
  3.0 0.8 %collective-permute-start = (bf16[512,256]{1,0:T(8,128)(2,1)S(1)}, bf16[512,256]{1,0:T(8,128)(2,1)S(1)}, u32[]{:S(2)}, u32[]{:S(2)}) collective-permute-start(bf16[512,256]{1,0:T(8,128)(2,1)S(1)} %get-tuple-element.72), channel_id=1, source_target_pairs={{0,1},{1,0},{2,3},{3,2},{4,5},{5,4},{6,7},{7,6},{8,9},{9,8},{10,11... | collective-permute-start | bytes 786440 | tf_op jit(solution)/shard_map/ppermute | solution.py:424
  3.8 0.0 copy-start
  3.8 3.6 %shard_map.88 = (bf16[512,256]{1,0:T(8,128)(2,1)S(1)}, bf16[512,256]{1,0:T(8,128)(2,1)S(1)}, bf16[2,512,512]{2,1,0:T(8,128)(2,1)S(1)}, bf16[2,512,512]{2,1,0:T(8...) custom-call(s32[1]{0:T(128)} %bitcast.1.refs_0_.where, ...), custom_call_target="tpu_custom_call", output_to_operand_aliasing={{7}: (7, {})} | custom-call | flops 1000 | bytes 1000 | tf_op jit(solution)/shard_map/pallas_call | solution.py:340
  7.4 0.0 copy-done
  7.4 0.4 shard_map.89
  7.8 3.4 %collective-permute-start.1 = (bf16[512,256]{1,0:T(8,128)(2,1)S(1)}, bf16[512,256]{1,0:T(8,128)(2,1)S(1)}, u32[]{:S(2)}, u32[]{:S(2)}) collective-permute-start(bf16[512,256]{1,0:T(8,128)(2,1)S(1)} %get-tuple-element.75), channel_id=1, source_target_pairs={{0,16},{1,2},{2,1},{3,4},{4,3},{5,6},{6,5},{7,8},{8,7},{9,10},{10,... | collective-permute-start | bytes 786440 | tf_op jit(solution)/shard_map/ppermute | solution.py:443
  11.2 1.4 %shard_map.90 = (f32[512,256]{1,0:T(8,128)S(1)}, f32[512,256]{1,0:T(8,128)S(1)}, f32[512,256]{1,0:T(8,128)S(1)}) custom-call(s32[1]{0:T(128)} %bitcast.1.refs_0_.where, s32[1]{0:T(128)} %constant.16.clone.1.refs_1_, s32[1]{0:T(128)} %bitcast.2.refs_2_, s32[1]{0:T(128)} %bitcast.3.refs_3_, ...), custom_call_target="tpu_custom_call", output_to_operand_aliasing={{0}: (14, {}), {1}: (15, {}), {2}: (16, {})} | custom-call | flops 1000 | bytes 1000 | tf_op jit(solution)/shard_map/pallas_call | solution.py:340
  12.6 0.0 collective-permute-done.refs_8_
  12.6 1.7 %shard_map.91 = (bf16[512,256]{1,0:T(8,128)(2,1)S(1)}, bf16[512,256]{1,0:T(8,128)(2,1)S(1)}, f32[512,256]{1,0:T(8,128)S(1)}) custom-call(s32[1]{0:T(128)} %bitcast.1.refs_0_.where, s32[1]{0:T(128)} %constant.16.clone.1.refs_1_, s32[1]{0:T(128)} %bitcast.2.refs_2_, s32[1]{0:T(128)} %bitcast.3.refs_3_, ...), custom_call_target="tpu_custom_call" | custom-call | flops 1000 | bytes 1000 | tf_op jit(solution)/shard_map/pallas_call | solution.py:340
  14.3 0.1 collective-permute-start.2
  14.4 2.8 %collective-permute-done.1.refs_8_ = bf16[512,256]{1,0:T(8,128)(2,1)S(1)} collective-permute-done((bf16[512,256]{1,0:T(8,128)(2,1)S(1)}, bf16[512,256]{1,0:T(8,128)(2,1)S(1)}, u32[]{:S(2)}, u32[]{:S(2)}) %collective-permute-start.1) | collective-permute-done | bytes 262176 | tf_op jit(solution)/shard_map/ppermute | solution.py:443
  17.2 0.4 shard_map.93
  17.6 0.4 shard_map.94
  18.1 5.4 %collective-permute-start.3 = (bf16[512,256]{1,0:T(8,128)(2,1)S(1)}, bf16[512,256]{1,0:T(8,128)(2,1)S(1)}, u32[]{:S(2)}, u32[]{:S(2)}) collective-permute-start(bf16[512,256]{1,0:T(8,128)(2,1)S(1)} %get-tuple-element.87), channel_id=1, source_target_pairs={{0,16},{1,2},{2,1},{3,4},{4,3},{5,6},{6,5},{7,8},{8,7},{9,10},{10,... | collective-permute-start | bytes 786440 | tf_op jit(solution)/shard_map/ppermute | solution.py:443
  23.4 1.4 %shard_map.95 = (f32[512,256]{1,0:T(8,128)S(1)}, f32[512,256]{1,0:T(8,128)S(1)}, f32[512,256]{1,0:T(8,128)S(1)}) custom-call(s32[1]{0:T(128)} %bitcast.1.refs_0_.where, s32[1]{0:T(128)} %constant.16.clone.1.refs_1_, s32[1]{0:T(128)} %bitcast.2.refs_2_, s32[1]{0:T(128)} %bitcast.3.refs_3_, ...), custom_call_target="tpu_custom_call", output_to_operand_aliasing={{0}: (14, {}), {1}: (15, {}), {2}: (16, {})} | custom-call | flops 1000 | bytes 1000 | tf_op jit(solution)/shard_map/pallas_call | solution.py:340
  24.8 0.0 collective-permute-done.2.refs_8_
  24.8 1.7 %shard_map.96 = (bf16[512,256]{1,0:T(8,128)(2,1)S(1)}, bf16[512,256]{1,0:T(8,128)(2,1)S(1)}, f32[512,256]{1,0:T(8,128)S(1)}) custom-call(s32[1]{0:T(128)} %bitcast.1.refs_0_.where, s32[1]{0:T(128)} %constant.16.clone.1.refs_1_, s32[1]{0:T(128)} %bitcast.2.refs_2_, s32[1]{0:T(128)} %bitcast.3.refs_3_, ...), custom_call_target="tpu_custom_call" | custom-call | flops 1000 | bytes 1000 | tf_op jit(solution)/shard_map/pallas_call | solution.py:340
  26.6 0.1 collective-permute-start.5
  26.6 2.9 %collective-permute-done.3.refs_8_ = bf16[512,256]{1,0:T(8,128)(2,1)S(1)} collective-permute-done((bf16[512,256]{1,0:T(8,128)(2,1)S(1)}, bf16[512,256]{1,0:T(8,128)(2,1)S(1)}, u32[]{:S(2)}, u32[]{:S(2)}) %collective-permute-start.3) | collective-permute-done | bytes 262176 | tf_op jit(solution)/shard_map/ppermute | solution.py:443
  29.5 0.4 shard_map.97
  30.0 1.4 %shard_map.98 = (f32[512,256]{1,0:T(8,128)S(1)}, f32[512,256]{1,0:T(8,128)S(1)}, f32[512,256]{1,0:T(8,128)S(1)}, bf16[512,256]{1,0:T(8,128)(2,1)S(1)}) custom-call(s32[1]{0:T(128)} %bitcast.1.refs_0_.where, s32[1]{0:T(128)} %constant.16.clone.1.refs_1_, s32[1]{0:T(128)} %bitcast.2.refs_2_, s32[1]{0:T(128)} %bitcast.3.refs_3_, ...), custom_call_target="tpu_custom_call" | custom-call | flops 1000 | bytes 1000 | tf_op jit(solution)/shard_map/pallas_call | solution.py:340
  31.4 2.6 %collective-permute-start.4 = (bf16[512,256]{1,0:T(8,128)(2,1)S(1)}, bf16[512,256]{1,0:T(8,128)(2,1)S(1)}, u32[]{:S(2)}, u32[]{:S(2)}) collective-permute-start(bf16[512,256]{1,0:T(8,128)(2,1)S(1)} %get-tuple-element.96), channel_id=1, source_target_pairs={{0,16},{1,2},{2,1},{3,4},{4,3},{5,6},{6,5},{7,8},{8,7},{9,10},{10,... | collective-permute-start | bytes 786440 | tf_op jit(solution)/shard_map/ppermute | solution.py:443
  34.0 0.4 shard_map.99
  34.4 0.0 copy-start.1
  34.4 0.0 copy-start.2
  34.4 0.0 copy-start.3
  34.4 0.5 %collective-permute-done.5.refs_8_ = bf16[512,256]{1,0:T(8,128)(2,1)S(1)} collective-permute-done((bf16[512,256]{1,0:T(8,128)(2,1)S(1)}, bf16[512,256]{1,0:T(8,128)(2,1)S(1)}, u32[]{:S(2)}, u32[]{:S(2)}) %collective-permute-start.5) | collective-permute-done | bytes 262176 | tf_op jit(solution)/shard_map/ppermute | solution.py:478
  34.9 0.4 shard_map.100
  35.3 0.5 %collective-permute-start.6 = (bf16[256,256]{1,0:T(8,128)(2,1)S(1)}, bf16[256,256]{1,0:T(8,128)(2,1)S(1)}, u32[]{:S(2)}, u32[]{:S(2)}) collective-permute-start(bf16[256,256]{1,0:T(8,128)(2,1)S(1)} %get-tuple-element.99.refs_1_), channel_id=1, source_target_pairs={{0,16},{1,17},{2,18},{3,19},{4,20},{5,21},{6,22},{7,23},{8,24},{9,... | collective-permute-start | bytes 393224 | tf_op jit(solution)/shard_map/ppermute | solution.py:471
  35.8 0.1 collective-permute-start.7
  35.9 0.0 copy-done.1
  35.9 0.0 copy-done.2
  35.9 0.0 copy-done.3
  35.9 0.7 %shard_map.86.refs_0_.scales = f32[256,8]{1,0:T(8,128)S(1)} custom-call(s32[1]{0:T(128)} %bitcast.1.refs_0_.where, s32[1]{0:T(128)} %constant.16.clone.1.refs_1_, s32[1]{0:T(128)} %bitcast.2.refs_2_, s32[1]{0:T(128)} %bitcast.3.refs_3_, f32[2,128]{1,0:T(2,128)S(1)} %copy-done.1, s32[2,4]{1,0:T(2,128)S(1)} %copy-done.2, f32[2,4]{1,0:T(2,128)S(1)} %copy-done.3), custom_call_target="tpu_custom_call" | custom-call | flops 1000 | bytes 1000 | tf_op jit(solution)/shard_map/pallas_call | solution.py:340
  36.6 0.8 %shard_map.101 = (f32[2,512,512]{2,1,0:T(8,128)S(1)}, f32[2,512,256]{2,1,0:T(8,128)S(1)}) custom-call(f32[256,8]{1,0:T(8,128)S(1)} %shard_map.86.refs_0_.scales, bf16[256,256]{1,0:T(8,128)(2,1)S(1)} %get-tuple-element.99.refs_1_, bf16[256,256]{1,0:T(8,128)(2,1)S(1)} %get-tuple-element.100.refs_2_), custom_call_target="tpu_custom_call" | custom-call | flops 1000 | bytes 1000 | tf_op jit(solution)/shard_map/pallas_call | solution.py:340
  37.3 0.0 collective-permute-done.6.rest_0_
  37.4 0.0 collective-permute-done.7.rest_1_
  37.4 1.8 %shard_map.102 = (bf16[2,2,512,512]{3,2,1,0:T(8,128)(2,1)}, bf16[2,2,512,512]{3,2,1,0:T(8,128)(2,1)}, f32[8,128]{1,0:T(8,128)S(1)}) custom-call(s32[1]{0:T(128)} %bitcast.1.refs_0_.where, f32[256,8]{1,0:T(8,128)S(1)} %shard_map.86.refs_0_.scales, f32[2,512,512]{2,1,0:T(8,128)S(1)} %get-tuple-element.101.tops, f32[2,512,256]{2,1,0:T(8,128)S(1)} %get-tuple-element.102.lows, ...), custom_call_target="tpu_custom_call" | custom-call | flops 1000 | bytes 1000 | tf_op jit(solution)/shard_map/pallas_call | solution.py:365
  39.2 1.4 %collective-permute-done.4.refs_8_ = bf16[512,256]{1,0:T(8,128)(2,1)S(1)} collective-permute-done((bf16[512,256]{1,0:T(8,128)(2,1)S(1)}, bf16[512,256]{1,0:T(8,128)(2,1)S(1)}, u32[]{:S(2)}, u32[]{:S(2)}) %collective-permute-start.4) | collective-permute-done | bytes 262176 | tf_op jit(solution)/shard_map/ppermute | solution.py:443
  40.6 0.5 shard_map.103.refs_1_
  41.0 1.4 %collective-permute-start.8 = (bf16[512,256]{1,0:T(8,128)(2,1)S(1)}, bf16[512,256]{1,0:T(8,128)(2,1)S(1)}, u32[]{:S(2)}, u32[]{:S(2)}) collective-permute-start(bf16[512,256]{1,0:T(8,128)(2,1)S(1)} %shard_map.103.refs_1_), channel_id=1, source_target_pairs={{0,16},{1,17},{2,18},{3,19},{4,20},{5,21},{6,22},{7,23},{8,24},{9,... | collective-permute-start | bytes 786440 | tf_op jit(solution)/shard_map/ppermute | solution.py:471
  42.5 0.7 %shard_map.104 = (f32[2,512,512]{2,1,0:T(8,128)S(1)}, f32[2,512,256]{2,1,0:T(8,128)S(1)}) custom-call(f32[256,8]{1,0:T(8,128)S(1)} %shard_map.86.refs_0_.scales, bf16[512,256]{1,0:T(8,128)(2,1)S(1)} %shard_map.103.refs_1_), custom_call_target="tpu_custom_call" | custom-call | flops 1000 | bytes 1000 | tf_op jit(solution)/shard_map/pallas_call | solution.py:340
  43.2 0.4 collective-permute-done.8.rest_0_
  43.6 1.8 %shard_map.105 = (bf16[2,2,512,512]{3,2,1,0:T(8,128)(2,1)}, bf16[2,2,512,512]{3,2,1,0:T(8,128)(2,1)}) custom-call(s32[1]{0:T(128)} %bitcast.where, f32[256,8]{1,0:T(8,128)S(1)} %shard_map.86.refs_0_.scales, f32[2,512,512]{2,1,0:T(8,128)S(1)} %get-tuple-element.104.tops, ...), custom_call_target="tpu_custom_call", output_to_operand_aliasing={{0}: (5, {}), {1}: (6, {})} | custom-call | flops 1000 | bytes 1000 | tf_op jit(solution)/shard_map/pallas_call | solution.py:365
  (1 shorter events, 0.0 us)
Async XLA Ops:
  3.0 9.6 %collective-permute-start = (bf16[512,256]{1,0:T(8,128)(2,1)S(1)}, bf16[512,256]{1,0:T(8,128)(2,1)S(1)}, u32[]{:S(2)}, u32[]{:S(2)}) collective-permute-start(bf16[512,256]{1,0:T(8,128)(2,1)S(1)} %get-tuple-element.72), channel_id=1, source_target_pairs={{0,1},{1,0},{2,3},{3,2},{4,5},{5,4},{6,7},{7,6},{8,9},{9,8},{10,11... | collective-permute-start | bytes 786440 | tf_op jit(solution)/shard_map/ppermute | solution.py:424
  3.8 3.6 %copy-start = (f32[1,2,2,512]{3,2,1,0:T(2,128)S(1)}, f32[1,2,2,512]{3,2,1,0:T(2,128)}, u32[]{:S(2)}) copy-start(f32[1,2,2,512]{3,2,1,0:T(2,128)} %param.10) | copy-start | bytes 24580
  7.8 9.4 %collective-permute-start.1 = (bf16[512,256]{1,0:T(8,128)(2,1)S(1)}, bf16[512,256]{1,0:T(8,128)(2,1)S(1)}, u32[]{:S(2)}, u32[]{:S(2)}) collective-permute-start(bf16[512,256]{1,0:T(8,128)(2,1)S(1)} %get-tuple-element.75), channel_id=1, source_target_pairs={{0,16},{1,2},{2,1},{3,4},{4,3},{5,6},{6,5},{7,8},{8,7},{9,10},{10,... | collective-permute-start | bytes 786440 | tf_op jit(solution)/shard_map/ppermute | solution.py:443
  14.3 10.5 %collective-permute-start.2 = (bf16[512,256]{1,0:T(8,128)(2,1)S(1)}, bf16[512,256]{1,0:T(8,128)(2,1)S(1)}, u32[]{:S(2)}, u32[]{:S(2)}) collective-permute-start(bf16[512,256]{1,0:T(8,128)(2,1)S(1)} %get-tuple-element.84), channel_id=1, source_target_pairs={{0,1},{1,0},{2,3},{3,2},{4,5},{5,4},{6,7},{7,6},{8,9},{9,8},{10,11... | collective-permute-start | bytes 786440 | tf_op jit(solution)/shard_map/ppermute | solution.py:478
  18.1 11.5 %collective-permute-start.3 = (bf16[512,256]{1,0:T(8,128)(2,1)S(1)}, bf16[512,256]{1,0:T(8,128)(2,1)S(1)}, u32[]{:S(2)}, u32[]{:S(2)}) collective-permute-start(bf16[512,256]{1,0:T(8,128)(2,1)S(1)} %get-tuple-element.87), channel_id=1, source_target_pairs={{0,16},{1,2},{2,1},{3,4},{4,3},{5,6},{6,5},{7,8},{8,7},{9,10},{10,... | collective-permute-start | bytes 786440 | tf_op jit(solution)/shard_map/ppermute | solution.py:443
  26.6 8.3 %collective-permute-start.5 = (bf16[512,256]{1,0:T(8,128)(2,1)S(1)}, bf16[512,256]{1,0:T(8,128)(2,1)S(1)}, u32[]{:S(2)}, u32[]{:S(2)}) collective-permute-start(bf16[512,256]{1,0:T(8,128)(2,1)S(1)} %get-tuple-element.98), channel_id=1, source_target_pairs={{0,1},{1,0},{2,3},{3,2},{4,5},{5,4},{6,7},{7,6},{8,9},{9,8},{10,11... | collective-permute-start | bytes 786440 | tf_op jit(solution)/shard_map/ppermute | solution.py:478
  31.4 9.2 %collective-permute-start.4 = (bf16[512,256]{1,0:T(8,128)(2,1)S(1)}, bf16[512,256]{1,0:T(8,128)(2,1)S(1)}, u32[]{:S(2)}, u32[]{:S(2)}) collective-permute-start(bf16[512,256]{1,0:T(8,128)(2,1)S(1)} %get-tuple-element.96), channel_id=1, source_target_pairs={{0,16},{1,2},{2,1},{3,4},{4,3},{5,6},{6,5},{7,8},{8,7},{9,10},{10,... | collective-permute-start | bytes 786440 | tf_op jit(solution)/shard_map/ppermute | solution.py:443
  34.4 1.5 %copy-start.1 = (f32[2,128]{1,0:T(2,128)S(1)}, f32[2,128]{1,0:T(2,128)}, u32[]{:S(2)}) copy-start(f32[2,128]{1,0:T(2,128)} %refs_4_.1) | copy-start | bytes 3076
  34.4 1.5 %copy-start.2 = (s32[2,4]{1,0:T(2,128)S(1)}, s32[2,4]{1,0:T(2,128)}, u32[]{:S(2)}) copy-start(s32[2,4]{1,0:T(2,128)} %refs_5_.3) | copy-start | bytes 100
  34.4 1.5 %copy-start.3 = (f32[2,4]{1,0:T(2,128)S(1)}, f32[2,4]{1,0:T(2,128)}, u32[]{:S(2)}) copy-start(f32[2,4]{1,0:T(2,128)} %refs_6_.1) | copy-start | bytes 100
  35.3 2.0 %collective-permute-start.6 = (bf16[256,256]{1,0:T(8,128)(2,1)S(1)}, bf16[256,256]{1,0:T(8,128)(2,1)S(1)}, u32[]{:S(2)}, u32[]{:S(2)}) collective-permute-start(bf16[256,256]{1,0:T(8,128)(2,1)S(1)} %get-tuple-element.99.refs_1_), channel_id=1, source_target_pairs={{0,16},{1,17},{2,18},{3,19},{4,20},{5,21},{6,22},{7,23},{8,24},{9,... | collective-permute-start | bytes 393224 | tf_op jit(solution)/shard_map/ppermute | solution.py:471
  35.8 1.6 %collective-permute-start.7 = (bf16[256,256]{1,0:T(8,128)(2,1)S(1)}, bf16[256,256]{1,0:T(8,128)(2,1)S(1)}, u32[]{:S(2)}, u32[]{:S(2)}) collective-permute-start(bf16[256,256]{1,0:T(8,128)(2,1)S(1)} %get-tuple-element.100.refs_2_), channel_id=1, source_target_pairs={{0,16},{1,17},{2,18},{3,19},{4,20},{5,21},{6,22},{7,23},{8,24},{9,... | collective-permute-start | bytes 393224 | tf_op jit(solution)/shard_map/ppermute | solution.py:471
  41.0 2.6 %collective-permute-start.8 = (bf16[512,256]{1,0:T(8,128)(2,1)S(1)}, bf16[512,256]{1,0:T(8,128)(2,1)S(1)}, u32[]{:S(2)}, u32[]{:S(2)}) collective-permute-start(bf16[512,256]{1,0:T(8,128)(2,1)S(1)} %shard_map.103.refs_1_), channel_id=1, source_target_pairs={{0,16},{1,17},{2,18},{3,19},{4,20},{5,21},{6,22},{7,23},{8,24},{9,... | collective-permute-start | bytes 786440 | tf_op jit(solution)/shard_map/ppermute | solution.py:471

commit v8 on v7

--- a/solution.py
+++ b/solution.py
@@ -232,6 +232,8 @@
     slab = 1 - where[0] if side else where[0]
 
     def message():
+        if (side == 0) == LEAD_A:
+            return arrived[...]
         return jnp.where(where[1 + side] != 0, arrived[...], jnp.zeros_like(arrived))
 
     def keep(fresh):

time: 46.3 us -> 46.3 us (level)
  no operation moved by 1% of the time
where the time goes in v8:
time: 46.3 us; the launch traced here: 45.6 us
  Pallas kernels  22.3 us (48%)
  starting transfers between devices  14.3 us (31%)
  waiting for transfers between devices  7.95 us (17%)
  between operations  1.04 us (2%)
    pallas_call x18, Pallas kernels, call(): pl.pallas_call(unpacked, out_shape=outs, in_specs=specs, out_specs=[NEAR]...  18.7 us
    ppermute x3, starting transfers between devices, body(): arrived[1] = lax.ppermute(send, AXES, pairings[1])  11.4 us
    ppermute x3, waiting for transfers between devices, body(): arrived[1] = lax.ppermute(send, AXES, pairings[1])  7.06 us
    pallas_call x2, Pallas kernels, self_blocks(): pl.pallas_call(functools.partial(sigma_kernel, pieces, len(previous)), ou...  3.61 us
    ppermute x3, starting transfers between devices, body(): others = [lax.ppermute(result, AXES, swap) for result in results]  2.01 us
  transfers between devices with their start and end apart: 9, of which 5 were waited for; matrix products, arithmetic and copies ran while one was open for 0% of the time, Pallas kernels for 39%

profile of v8, /device:TPU:25, one launch (start us, length us, event | category | flops | bytes accessed | tf_op | source)
XLA Modules:
  0.0 45.6 jit_solution(6175094248701090454)
XLA Ops:
  0.6 2.4 %shard_map.87 = (bf16[512,256]{1,0:T(8,128)(2,1)S(1)}, bf16[512,256]{1,0:T(8,128)(2,1)S(1)}, bf16[2,512,512]{2,1,0:T(8,128)(2,1)S(1)}, bf16[2,512,512]{2,1,0:T(8,128)(2,1)S(1)}, f32[2,512,128]{2,1,0:T(8,128)S(1)}) custom-call(s32[1]{0:T(128)} %bitcast.1.refs_0_.where, s32[1]{0:T(128)} %constant.16.clone.1.refs_1_, s32[1]{0:T(128)} %bitcast.2.refs_2_, ...), custom_call_target="tpu_custom_call" | custom-call | flops 1000 | bytes 1000 | tf_op jit(solution)/shard_map/pallas_call | solution.py:342
  3.0 0.8 %collective-permute-start = (bf16[512,256]{1,0:T(8,128)(2,1)S(1)}, bf16[512,256]{1,0:T(8,128)(2,1)S(1)}, u32[]{:S(2)}, u32[]{:S(2)}) collective-permute-start(bf16[512,256]{1,0:T(8,128)(2,1)S(1)} %get-tuple-element.72), channel_id=1, source_target_pairs={{0,1},{1,0},{2,3},{3,2},{4,5},{5,4},{6,7},{7,6},{8,9},{9,8},{10,11... | collective-permute-start | bytes 786440 | tf_op jit(solution)/shard_map/ppermute | solution.py:426
  3.8 0.0 copy-start
  3.8 3.6 %shard_map.88 = (bf16[512,256]{1,0:T(8,128)(2,1)S(1)}, bf16[512,256]{1,0:T(8,128)(2,1)S(1)}, bf16[2,512,512]{2,1,0:T(8,128)(2,1)S(1)}, bf16[2,512,512]{2,1,0:T(8...) custom-call(s32[1]{0:T(128)} %bitcast.1.refs_0_.where, ...), custom_call_target="tpu_custom_call", output_to_operand_aliasing={{7}: (7, {})} | custom-call | flops 1000 | bytes 1000 | tf_op jit(solution)/shard_map/pallas_call | solution.py:342
  7.4 0.0 copy-done
  7.4 0.4 shard_map.89
  7.8 3.4 %collective-permute-start.1 = (bf16[512,256]{1,0:T(8,128)(2,1)S(1)}, bf16[512,256]{1,0:T(8,128)(2,1)S(1)}, u32[]{:S(2)}, u32[]{:S(2)}) collective-permute-start(bf16[512,256]{1,0:T(8,128)(2,1)S(1)} %get-tuple-element.75), channel_id=1, source_target_pairs={{0,16},{1,2},{2,1},{3,4},{4,3},{5,6},{6,5},{7,8},{8,7},{9,10},{10,... | collective-permute-start | bytes 786440 | tf_op jit(solution)/shard_map/ppermute | solution.py:445
  11.2 1.4 %shard_map.90 = (f32[512,256]{1,0:T(8,128)S(1)}, f32[512,256]{1,0:T(8,128)S(1)}, f32[512,256]{1,0:T(8,128)S(1)}) custom-call(s32[1]{0:T(128)} %bitcast.1.refs_0_.where, s32[1]{0:T(128)} %constant.16.clone.1.refs_1_, s32[1]{0:T(128)} %bitcast.2.refs_2_, s32[1]{0:T(128)} %bitcast.3.refs_3_, ...), custom_call_target="tpu_custom_call", output_to_operand_aliasing={{0}: (14, {}), {1}: (15, {}), {2}: (16, {})} | custom-call | flops 1000 | bytes 1000 | tf_op jit(solution)/shard_map/pallas_call | solution.py:342
  12.6 0.0 collective-permute-done.refs_8_
  12.6 1.7 %shard_map.91 = (bf16[512,256]{1,0:T(8,128)(2,1)S(1)}, bf16[512,256]{1,0:T(8,128)(2,1)S(1)}, f32[512,256]{1,0:T(8,128)S(1)}) custom-call(s32[1]{0:T(128)} %bitcast.1.refs_0_.where, s32[1]{0:T(128)} %constant.16.clone.1.refs_1_, s32[1]{0:T(128)} %bitcast.2.refs_2_, s32[1]{0:T(128)} %bitcast.3.refs_3_, ...), custom_call_target="tpu_custom_call" | custom-call | flops 1000 | bytes 1000 | tf_op jit(solution)/shard_map/pallas_call | solution.py:342
  14.3 0.1 collective-permute-start.2
  14.4 2.8 %collective-permute-done.1.refs_8_ = bf16[512,256]{1,0:T(8,128)(2,1)S(1)} collective-permute-done((bf16[512,256]{1,0:T(8,128)(2,1)S(1)}, bf16[512,256]{1,0:T(8,128)(2,1)S(1)}, u32[]{:S(2)}, u32[]{:S(2)}) %collective-permute-start.1) | collective-permute-done | bytes 262176 | tf_op jit(solution)/shard_map/ppermute | solution.py:445
  17.2 0.4 shard_map.93
  17.6 0.4 shard_map.94
  18.1 5.4 %collective-permute-start.3 = (bf16[512,256]{1,0:T(8,128)(2,1)S(1)}, bf16[512,256]{1,0:T(8,128)(2,1)S(1)}, u32[]{:S(2)}, u32[]{:S(2)}) collective-permute-start(bf16[512,256]{1,0:T(8,128)(2,1)S(1)} %get-tuple-element.87), channel_id=1, source_target_pairs={{0,16},{1,2},{2,1},{3,4},{4,3},{5,6},{6,5},{7,8},{8,7},{9,10},{10,... | collective-permute-start | bytes 786440 | tf_op jit(solution)/shard_map/ppermute | solution.py:445
  23.4 1.4 %shard_map.95 = (f32[512,256]{1,0:T(8,128)S(1)}, f32[512,256]{1,0:T(8,128)S(1)}, f32[512,256]{1,0:T(8,128)S(1)}) custom-call(s32[1]{0:T(128)} %bitcast.1.refs_0_.where, s32[1]{0:T(128)} %constant.16.clone.1.refs_1_, s32[1]{0:T(128)} %bitcast.2.refs_2_, s32[1]{0:T(128)} %bitcast.3.refs_3_, ...), custom_call_target="tpu_custom_call", output_to_operand_aliasing={{0}: (14, {}), {1}: (15, {}), {2}: (16, {})} | custom-call | flops 1000 | bytes 1000 | tf_op jit(solution)/shard_map/pallas_call | solution.py:342
  24.8 0.0 collective-permute-done.2.refs_8_
  24.8 1.7 %shard_map.96 = (bf16[512,256]{1,0:T(8,128)(2,1)S(1)}, bf16[512,256]{1,0:T(8,128)(2,1)S(1)}, f32[512,256]{1,0:T(8,128)S(1)}) custom-call(s32[1]{0:T(128)} %bitcast.1.refs_0_.where, s32[1]{0:T(128)} %constant.16.clone.1.refs_1_, s32[1]{0:T(128)} %bitcast.2.refs_2_, s32[1]{0:T(128)} %bitcast.3.refs_3_, ...), custom_call_target="tpu_custom_call" | custom-call | flops 1000 | bytes 1000 | tf_op jit(solution)/shard_map/pallas_call | solution.py:342
  26.5 0.1 collective-permute-start.5
  26.6 2.9 %collective-permute-done.3.refs_8_ = bf16[512,256]{1,0:T(8,128)(2,1)S(1)} collective-permute-done((bf16[512,256]{1,0:T(8,128)(2,1)S(1)}, bf16[512,256]{1,0:T(8,128)(2,1)S(1)}, u32[]{:S(2)}, u32[]{:S(2)}) %collective-permute-start.3) | collective-permute-done | bytes 262176 | tf_op jit(solution)/shard_map/ppermute | solution.py:445
  29.5 0.4 shard_map.97
  30.0 1.4 %shard_map.98 = (f32[512,256]{1,0:T(8,128)S(1)}, f32[512,256]{1,0:T(8,128)S(1)}, f32[512,256]{1,0:T(8,128)S(1)}, bf16[512,256]{1,0:T(8,128)(2,1)S(1)}) custom-call(s32[1]{0:T(128)} %bitcast.1.refs_0_.where, s32[1]{0:T(128)} %constant.16.clone.1.refs_1_, s32[1]{0:T(128)} %bitcast.2.refs_2_, s32[1]{0:T(128)} %bitcast.3.refs_3_, ...), custom_call_target="tpu_custom_call" | custom-call | flops 1000 | bytes 1000 | tf_op jit(solution)/shard_map/pallas_call | solution.py:342
  31.4 2.6 %collective-permute-start.4 = (bf16[512,256]{1,0:T(8,128)(2,1)S(1)}, bf16[512,256]{1,0:T(8,128)(2,1)S(1)}, u32[]{:S(2)}, u32[]{:S(2)}) collective-permute-start(bf16[512,256]{1,0:T(8,128)(2,1)S(1)} %get-tuple-element.96), channel_id=1, source_target_pairs={{0,16},{1,2},{2,1},{3,4},{4,3},{5,6},{6,5},{7,8},{8,7},{9,10},{10,... | collective-permute-start | bytes 786440 | tf_op jit(solution)/shard_map/ppermute | solution.py:445
  34.0 0.4 shard_map.99
  34.4 0.0 copy-start.1
  34.4 0.0 copy-start.2
  34.4 0.0 copy-start.3
  34.4 0.5 %collective-permute-done.5.refs_8_ = bf16[512,256]{1,0:T(8,128)(2,1)S(1)} collective-permute-done((bf16[512,256]{1,0:T(8,128)(2,1)S(1)}, bf16[512,256]{1,0:T(8,128)(2,1)S(1)}, u32[]{:S(2)}, u32[]{:S(2)}) %collective-permute-start.5) | collective-permute-done | bytes 262176 | tf_op jit(solution)/shard_map/ppermute | solution.py:480
  34.9 0.4 shard_map.100
  35.3 0.5 %collective-permute-start.6 = (bf16[256,256]{1,0:T(8,128)(2,1)S(1)}, bf16[256,256]{1,0:T(8,128)(2,1)S(1)}, u32[]{:S(2)}, u32[]{:S(2)}) collective-permute-start(bf16[256,256]{1,0:T(8,128)(2,1)S(1)} %get-tuple-element.99.refs_1_), channel_id=1, source_target_pairs={{0,16},{1,17},{2,18},{3,19},{4,20},{5,21},{6,22},{7,23},{8,24},{9,... | collective-permute-start | bytes 393224 | tf_op jit(solution)/shard_map/ppermute | solution.py:473
  35.8 0.1 collective-permute-start.7
  35.9 0.0 copy-done.1
  35.9 0.0 copy-done.2
  35.9 0.0 copy-done.3
  35.9 0.7 %shard_map.86.refs_0_.scales = f32[256,8]{1,0:T(8,128)S(1)} custom-call(s32[1]{0:T(128)} %bitcast.1.refs_0_.where, s32[1]{0:T(128)} %constant.16.clone.1.refs_1_, s32[1]{0:T(128)} %bitcast.2.refs_2_, s32[1]{0:T(128)} %bitcast.3.refs_3_, f32[2,128]{1,0:T(2,128)S(1)} %copy-done.1, s32[2,4]{1,0:T(2,128)S(1)} %copy-done.2, f32[2,4]{1,0:T(2,128)S(1)} %copy-done.3), custom_call_target="tpu_custom_call" | custom-call | flops 1000 | bytes 1000 | tf_op jit(solution)/shard_map/pallas_call | solution.py:342
  36.6 0.7 %shard_map.101 = (f32[2,512,512]{2,1,0:T(8,128)S(1)}, f32[2,512,256]{2,1,0:T(8,128)S(1)}) custom-call(f32[256,8]{1,0:T(8,128)S(1)} %shard_map.86.refs_0_.scales, bf16[256,256]{1,0:T(8,128)(2,1)S(1)} %get-tuple-element.99.refs_1_, bf16[256,256]{1,0:T(8,128)(2,1)S(1)} %get-tuple-element.100.refs_2_), custom_call_target="tpu_custom_call" | custom-call | flops 1000 | bytes 1000 | tf_op jit(solution)/shard_map/pallas_call | solution.py:342
  37.3 0.0 collective-permute-done.6.rest_0_
  37.3 0.0 collective-permute-done.7.rest_1_
  37.4 1.8 %shard_map.102 = (bf16[2,2,512,512]{3,2,1,0:T(8,128)(2,1)}, bf16[2,2,512,512]{3,2,1,0:T(8,128)(2,1)}, f32[8,128]{1,0:T(8,128)S(1)}) custom-call(s32[1]{0:T(128)} %bitcast.1.refs_0_.where, f32[256,8]{1,0:T(8,128)S(1)} %shard_map.86.refs_0_.scales, f32[2,512,512]{2,1,0:T(8,128)S(1)} %get-tuple-element.101.tops, f32[2,512,256]{2,1,0:T(8,128)S(1)} %get-tuple-element.102.lows, ...), custom_call_target="tpu_custom_call" | custom-call | flops 1000 | bytes 1000 | tf_op jit(solution)/shard_map/pallas_call | solution.py:367
  39.2 1.4 %collective-permute-done.4.refs_8_ = bf16[512,256]{1,0:T(8,128)(2,1)S(1)} collective-permute-done((bf16[512,256]{1,0:T(8,128)(2,1)S(1)}, bf16[512,256]{1,0:T(8,128)(2,1)S(1)}, u32[]{:S(2)}, u32[]{:S(2)}) %collective-permute-start.4) | collective-permute-done | bytes 262176 | tf_op jit(solution)/shard_map/ppermute | solution.py:445
  40.6 0.5 shard_map.103.refs_1_
  41.0 1.4 %collective-permute-start.8 = (bf16[512,256]{1,0:T(8,128)(2,1)S(1)}, bf16[512,256]{1,0:T(8,128)(2,1)S(1)}, u32[]{:S(2)}, u32[]{:S(2)}) collective-permute-start(bf16[512,256]{1,0:T(8,128)(2,1)S(1)} %shard_map.103.refs_1_), channel_id=1, source_target_pairs={{0,16},{1,17},{2,18},{3,19},{4,20},{5,21},{6,22},{7,23},{8,24},{9,... | collective-permute-start | bytes 786440 | tf_op jit(solution)/shard_map/ppermute | solution.py:473
  42.5 0.7 %shard_map.104 = (f32[2,512,512]{2,1,0:T(8,128)S(1)}, f32[2,512,256]{2,1,0:T(8,128)S(1)}) custom-call(f32[256,8]{1,0:T(8,128)S(1)} %shard_map.86.refs_0_.scales, bf16[512,256]{1,0:T(8,128)(2,1)S(1)} %shard_map.103.refs_1_), custom_call_target="tpu_custom_call" | custom-call | flops 1000 | bytes 1000 | tf_op jit(solution)/shard_map/pallas_call | solution.py:342
  43.2 0.4 collective-permute-done.8.rest_0_
  43.6 1.8 %shard_map.105 = (bf16[2,2,512,512]{3,2,1,0:T(8,128)(2,1)}, bf16[2,2,512,512]{3,2,1,0:T(8,128)(2,1)}) custom-call(s32[1]{0:T(128)} %bitcast.where, f32[256,8]{1,0:T(8,128)S(1)} %shard_map.86.refs_0_.scales, f32[2,512,512]{2,1,0:T(8,128)S(1)} %get-tuple-element.104.tops, ...), custom_call_target="tpu_custom_call", output_to_operand_aliasing={{0}: (5, {}), {1}: (6, {})} | custom-call | flops 1000 | bytes 1000 | tf_op jit(solution)/shard_map/pallas_call | solution.py:367
  (1 shorter events, 0.0 us)
Async XLA Ops:
  3.0 9.6 %collective-permute-start = (bf16[512,256]{1,0:T(8,128)(2,1)S(1)}, bf16[512,256]{1,0:T(8,128)(2,1)S(1)}, u32[]{:S(2)}, u32[]{:S(2)}) collective-permute-start(bf16[512,256]{1,0:T(8,128)(2,1)S(1)} %get-tuple-element.72), channel_id=1, source_target_pairs={{0,1},{1,0},{2,3},{3,2},{4,5},{5,4},{6,7},{7,6},{8,9},{9,8},{10,11... | collective-permute-start | bytes 786440 | tf_op jit(solution)/shard_map/ppermute | solution.py:426
  3.8 3.6 %copy-start = (f32[1,2,2,512]{3,2,1,0:T(2,128)S(1)}, f32[1,2,2,512]{3,2,1,0:T(2,128)}, u32[]{:S(2)}) copy-start(f32[1,2,2,512]{3,2,1,0:T(2,128)} %param.10) | copy-start | bytes 24580
  7.8 9.4 %collective-permute-start.1 = (bf16[512,256]{1,0:T(8,128)(2,1)S(1)}, bf16[512,256]{1,0:T(8,128)(2,1)S(1)}, u32[]{:S(2)}, u32[]{:S(2)}) collective-permute-start(bf16[512,256]{1,0:T(8,128)(2,1)S(1)} %get-tuple-element.75), channel_id=1, source_target_pairs={{0,16},{1,2},{2,1},{3,4},{4,3},{5,6},{6,5},{7,8},{8,7},{9,10},{10,... | collective-permute-start | bytes 786440 | tf_op jit(solution)/shard_map/ppermute | solution.py:445
  14.3 10.5 %collective-permute-start.2 = (bf16[512,256]{1,0:T(8,128)(2,1)S(1)}, bf16[512,256]{1,0:T(8,128)(2,1)S(1)}, u32[]{:S(2)}, u32[]{:S(2)}) collective-permute-start(bf16[512,256]{1,0:T(8,128)(2,1)S(1)} %get-tuple-element.84), channel_id=1, source_target_pairs={{0,1},{1,0},{2,3},{3,2},{4,5},{5,4},{6,7},{7,6},{8,9},{9,8},{10,11... | collective-permute-start | bytes 786440 | tf_op jit(solution)/shard_map/ppermute | solution.py:480
  18.1 11.5 %collective-permute-start.3 = (bf16[512,256]{1,0:T(8,128)(2,1)S(1)}, bf16[512,256]{1,0:T(8,128)(2,1)S(1)}, u32[]{:S(2)}, u32[]{:S(2)}) collective-permute-start(bf16[512,256]{1,0:T(8,128)(2,1)S(1)} %get-tuple-element.87), channel_id=1, source_target_pairs={{0,16},{1,2},{2,1},{3,4},{4,3},{5,6},{6,5},{7,8},{8,7},{9,10},{10,... | collective-permute-start | bytes 786440 | tf_op jit(solution)/shard_map/ppermute | solution.py:445
  26.5 8.3 %collective-permute-start.5 = (bf16[512,256]{1,0:T(8,128)(2,1)S(1)}, bf16[512,256]{1,0:T(8,128)(2,1)S(1)}, u32[]{:S(2)}, u32[]{:S(2)}) collective-permute-start(bf16[512,256]{1,0:T(8,128)(2,1)S(1)} %get-tuple-element.98), channel_id=1, source_target_pairs={{0,1},{1,0},{2,3},{3,2},{4,5},{5,4},{6,7},{7,6},{8,9},{9,8},{10,11... | collective-permute-start | bytes 786440 | tf_op jit(solution)/shard_map/ppermute | solution.py:480
  31.4 9.2 %collective-permute-start.4 = (bf16[512,256]{1,0:T(8,128)(2,1)S(1)}, bf16[512,256]{1,0:T(8,128)(2,1)S(1)}, u32[]{:S(2)}, u32[]{:S(2)}) collective-permute-start(bf16[512,256]{1,0:T(8,128)(2,1)S(1)} %get-tuple-element.96), channel_id=1, source_target_pairs={{0,16},{1,2},{2,1},{3,4},{4,3},{5,6},{6,5},{7,8},{8,7},{9,10},{10,... | collective-permute-start | bytes 786440 | tf_op jit(solution)/shard_map/ppermute | solution.py:445
  34.4 1.5 %copy-start.1 = (f32[2,128]{1,0:T(2,128)S(1)}, f32[2,128]{1,0:T(2,128)}, u32[]{:S(2)}) copy-start(f32[2,128]{1,0:T(2,128)} %refs_4_.1) | copy-start | bytes 3076
  34.4 1.5 %copy-start.2 = (s32[2,4]{1,0:T(2,128)S(1)}, s32[2,4]{1,0:T(2,128)}, u32[]{:S(2)}) copy-start(s32[2,4]{1,0:T(2,128)} %refs_5_.3) | copy-start | bytes 100
  34.4 1.5 %copy-start.3 = (f32[2,4]{1,0:T(2,128)S(1)}, f32[2,4]{1,0:T(2,128)}, u32[]{:S(2)}) copy-start(f32[2,4]{1,0:T(2,128)} %refs_6_.1) | copy-start | bytes 100
  35.3 2.0 %collective-permute-start.6 = (bf16[256,256]{1,0:T(8,128)(2,1)S(1)}, bf16[256,256]{1,0:T(8,128)(2,1)S(1)}, u32[]{:S(2)}, u32[]{:S(2)}) collective-permute-start(bf16[256,256]{1,0:T(8,128)(2,1)S(1)} %get-tuple-element.99.refs_1_), channel_id=1, source_target_pairs={{0,16},{1,17},{2,18},{3,19},{4,20},{5,21},{6,22},{7,23},{8,24},{9,... | collective-permute-start | bytes 393224 | tf_op jit(solution)/shard_map/ppermute | solution.py:473
  35.8 1.6 %collective-permute-start.7 = (bf16[256,256]{1,0:T(8,128)(2,1)S(1)}, bf16[256,256]{1,0:T(8,128)(2,1)S(1)}, u32[]{:S(2)}, u32[]{:S(2)}) collective-permute-start(bf16[256,256]{1,0:T(8,128)(2,1)S(1)} %get-tuple-element.100.refs_2_), channel_id=1, source_target_pairs={{0,16},{1,17},{2,18},{3,19},{4,20},{5,21},{6,22},{7,23},{8,24},{9,... | collective-permute-start | bytes 393224 | tf_op jit(solution)/shard_map/ppermute | solution.py:473
  41.0 2.6 %collective-permute-start.8 = (bf16[512,256]{1,0:T(8,128)(2,1)S(1)}, bf16[512,256]{1,0:T(8,128)(2,1)S(1)}, u32[]{:S(2)}, u32[]{:S(2)}) collective-permute-start(bf16[512,256]{1,0:T(8,128)(2,1)S(1)} %shard_map.103.refs_1_), channel_id=1, source_target_pairs={{0,16},{1,17},{2,18},{3,19},{4,20},{5,21},{6,22},{7,23},{8,24},{9,... | collective-permute-start | bytes 786440 | tf_op jit(solution)/shard_map/ppermute | solution.py:473
